TPU v7x, 128 devices: a whole 4x4x4 slice. The times are simulated.
128 devices in a mesh: tm: 8 (over z, y_lo), tmpl: 16 (over y_hi, x, core).
Axes of the slice: x: 4, y: 4 (y_hi: 2, y_lo: 2; y = y_hi * 2 + y_lo), z: 4, core: 2. Of those that a mesh axis runs over, the one named last changes fastest.
Arguments:
- strain: float32 [16, 262144], P('tmpl', 'tm'), may hold values from -6 to 6
- psd_bins: int32 [8, 65536], P(None, 'tmpl'), may hold values from 0 to 8191, as said below
- psd_values: float32 [8, 8192], P('tm'), may hold values from 0.25 to 4
- chirp_slope: int32 [32], P('tmpl'), may hold values from 0 to 1023
- chirp_curve: int32 [32], P('tmpl'), may hold values from 1 to 63
Outputs:
- snr: float32 [32, 4194304], P('tmpl', 'tm')
Inputs may be any that keep to these rules, and one draw needn't show every extreme that they name: psd_bins[r, c] names the row of psd_values that serves frequency bin r * 65536 + c.
All inputs are finite; a program needn't handle non-finite values.
Results may differ from a plain program's by a relative error of at most 0.0003.
Values sent between devices are 32-bit elements; how exact they have to be, the bound alone decides.
No kernel may reach another device: no remote copies, remote signals or barrier semaphores. Data moves between devices by JAX's collectives and lax.ppermute only.
A program may use at most 128 MiB of HBM per device.

v0:
```python
import math

import jax
import jax.numpy as jnp
from jax import lax
from jax.sharding import PartitionSpec as P

OR = 32768


HIGHEST = lax.Precision.HIGHEST
TWO_PI = 2.0 * math.pi


def shifted(block, axis, distance):
    devices = range(lax.axis_size(axis))
    route = [(i - distance, i) for i in devices if i - distance in devices]
    return lax.ppermute(block, axis, route)


def over_pieces(x, axis):
    return lax.all_gather(x, axis).sum(0)


def in_one_piece(arrays, axis, dim, along):
    both = jnp.concatenate(arrays, axis=along)
    result, at, outs = (lax.all_gather(both, axis, axis=dim, tiled=True), 0, [])
    for a in arrays:
        outs.append(lax.slice_in_dim(result, at, at + a.shape[along], axis=along))
        at += a.shape[along]
    return tuple(outs)


def split_sizes(length):
    count = 0
    while length > 512:
        length = length // 128
        count = count + 1
    return [length] + [128] * count


def angle_table(rows_count, cols_count, modulus, direction):
    product = (
        jnp.arange(rows_count, dtype=jnp.int32)[:, None]
        * jnp.arange(cols_count, dtype=jnp.int32)[None, :]
    )
    angles = (product % modulus).astype(jnp.float32) * (direction * TWO_PI / modulus)
    return (jnp.cos(angles), jnp.sin(angles))


def complex_left(cos_part, sin_part, real_part, imag_part):
    new_re = jnp.einsum("qp,...pk->...qk", cos_part, real_part, precision=HIGHEST) - jnp.einsum(
        "qp,...pk->...qk", sin_part, imag_part, precision=HIGHEST
    )
    new_im = jnp.einsum("qp,...pk->...qk", sin_part, real_part, precision=HIGHEST) + jnp.einsum(
        "qp,...pk->...qk", cos_part, imag_part, precision=HIGHEST
    )
    return (new_re, new_im)


def apply_sizes(real_part, imag_part, sizes, direction):
    length = real_part.shape[-1]
    if len(sizes) == 1:
        cos_part, sin_part = angle_table(length, length, length, direction)
        new_re = jnp.matmul(real_part, cos_part, precision=HIGHEST) - jnp.matmul(
            imag_part, sin_part, precision=HIGHEST
        )
        new_im = jnp.matmul(real_part, sin_part, precision=HIGHEST) + jnp.matmul(
            imag_part, cos_part, precision=HIGHEST
        )
        return (new_re, new_im)
    outer_size = sizes[0]
    inner_size = length // outer_size
    leading = real_part.shape[:-1]
    real_part = real_part.reshape(leading + (outer_size, inner_size))
    imag_part = imag_part.reshape(leading + (outer_size, inner_size))
    mat_cos, mat_sin = angle_table(outer_size, outer_size, outer_size, direction)
    real_part, imag_part = complex_left(mat_cos, mat_sin, real_part, imag_part)
    cos_part, sin_part = angle_table(outer_size, inner_size, length, direction)
    real_part, imag_part = (
        real_part * cos_part - imag_part * sin_part,
        real_part * sin_part + imag_part * cos_part,
    )
    return apply_sizes(real_part, imag_part, sizes[1:], direction)


def transform(real_part, imag_part, direction):
    length = real_part.shape[-1]
    leading = real_part.shape[:-1]
    sizes = split_sizes(length)
    new_re, new_im = apply_sizes(real_part, imag_part, sizes, direction)
    lead_count = len(leading)
    last_axis = new_re.ndim - 1
    order = tuple(range(lead_count)) + tuple(range(last_axis, lead_count - 1, -1))
    new_re = jnp.transpose(new_re, order)
    new_im = jnp.transpose(new_im, order)
    return (new_re.reshape(leading + (length,)), new_im.reshape(leading + (length,)))


def chirp_phase(frequency, slope, curve, modulus):
    high_part = frequency // 1024
    low_part = frequency % 1024
    square = 2 * high_part * low_part % (modulus // 1024) * 1024 + low_part * low_part
    square = square % modulus
    return (slope * frequency + curve * square) % modulus


def amplitude_of(frequency, k_low, k_cut):
    ratio = frequency.astype(jnp.float32) / k_low
    inside = (frequency >= k_low) & (frequency < k_cut)
    return jnp.where(inside, jnp.power(jnp.maximum(ratio, 1.0), -7.0 / 6.0), 0.0)


def template_parts(frequency, chirp_slope, chirp_curve, modulus, k_low, k_cut):
    phase = chirp_phase(frequency[None, :], chirp_slope[:, None], chirp_curve[:, None], modulus)
    angles = phase.astype(jnp.float32) * (TWO_PI / modulus)
    amplitude = amplitude_of(frequency, k_low, k_cut)
    return (amplitude * jnp.cos(angles), -amplitude * jnp.sin(angles))


def local(strain, psd_bins, psd_values, chirp_slope, chirp_curve):
    groups = lax.axis_size("tmpl")
    member = lax.axis_index("tmpl")
    own_part = strain[0]
    edge_tail = shifted(own_part, "tm", 1)
    local_seq = jnp.concatenate([edge_tail, own_part])
    sub_len = local_seq.shape[0]
    total_len = sub_len * groups
    block_len = sub_len // groups
    norm_scale = 1.0 / math.sqrt(total_len)
    k_low = total_len // 200
    k_cut = 3 * total_len // 8
    band_rows = 3 * groups // 8
    inv_psd = 1.0 / jnp.take(psd_values[0], psd_bins[:band_rows])
    own_freq = (
        jnp.arange(band_rows, dtype=jnp.int32)[:, None] * sub_len
        + member * block_len
        + jnp.arange(block_len, dtype=jnp.int32)[None, :]
    )
    own_amp = amplitude_of(own_freq, k_low, k_cut)
    sigma_sq = over_pieces(jnp.sum(own_amp * own_amp * inv_psd), "tmpl")
    local_re, local_im = transform(local_seq, jnp.zeros_like(local_seq), -1.0)
    index_k = jnp.arange(sub_len, dtype=jnp.int32)
    angles = (member * index_k % total_len).astype(jnp.float32) * (-TWO_PI / total_len)
    twist_cos = jnp.cos(angles)
    twist_sin = jnp.sin(angles)
    part_re = local_re * twist_cos - local_im * twist_sin
    part_im = local_re * twist_sin + local_im * twist_cos
    cross_cos, cross_sin = angle_table(band_rows, groups, groups, -1.0)
    piece_re = lax.all_to_all(
        part_re.reshape(groups, 1, block_len), "tmpl", split_axis=0, concat_axis=1, tiled=True
    )
    piece_im = lax.all_to_all(
        part_im.reshape(groups, 1, block_len), "tmpl", split_axis=0, concat_axis=1, tiled=True
    )
    spec_re, spec_im = complex_left(cross_cos, cross_sin, piece_re[0], piece_im[0])
    white_re = spec_re * inv_psd * norm_scale
    white_im = spec_im * inv_psd * norm_scale
    white_re, white_im = in_one_piece((white_re, white_im), "tmpl", 1, 0)
    band_len = band_rows * sub_len
    white_re = white_re.reshape(band_len)
    white_im = white_im.reshape(band_len)
    frequency = jnp.arange(band_len, dtype=jnp.int32)
    tmpl_re, tmpl_im = template_parts(frequency, chirp_slope, chirp_curve, total_len, k_low, k_cut)
    coef_re = white_re * tmpl_re + white_im * tmpl_im
    coef_im = white_im * tmpl_re - white_re * tmpl_im
    widths = ((0, 0), (0, total_len - band_len))
    series_re, series_im = transform(jnp.pad(coef_re, widths), jnp.pad(coef_im, widths), 1.0)
    magnitude = (
        jnp.sqrt(series_re * series_re + series_im * series_im) / jnp.sqrt(sigma_sq)[..., None]
    )
    return magnitude[:, OR * groups :]


def solution(mesh):
    placed = (P("tmpl", "tm"), P(None, "tmpl"), P("tm", None), P("tmpl"), P("tmpl"))
    return jax.shard_map(
        local, mesh=mesh, in_specs=placed, out_specs=P("tmpl", "tm"), check_vma=False
    )
```

profile of v0, /device:TPU:1, one launch (start us, length us, event | category | flops | bytes accessed | tf_op | source)
XLA Modules:
  0.0 618.6 jit_solution(15087081567052045883)
XLA Ops:
  6.5 4.2 collective-permute-start
  10.7 2.7 add_select_fusion.1
  13.4 0.9 compare_select_fusion.2
  14.3 0.1 reshape.360
  14.4 0.0 copy-start.8
  14.4 5.2 fusion.65
  19.6 5.4 fusion.69
  25.1 4.8 convolution_add_fusion.3
  29.9 4.8 convolution_subtract_fusion.3
  34.7 1.7 fusion.120
  36.3 1.9 fusion.121
  38.2 1.7 convolution_subtract_fusion.2
  39.9 0.1 reshape.352
  40.0 1.7 convolution_add_fusion.2
  41.6 0.1 reshape.353
  41.7 1.2 multiply_add_fusion.2
  42.8 1.0 copy.42
  43.8 7.6 %all-to-all-start = ((f32[16,1,4096]{2,1,0:T(1,128)}), f32[16,1,4096]{2,1,0:T(1,128)S(1)}, u32[]{:S(2)}, u32[]{:S(2)}) async-start(f32[16,1,4096]{2,1,0:T(1,128)} %copy.42), calls=%async_computation | async-start | bytes 524288 | tf_op jit(solution)/shard_map/all_to_all | solution.py:150
  51.5 135.5 %gather_fusion = f32[24576]{0:T(1024)S(1)} fusion(f32[8192]{0:T(1024)S(1)} %bitcast.118, s32[24576]{0:T(1024)S(1)} %broadcast_clamp_fusion), kind=kCustom, calls=%fused_computation | custom fusion | bytes 294912 | tf_op jit(solution)/shard_map/jit(_take)/gather | solution.py:134
  187.0 0.8 multiply_reduce_fusion
  187.8 1.0 copy.43
  188.8 7.2 %all-to-all-start.1 = ((f32[16,1,4096]{2,1,0:T(1,128)}), f32[16,1,4096]{2,1,0:T(1,128)S(1)}, u32[]{:S(2)}, u32[]{:S(2)}) async-start(f32[16,1,4096]{2,1,0:T(1,128)} %copy.43), calls=%async_computation.1 | async-start | bytes 524288 | tf_op jit(solution)/shard_map/all_to_all | solution.py:153
  196.0 0.0 all-gather.2.cloned.1.call-start
  196.1 0.4 fusion.81
  196.5 0.4 fusion.79
  196.9 7.8 %all-to-all-done.1 = f32[16,1,4096]{2,1,0:T(1,128)S(1)} async-done(((f32[16,1,4096]{2,1,0:T(1,128)}), f32[16,1,4096]{2,1,0:T(1,128)S(1)}, u32[]{:S(2)}, u32[]{:S(2)}) %all-to-all-start.1) | async-done | bytes 262176 | tf_op jit(solution)/shard_map/all_to_all | solution.py:153
  204.7 0.4 fusion.25
  205.1 0.4 fusion.23
  205.5 0.8 pad_maximum_fusion.1
  206.3 0.0 all-gather.2.cloned.1.call-update
  206.3 0.0 copy-start.9
  206.3 17.6 %fusion.39 = (f32[64,16384]{1,0:T(8,128)}, f32[64,16384]{1,0:T(8,128)}) fusion(), kind=kLoop, calls=%fused_computation.74 | loop fusion | flops 14680064 | bytes 8388608 | tf_op jit(solution)/shard_map/sin | solution.py:48
  224.0 0.3 fusion.156
  224.2 0.1 copy.46
  224.3 0.3 fusion.155
  224.6 0.1 copy.49
  224.7 0.6 dynamic-slice
  225.3 1.3 dynamic-update-slice
  226.7 33.9 %all-reduce.2 = f32[16]{0:T(128)S(1)} all-reduce(f32[16]{0:T(128)S(1)} %dynamic-update-slice), channel_id=1, replica_groups=mesh['tm'=8,'tmpl'=16] {'tmpl'}, use_global_device_ids=true, to_apply=%add.2 | all-reduce | flops 16 | bytes 128
  260.6 0.6 reduce_sum.19
  261.7 2.7 fusion.52
  264.5 4.5 fusion.288
  269.0 3.6 mul.750
  272.6 2.0 mul.768
  274.5 55.4 %multiply_subtract_fusion.1 = (f32[2,393216]{1,0:T(2,128)S(1)}, f32[2,393216]{1,0:T(2,128)S(1)}) fusion(f32[393216]{0:T(1024)} %get-tuple-element.18, f32[393216]{0:T(1024)} %mul.768, f32[393216]{0:T(1024)} %get-tuple-element.17, f32[393216]{0:T(1024)} %mul.750, s32[393216]{0:T(1024)} %add_select_fusion.1, s32[2]{0:T(128)S(1)} %copy-done.6, s32[2]{0:T(128)S(1)} %copy-done.7), kind=kLoop, calls=%fused_computation.53 | loop fusion | flops 18874368 | bytes 14155792 | tf_op jit(solution)/shard_map/sub | solution.py:166
  329.9 13.3 %pad.7 = f32[2,1048576]{1,0:T(2,128)S(1)} pad(f32[2,393216]{1,0:T(2,128)S(1)} %get-tuple-element.12, f32[]{:T(128)} %constant.200.clone.1), padding=0_0x0_655360 | pad | bytes 11534340 | tf_op jit(solution)/shard_map/jit(_pad)/pad | solution.py:168
  343.2 13.0 %fusion.14 = f32[2,16384,64]{1,2,0:T(8,128)S(1)} fusion(f32[1,2,64,16384]{3,1,2,0:T(2,128)S(1)} %bitcast.127), kind=kOutput, calls=%fused_computation.17 | convolution fusion | flops 1610670080 | bytes 16777216 | tf_op jit(solution)/shard_map/qp,...pk->...qk/dot_general | solution.py:52
  356.2 13.4 %fusion.12 = f32[2,16384,64]{1,2,0:T(8,128)} fusion(f32[1,2,64,16384]{3,1,2,0:T(2,128)S(1)} %bitcast.128), kind=kOutput, calls=%fused_computation.15 | convolution fusion | flops 1610670080 | bytes 16777216 | tf_op jit(solution)/shard_map/qp,...pk->...qk/dot_general | solution.py:55
  369.6 13.1 %pad.8 = f32[2,1048576]{1,0:T(2,128)S(1)} pad(f32[2,393216]{1,0:T(2,128)S(1)} %get-tuple-element.11, f32[]{:T(128)} %constant.200.clone.1), padding=0_0x0_655360 | pad | bytes 11534340 | tf_op jit(solution)/shard_map/jit(_pad)/pad | solution.py:168
  382.6 13.5 %fusion.1 = f32[2,64,16384]{2,1,0:T(8,128)} fusion(f32[2,16384,64]{1,2,0:T(8,128)S(1)} %fusion.14, f32[1,2,64,16384]{3,1,2,0:T(2,128)S(1)} %bitcast.125), kind=kOutput, calls=%fused_computation.4 | convolution fusion | flops 1612767232 | bytes 25165824 | tf_op jit(solution)/shard_map/qp,...pk->...qk/dot_general | solution.py:52
  396.1 25.4 %multiply_add_fusion = (f32[2,64,16384]{2,1,0:T(8,128)}, f32[2,64,16384]{2,1,0:T(8,128)}) fusion(f32[2,64,16384]{2,1,0:T(8,128)} %fusion.1, f32[64,16384]{1,0:T(8,128)} %get-tuple-element.19, f32[64,16384]{1,0:T(8,128)} %get-tuple-element.20, f32[2,16384,64]{1,2,0:T(8,128)} %fusion.12, f32[1,2,64,16384]{3,1,2,0:T(2,128)} %bitcast.126), kind=kOutput, calls=%fused_computation.26 | convolution fusion | flops 1625350144 | bytes 50331648 | tf_op jit(solution)/shard_map/qp,...pk->...qk/dot_general | solution.py:55
  421.5 4.8 copy.70
  426.3 16.4 %fusion.2 = f32[2,64,128,128]{3,2,1,0:T(8,128)} fusion(f32[2,64,128,128]{3,2,1,0:T(8,128)S(1)} %bitcast.119), kind=kOutput, calls=%fused_computation.5 | convolution fusion | flops 3221454848 | bytes 16777216 | tf_op jit(solution)/shard_map/qp,...pk->...qk/dot_general | solution.py:55
  442.7 16.2 %fusion.4 = f32[2,64,128,128]{3,2,1,0:T(8,128)} fusion(f32[2,64,128,128]{3,2,1,0:T(8,128)S(1)} %bitcast.120), kind=kOutput, calls=%fused_computation.7 | convolution fusion | flops 3221454848 | bytes 16777216 | tf_op jit(solution)/shard_map/qp,...pk->...qk/dot_general | solution.py:52
  458.9 1.5 copy.69
  460.4 16.3 %fusion.8 = f32[2,64,128,128]{3,2,1,0:T(8,128)} fusion(f32[2,64,128,128]{3,2,1,0:T(8,128)S(1)} %bitcast.123), kind=kOutput, calls=%fused_computation.11 | convolution fusion | flops 3221454848 | bytes 16777216 | tf_op jit(solution)/shard_map/qp,...pk->...qk/dot_general | solution.py:52
  476.7 23.8 %fusion.17 = (f32[2,64,128,128]{2,3,1,0:T(8,128)}, f32[2,64,128,128]{2,3,1,0:T(8,128)}) fusion(f32[128,128]{0,1:T(8,128)S(1)} %copy.49, f32[128,128]{0,1:T(8,128)S(1)} %copy.46, f32[2,64,128,128]{3,2,1,0:T(8,128)} %fusion.2, f32[2,64,128,128]{3,2,1,0:T(8,128)} %fusion.8, f32[2,64,128,128]{3,2,1,0:T(8,128)} %fusion.4, f32[2,64,128,128]{3,2,1,0:T(8,128)} %bitcast.124), kind=kOutput, calls=%fused_computation.22 | convolution fusion | flops 3238232064 | bytes 50462720 | tf_op jit(solution)/shard_map/qp,...pk->...qk/dot_general | solution.py:55
  500.5 17.9 %fusion.103 = f32[2,64,128,128]{3,2,1,0:T(8,128)} fusion(f32[2,64,128,128]{2,3,1,0:T(8,128)} %get-tuple-element.8), kind=kOutput, calls=%fused_computation.162 | convolution fusion | flops 3221454848 | bytes 16777216 | tf_op jit(solution)/shard_map/dot_general | solution.py:65
  518.4 16.1 %fusion.107 = f32[2,64,128,128]{3,2,1,0:T(8,128)} fusion(f32[2,64,128,128]{2,3,1,0:T(8,128)S(1)} %copy-done.2), kind=kOutput, calls=%fused_computation.166 | convolution fusion | flops 3221454848 | bytes 16777216 | tf_op jit(solution)/shard_map/dot_general | solution.py:68
  534.5 16.3 %fusion.109 = f32[2,64,128,128]{3,2,1,0:T(8,128)} fusion(f32[2,64,128,128]{2,3,1,0:T(8,128)S(1)} %bitcast.122), kind=kOutput, calls=%fused_computation.168 | convolution fusion | flops 3221454848 | bytes 16777216 | tf_op jit(solution)/shard_map/dot_general | solution.py:65
  550.8 21.0 %divide_bitcast_fusion = f32[2,128,128,64]{1,2,3,0:T(8,128)} fusion(f32[2,64,128,128]{3,2,1,0:T(8,128)} %fusion.107, f32[2,64,128,128]{3,2,1,0:T(8,128)} %fusion.103, f32[2,64,128,128]{3,2,1,0:T(8,128)} %fusion.109, f32[]{:T(128)S(6)} %sqrt.12, f32[2,64,128,128]{2,3,1,0:T(8,128)S(1)} %bitcast.122), kind=kOutput, calls=%fused_computation.25 | convolution fusion | flops 3234037760 | bytes 41943044 | tf_op jit(solution)/shard_map/dot_general | solution.py:68
  571.8 16.6 %copy.54 = f32[2,128,128,64]{3,2,1,0:T(8,128)} copy(f32[2,128,128,64]{1,2,3,0:T(8,128)} %divide_bitcast_fusion) | data formatting | bytes 16777216 | tf_op jit(solution)/shard_map/div | solution.py:170
  588.4 18.4 %div.45 = f32[2,1048576]{1,0:T(2,128)} reshape(f32[2,128,128,64]{3,2,1,0:T(8,128)} %copy.54) | data formatting | bytes 16777216 | tf_op jit(solution)/shard_map/div | solution.py:170
  606.8 4.7 slice.20
  (35 shorter events, 0.1 us)
Async XLA Ops:
  6.5 44.9 %copy-start = (f32[1,8192]{1,0:T(1,128)S(1)}, f32[1,8192]{1,0:T(1,128)}, u32[]{:S(2)}) copy-start(f32[1,8192]{1,0:T(1,128)} %param.7) | copy-start | bytes 98308
  6.5 18.5 %collective-permute-start = (f32[32768]{0:T(1024)}, f32[32768]{0:T(1024)S(1)}, u32[]{:S(2)}, u32[]{:S(2)}) collective-permute-start(f32[32768]{0:T(1024)} %bitcast.133), channel_id=1, source_target_pairs={{0,16},{16,32},{32,48},{48,64},{64,80},{80,96},{96,112},{1,17},{17... | collective-permute-start | bytes 393224 | tf_op jit(solution)/shard_map/ppermute | solution.py:18
  14.4 10.7 %copy-start.8 = (f32[1,32768]{1,0:T(1,128)S(1)}, f32[1,32768]{1,0:T(1,128)}, u32[]{:S(2)}) copy-start(f32[1,32768]{1,0:T(1,128)} %param.5) | copy-start | bytes 393220
  43.8 145.0 %all-to-all-start = ((f32[16,1,4096]{2,1,0:T(1,128)}), f32[16,1,4096]{2,1,0:T(1,128)S(1)}, u32[]{:S(2)}, u32[]{:S(2)}) async-start(f32[16,1,4096]{2,1,0:T(1,128)} %copy.42), calls=%async_computation | async-start | bytes 524288 | tf_op jit(solution)/shard_map/all_to_all | solution.py:150
  51.4 135.6 %copy-start.5 = (s32[8,4096]{1,0:T(8,128)S(1)}, s32[8,4096]{1,0:T(8,128)}, u32[]{:S(2)}) copy-start(s32[8,4096]{1,0:T(8,128)} %param.6) | copy-start | bytes 393220
  188.8 15.9 %all-to-all-start.1 = ((f32[16,1,4096]{2,1,0:T(1,128)}), f32[16,1,4096]{2,1,0:T(1,128)S(1)}, u32[]{:S(2)}, u32[]{:S(2)}) async-start(f32[16,1,4096]{2,1,0:T(1,128)} %copy.43), calls=%async_computation.1 | async-start | bytes 524288 | tf_op jit(solution)/shard_map/all_to_all | solution.py:153
  196.0 68.4 %all-gather.2.cloned.1.call-start = ((), (), s32[]{:S(2)}) async-start(), calls=%async_computation.2 | async-start | bytes 4456448 | tf_op jit(solution)/shard_map/all_gather | solution.py:27
  206.3 18.4 %copy-start.9 = (u32[128]{0:T(128)S(1)}, u32[128]{0:T(128)}, u32[]{:S(2)}) copy-start(u32[128]{0:T(128)} %constant.242) | copy-start | bytes 1540
  269.0 5.6 copy-start.6
  269.0 5.6 copy-start.7
  382.6 13.5 %copy-start.4 = (f32[2,1048576]{1,0:T(2,128)}, f32[2,1048576]{1,0:T(2,128)S(1)}, u32[]{:S(2)}) copy-start(f32[2,1048576]{1,0:T(2,128)S(1)} %pad.8) | copy-start | bytes 25165828
  442.7 16.2 %slice-start.2 = ((s8[8388608]{0:T(1024)(128)(4,1)}), s8[4194304]{0:T(1024)(128)(4,1)S(1)}, s32[]{:S(2)}) async-start(s8[8388608]{0:T(1024)(128)(4,1)} %bitcast.129), calls=%async_computation.5 | async-start | bytes 8388608
  442.7 16.2 %slice-start.3 = ((s8[8388608]{0:T(1024)(128)(4,1)}), s8[4194304]{0:T(1024)(128)(4,1)S(1)}, s32[]{:S(2)}) async-start(s8[8388608]{0:T(1024)(128)(4,1)} %bitcast.129), calls=%async_computation.6 | async-start | bytes 8388608
  460.4 16.4 %copy-start.3 = (f32[16,8,128,128]{3,2,1,0:T(8,128)}, f32[16,8,128,128]{3,2,1,0:T(8,128)S(1)}, u32[]{:S(2)}) copy-start(f32[16,8,128,128]{3,2,1,0:T(8,128)S(1)} %copy.69) | copy-start | bytes 25165828
  500.5 17.9 %copy-start.2 = (f32[2,64,128,128]{2,3,1,0:T(8,128)S(1)}, f32[2,64,128,128]{2,3,1,0:T(8,128)}, u32[]{:S(2)}) copy-start(f32[2,64,128,128]{2,3,1,0:T(8,128)} %get-tuple-element.8) | copy-start | bytes 25165828
  500.5 33.9 %slice-start = ((s8[8388608]{0:T(1024)(128)(4,1)}), s8[4194304]{0:T(1024)(128)(4,1)S(1)}, s32[]{:S(2)}) async-start(s8[8388608]{0:T(1024)(128)(4,1)} %bitcast.121), calls=%async_computation.3 | async-start | bytes 8388608
  518.4 16.1 %slice-start.1 = ((s8[8388608]{0:T(1024)(128)(4,1)}), s8[4194304]{0:T(1024)(128)(4,1)S(1)}, s32[]{:S(2)}) async-start(s8[8388608]{0:T(1024)(128)(4,1)} %bitcast.121), calls=%async_computation.4 | async-start | bytes 8388608
  588.4 23.1 %copy-start.1 = (f32[1,8192]{1,0:T(1,128)S(1)}, f32[1,8192]{1,0:T(1,128)}, u32[]{:S(2)}) copy-start(f32[1,8192]{1,0:T(1,128)} %param.7) | copy-start | bytes 98308
Sparse Core Ops, SparseCore 0:
  206.4 54.6 all-gather.1
where the time goes:
time: 624 us; the launch traced here: 619 us
  matrix products  238 us (38%)
  local copies, waits for them, and re-layouts  222 us (36%)
  other arithmetic  83.2 us (13%)
  blocking collectives  33.9 us (5%)
  starting transfers between devices  19 us (3%)
  between operations  14.6 us (2%)
  waiting for transfers between devices  7.82 us (1%)
    gather x2, local copies, waits for them, and re-layouts, local(): inv_psd = 1.0 / jnp.take(psd_values[0], psd_bins[:band_rows])  136 us
    sub x1, other arithmetic, local(): coef_im = white_im * tmpl_re - white_re * tmpl_im  55.4 us
    dot_general x4, matrix products, complex_left(): jnp.einsum('qp,...pk->...qk', cos_part, imag_part, precision=HIGHEST)  47.4 us
    dot_general x4, matrix products, complex_left(): jnp.einsum('qp,...pk->...qk', sin_part, real_part, precision=HIGHEST)  42.4 us
    dot_general x4, matrix products, complex_left(): jnp.einsum('qp,...pk->...qk', sin_part, imag_part, precision=HIGHEST)  35.5 us
    div x2, local copies, waits for them, and re-layouts, local(): jnp.sqrt(series_re * series_re + series_im * series_im)  35 us
    dot_general x4, matrix products, complex_left(): jnp.einsum('qp,...pk->...qk', cos_part, real_part, precision=HIGHEST)  34.5 us
    unnamed x1, blocking collectives  33.9 us
  transfers between devices with their start and end apart: 4, of which 1 were waited for; matrix products, arithmetic and copies ran while one was open for 28% of the time, Pallas kernels for 0%

commit v1 on v0

v1 whole, which is shorter than its diff:
```python
import functools
import math

import jax
import jax.numpy as jnp
import ml_dtypes
import numpy as np
from jax import lax
from jax.experimental import pallas as pl
from jax.experimental.pallas import tpu as pltpu
from jax.sharding import PartitionSpec as P

N = 1 << 20
K_LOW = N // 200
BF = jnp.bfloat16
F32 = jnp.float32


def halves(x):
    x = np.asarray(x, np.float32)
    hi = x.astype(ml_dtypes.bfloat16)
    lo = (x - hi.astype(np.float32)).astype(ml_dtypes.bfloat16)
    return hi, lo


def unit(num, den, sign):
    ang = (num % den) * (sign * 2.0 * math.pi / den)
    return np.cos(ang), np.sin(ang)


LANE = np.arange(128)
B1 = 64 * (LANE // 64) + 8 * (LANE % 8) + (LANE // 8) % 8


@functools.lru_cache(None)
def tables():
    t = {}
    rows = np.arange(512)
    low = rows // 8 + 64 * (rows % 8)
    c, s = unit(low[:, None] * np.arange(512)[None, :], 512, -1)
    hi, lo = halves(np.concatenate([c, s]))
    t["l1"] = np.stack([hi, lo])
    c, s = unit(low[:, None] * LANE[None, :], 65536, -1)
    t["tw1"] = np.stack([c, s]).astype(np.float32)
    h, al, bh = LANE // 64, (LANE // 8) % 8, LANE % 8
    top = 16 * al + 8 * h + bh
    c, s = unit(LANE[:, None] * top[None, :], 128, -1)
    hi, lo = halves(np.block([[c, s], [-s, c]]))
    t["m2"] = np.concatenate([hi, hi, lo])
    q = low[:, None] + 512 * top[None, :]
    c, s = unit(np.arange(16)[:, None, None] * q[None], N, -1)
    t["tj"] = np.stack([c, s], 1).astype(np.float32)
    a = np.arange(48)
    c, s = unit(a[:, None] * LANE[None, :], 128, 1)
    hi, lo = halves(np.block([[c, s], [-s, c]]))
    t["e1"] = np.concatenate([hi, hi, lo])
    c, s = unit(LANE[:, None] * B1[None, :], 128, 1)
    hi, lo = halves(np.block([[c, -s], [s, c]]))
    t["e2"] = np.concatenate([hi, hi, lo], 1)
    b = 64 * B1[None, :] + np.arange(64)[:, None]
    c, s = unit(b[:, :, None] * LANE[None, None, :], N, 1)
    t["tw"] = np.concatenate([c, s], 1).astype(np.float32)
    c, s = unit(np.arange(64)[:, None] * LANE[None, :], 8192, 1)
    t3 = np.zeros((64, 128, 128), np.float32)
    t3[:, :, 0], t3[:, :, 1] = c, s
    t["tw3"] = t3
    k = np.arange(6)[:, None] * 65536 + np.arange(65536)[None, :]
    amp = np.where(k >= K_LOW, (np.maximum(k, 1) / K_LOW) ** (-7.0 / 6.0), 0.0)
    amp = np.concatenate([amp, np.zeros((2, 65536))])
    t["amp"] = amp.reshape(8, 16, 4096).transpose(1, 0, 2).astype(np.float32)
    return t


def split2(x):
    hi = x.astype(BF)
    lo = (x - hi.astype(F32)).astype(BF)
    return hi, lo


def dot(a, b):
    return jnp.dot(a, b, preferred_element_type=F32)


def psd_kernel(me, bins, vals, amp, g_out, sig_out):
    def tile(i, total):
        at = pl.multiple_of(i * 128, 128)
        idx = bins[:, pl.ds(at, 128)]
        hi, lo = idx >> 7, idx & 127
        acc = jnp.ones((8, 128), F32)
        for h in range(64):
            row = jnp.broadcast_to(vals[h : h + 1, :], (8, 128))
            got = jnp.take_along_axis(row, lo, axis=1)
            acc = jnp.where(hi == h, got, acc)
        inv = 1.0 / acc
        a = amp[0, :, pl.ds(at, 128)]
        g = inv * a
        g_out[:, pl.ds(at, 128)] = g * (1.0 / 1024.0)
        return total + g * a

    total = lax.fori_loop(0, 32, tile, jnp.zeros((8, 128), F32))
    sig_out[...] = jnp.broadcast_to(jnp.sum(total, keepdims=True), (8, 128))


def psd_call(me, bins, vals, amp):
    return pl.pallas_call(
        psd_kernel,
        grid_spec=pltpu.PrefetchScalarGridSpec(
            num_scalar_prefetch=1,
            grid=(1,),
            in_specs=[
                pl.BlockSpec((8, 4096), lambda i, m: (0, 0)),
                pl.BlockSpec((64, 128), lambda i, m: (0, 0)),
                pl.BlockSpec((1, 8, 4096), lambda i, m: (m[0], 0, 0)),
            ],
            out_specs=[
                pl.BlockSpec((8, 4096), lambda i, m: (0, 0)),
                pl.BlockSpec((8, 128), lambda i, m: (0, 0)),
            ],
        ),
        out_shape=[
            jax.ShapeDtypeStruct((8, 4096), F32),
            jax.ShapeDtypeStruct((8, 128), F32),
        ],
    )(me, bins, vals, amp)


def fwd_kernel(me, tail, own, l1, tw1, m2, tj, extra, out):
    th, tl = split2(tail[...])
    oh, ol = split2(own[...])
    xh = jnp.concatenate([th, oh])
    xl = jnp.concatenate([tl, ol])
    y = dot(l1[0], xh) + dot(l1[0], xl) + dot(l1[1], xh)
    yr, yi = y[:512], y[512:]
    c, s = tw1[0], tw1[1]
    yr, yi = yr * c - yi * s, yr * s + yi * c
    rh, rl = split2(yr)
    ih, il = split2(yi)
    f = dot(jnp.concatenate([rh, ih, rl, il, rh, ih], 1), m2[...])
    fr, fi = f[:, :128], f[:, 128:]
    c, s = tj[0, 0], tj[0, 1]
    gr, gi = fr * c - fi * s, fr * s + fi * c
    for d in range(16):
        out[d, 0:32, :] = gr[32 * d : 32 * d + 32]
        out[d, 32:64, :] = gi[32 * d : 32 * d + 32]
        out[d, 64:80, :] = extra[d]


def fwd_call(me, tail, own, l1, tw1, m2, tj, extra):
    def whole(x):
        return pl.BlockSpec(x.shape, lambda i, m, n=x.ndim: (0,) * n)

    return pl.pallas_call(
        fwd_kernel,
        grid_spec=pltpu.PrefetchScalarGridSpec(
            num_scalar_prefetch=1,
            grid=(1,),
            in_specs=[
                whole(tail),
                whole(own),
                whole(l1),
                whole(tw1),
                whole(m2),
                pl.BlockSpec((1, 2, 512, 128), lambda i, m: (m[0], 0, 0, 0)),
                whole(extra),
            ],
            out_specs=pl.BlockSpec((16, 80, 128), lambda i, m: (0, 0, 0)),
        ),
        out_shape=jax.ShapeDtypeStruct((16, 80, 128), F32),
        compiler_params=pltpu.CompilerParams(vmem_limit_bytes=40 << 20),
    )(me, tail, own, l1, tw1, m2, tj, extra)


def swap_groups(x):
    row = lax.broadcasted_iota(jnp.int32, x.shape, 0)
    lane = lax.broadcasted_iota(jnp.int32, x.shape, 1)
    n = x.shape[0]
    for t in range(3):
        d, w = 1 << t, 8 << t
        rb, lb = (row >> t) & 1, (lane >> (3 + t)) & 1
        up = pltpu.roll(pltpu.roll(x, d, 0), 128 - w, 1)
        dn = pltpu.roll(pltpu.roll(x, n - d, 0), w, 1)
        x = jnp.where(rb == lb, x, jnp.where(rb == 1, up, dn))
    return x


def mix_kernel(p, w_out, sig_out):
    lane = lax.broadcasted_iota(jnp.int32, (8, 128), 1)
    for ah in range(6):
        re = jnp.zeros((32, 128), F32)
        im = jnp.zeros((32, 128), F32)
        for j in range(16):
            c = math.cos(2 * math.pi * (j * ah % 16) / 16)
            s = -math.sin(2 * math.pi * (j * ah % 16) / 16)
            pr = p[80 * j : 80 * j + 32, :]
            pi = p[80 * j + 32 : 80 * j + 64, :]
            re = re + (pr * c - pi * s)
            im = im + (pr * s + pi * c)
        re, im = swap_groups(re), swap_groups(im)
        for pair in range(2):
            row = 64 + 2 * ah + pair
            g0 = p[pl.ds(row, 8, stride=160), :]
            g1 = p[pl.ds(row + 80, 8, stride=160), :]
            g = (
                jnp.where(lane < 64, g0, pltpu.roll(g1, 64, 1)),
                jnp.where(lane < 64, pltpu.roll(g0, 64, 1), g1),
            )
            for odd in range(2):
                b = 2 * pair + odd
                w_out[b, 8 * ah : 8 * ah + 8, :] = re[8 * b : 8 * b + 8] * g[odd]
                w_out[b, 48 + 8 * ah : 56 + 8 * ah, :] = im[8 * b : 8 * b + 8] * g[odd]
    sig = jnp.sum(p[pl.ds(76, 16, stride=80), :], axis=0, keepdims=True)
    sig_out[...] = jnp.broadcast_to(lax.rsqrt(sig), (8, 128))


def mix_call(p):
    return pl.pallas_call(
        mix_kernel,
        out_shape=[
            jax.ShapeDtypeStruct((4, 96, 128), F32),
            jax.ShapeDtypeStruct((8, 128), F32),
        ],
    )(p)


def inv_kernel(b0s, w, ph, tw, tw3, e1, e2, *rest):
    h_out = rest[-1]
    wr, wi = w[0, 0:48, :], w[0, 48:96, :]
    zr, zi = [], []
    for m in range(2):
        c, s = ph[m, 0, 0], ph[m, 0, 1]
        v = jnp.concatenate([wr * c - wi * s, wr * s + wi * c])
        vh, vl = split2(v)
        g = lax.dot_general(
            jnp.concatenate([vh, vl, vh]),
            e1[...],
            (((0,), (0,)), ((), ())),
            preferred_element_type=F32,
        )
        gr, gi = g[:, :128], g[:, 128:]
        c, s = tw[0, :128], tw[0, 128:]
        zr.append(gr * c - gi * s)
        zi.append(gr * s + gi * c)
    z = jnp.concatenate([jnp.concatenate(zr, 1), jnp.concatenate(zi, 1)], 0)
    zh, zl = split2(z)
    h = dot(e2[...], jnp.concatenate([zh, zl, zh], 0))
    c, s = tw3[0, :, 0:1], tw3[0, :, 1:2]
    hr, hi = h[:128], h[128:]
    h_out[0, 0] = hr * c - hi * s
    h_out[0, 1] = hr * s + hi * c


def inv_call(b0s, w, ph, tw, tw3, e1, e2, prev):
    count = w.shape[0]
    in_specs = [
        pl.BlockSpec((1, 96, 128), lambda i, b: (i, 0, 0)),
        pl.BlockSpec((2, 1, 2, 48, 128), lambda i, b: (0, b[i], 0, 0, 0)),
        pl.BlockSpec((1, 256, 128), lambda i, b: (b[i], 0, 0)),
        pl.BlockSpec((1, 128, 128), lambda i, b: (b[i], 0, 0)),
        pl.BlockSpec((288, 256), lambda i, b: (0, 0)),
        pl.BlockSpec((256, 768), lambda i, b: (0, 0)),
    ]
    args = [b0s, w, ph, tw, tw3, e1, e2]
    alias = {}
    if prev is not None:
        in_specs.append(pl.BlockSpec(memory_space=pl.ANY))
        args.append(prev)
        alias = {7: 0}
    return pl.pallas_call(
        inv_kernel,
        grid_spec=pltpu.PrefetchScalarGridSpec(
            num_scalar_prefetch=1,
            grid=(count,),
            in_specs=in_specs,
            out_specs=pl.BlockSpec((1, 2, 128, 256), lambda i, b: (b[i], 0, 0, 0)),
        ),
        out_shape=jax.ShapeDtypeStruct((64, 2, 128, 256), F32),
        input_output_aliases=alias,
        compiler_params=pltpu.CompilerParams(vmem_limit_bytes=32 << 20),
        cost_estimate=pl.CostEstimate(
            flops=count * 300_000_000, bytes_accessed=count * 700_000, transcendentals=0
        ),
    )(*args)


def cmul(x, num, den):
    num %= den
    re, im = x
    if num == 0:
        return re, im
    if 4 * num == den:
        return -im, re
    if 2 * num == den:
        return -re, -im
    if 4 * num == 3 * den:
        return im, -re
    c = float(math.cos(2 * math.pi * num / den))
    s = float(math.sin(2 * math.pi * num / den))
    if (8 * num) % den == 0:
        r = math.sqrt(0.5)
        a = r if c > 0 else -r
        b = r if s > 0 else -r
        if a == b:
            return a * (re - im), a * (re + im)
        return a * (re + im), a * (im - re)
    return re * c - im * s, re * s + im * c


def add(x, y):
    return x[0] + y[0], x[1] + y[1]


def sub(x, y):
    return x[0] - y[0], x[1] - y[1]


def fft4(x):
    p, q = add(x[0], x[2]), sub(x[0], x[2])
    r, s = add(x[1], x[3]), sub(x[1], x[3])
    s = (-s[1], s[0])
    return [add(p, r), add(q, s), sub(p, r), sub(q, s)]


def out_kernel(h, sig, out, mid):
    scale = sig[...]
    for m in range(2):
        at = slice(128 * m, 128 * m + 128)
        for lo in range(8):
            x = [(h[8 * hi + lo, 0, :, at], h[8 * hi + lo, 1, :, at]) for hi in range(8)]
            ev, od = fft4(x[0::2]), fft4(x[1::2])
            for f in range(4):
                o = cmul(od[f], f, 8)
                for f2, v in ((f, add(ev[f], o)), (f + 4, sub(ev[f], o))):
                    v = cmul(v, lo * f2, 64)
                    mid[f2, lo, 0] = v[0]
                    mid[f2, lo, 1] = v[1]
        for f2 in range(8):
            x = [(mid[f2, lo, 0], mid[f2, lo, 1]) for lo in range(8)]
            ev, od = fft4(x[0::2]), fft4(x[1::2])
            for f in range(4):
                v = sub(ev[f], cmul(od[f], f, 8))
                mag = jnp.sqrt(v[0] * v[0] + v[1] * v[1]) * scale
                out[f2 + 8 * f, pl.ds(m, 8, stride=2), :] = mag


def out_call(h, sig):
    return pl.pallas_call(
        out_kernel,
        grid=(16,),
        in_specs=[
            pl.BlockSpec((64, 2, 8, 256), lambda i: (0, 0, i, 0)),
            pl.BlockSpec((8, 128), lambda i: (0, 0)),
        ],
        out_specs=pl.BlockSpec((32, 16, 128), lambda i: (0, i, 0)),
        out_shape=jax.ShapeDtypeStruct((32, 256, 128), F32),
        scratch_shapes=[pltpu.VMEM((8, 8, 2, 8, 128), F32)],
        compiler_params=pltpu.CompilerParams(vmem_limit_bytes=32 << 20),
    )(h, sig)


def place(y, x, c):
    return (y % 2 * 4 + x % 4) * 2 + c


def sent(v, dy, dx, dc):
    route = [
        (place(y, x, c), place(y + dy, x + dx, (c + dc) % 2))
        for y in range(2)
        for x in range(4)
        for c in range(2)
    ]
    return lax.ppermute(v, "tmpl", route)


def phases(chirp_slope, chirp_curve):
    s, c = chirp_slope[:, None, None], chirp_curve[:, None, None]
    b0 = jnp.arange(64, dtype=jnp.int32)
    b = 64 * jnp.asarray(B1, jnp.int32)[None, :] + b0[:, None]
    p = (s * b[None] + c * (b * b % N)[None]) % N
    ang = p.astype(F32) * (2 * math.pi / N)
    pc, ps = jnp.cos(ang)[:, :, None, :], jnp.sin(ang)[:, :, None, :]
    a = jnp.arange(48, dtype=jnp.int32)
    p = a[None, None, :] * ((s + 2 * c * b0[None, :, None]) % 128) % 128
    ang = p.astype(F32) * (2 * math.pi / 128)
    qc, qs = jnp.cos(ang)[:, :, :, None], jnp.sin(ang)[:, :, :, None]
    return jnp.stack([pc * qc - ps * qs, pc * qs + ps * qc], 2)


def local(strain, psd_bins, psd_values, chirp_slope, chirp_curve):
    t = {k: jnp.asarray(v) for k, v in tables().items()}
    member = lax.axis_index("tmpl")
    me = member.astype(jnp.int32).reshape(1)
    own = strain.reshape(256, 128)
    count = lax.axis_size("tm")
    tail = lax.ppermute(own, "tm", [(i, i + 1) for i in range(count - 1)])

    g, sig = psd_call(me, psd_bins, psd_values.reshape(64, 128), t["amp"])
    g = g[:6].reshape(6, 8, 8, 16, 4).transpose(3, 0, 4, 2, 1).reshape(16, 12, 128)
    sig = jnp.broadcast_to(sig[0, 0], (16, 4, 128))
    extra = jnp.concatenate([g, sig], 1)

    sent_out = fwd_call(me, tail, own, t["l1"], t["tw1"], t["m2"], t["tj"], extra)
    parts = lax.all_to_all(sent_out, "tmpl", split_axis=0, concat_axis=0, tiled=True)
    w, scale = mix_call(parts.reshape(1280, 128))

    ph = phases(chirp_slope, chirp_curve)
    y, x, c = member // 8, member // 2 % 4, member % 2

    def ids(dy, dx, dc, rows):
        d = ((y + dy) % 2 * 4 + (x + dx) % 4) * 2 + (c + dc) % 2
        return (4 * d + jnp.arange(rows.start, rows.stop)).astype(jnp.int32)

    def work(blocks, prev):
        mine = jnp.concatenate([v for v, *_ in blocks])
        other = sent(mine, 0, 0, 1)
        both = jnp.concatenate([mine, other])
        order = [ids(dy, dx, 0, rows) for _, dy, dx, rows in blocks]
        order += [ids(dy, dx, 1, rows) for _, dy, dx, rows in blocks]
        return inv_call(
            jnp.concatenate(order), both, ph, t["tw"], t["tw3"], t["e1"], t["e2"], prev
        )

    full, first, last = slice(0, 4), slice(0, 2), slice(2, 4)
    up = sent(w, 1, 0, 0)
    right = sent(w, 0, 1, 0)
    left = sent(w, 0, -1, 0)
    h = work([(w, 0, 0, full)], None)
    right2 = sent(jnp.concatenate([up, right[:2]]), 0, 1, 0)
    left2 = sent(jnp.concatenate([up, left[2:]]), 0, -1, 0)
    h = work([(up, 1, 0, full), (right, 0, -1, full), (left, 0, 1, full)], h)
    right3 = sent(right2[:2], 0, 1, 0)
    left3 = sent(left2[2:4], 0, -1, 0)
    h = work(
        [
            (right2[:4], 1, -1, full),
            (left2[:4], 1, 1, full),
            (right2[4:], 0, -2, first),
            (left2[4:], 0, 2, last),
        ],
        h,
    )
    h = work([(right3, 1, -2, first), (left3, 1, 2, last)], h)
    out = out_call(h, scale)
    return out.reshape(4096, 2, 128).transpose(1, 0, 2).reshape(2, 4096 * 128)


def solution(mesh):
    placed = (P("tmpl", "tm"), P(None, "tmpl"), P("tm", None), P("tmpl"), P("tmpl"))
    return jax.shard_map(
        local, mesh=mesh, in_specs=placed, out_specs=P("tmpl", "tm"), check_vma=False
    )
```

time: 624 us -> 153 us (0.25)
  matrix products: 238 us -> 0 us
  local copies, waits for them, and re-layouts: 222 us -> 25.2 us
  Pallas kernels: 0 us -> 69.2 us
  other arithmetic: 83.2 us -> 16.9 us
  blocking collectives: 33.9 us -> 0 us
  between operations: 14.6 us -> 0.49 us
  starting transfers between devices: 19 us -> 27.6 us
    dot_general x24 -> x0, matrix products: 238 us -> none  [the longest x4 47.4 us: complex_left(): jnp.einsum('qp,...pk->...qk', cos_part, imag_part, precision=HIGHEST)]
    gather x2 -> x0, local copies, waits for them, and re-layouts: 136 us -> none  [local(): inv_psd = 1.0 / jnp.take(psd_values[0], psd_bins[:band_rows])]
    pallas_call x0 -> x8, Pallas kernels: none -> 69.2 us  [the longest x4 47 us: inv_call(): pl.pallas_call(inv_kernel, grid_spec=pltpu.PrefetchScalarGridSpec(num_sca...]
    sub x1, other arithmetic: 55.4 us -> 3.26 us  [phases(): return jnp.stack([pc * qc - ps * qs, pc * qs + ps * qc], 2)]
    div x2 -> x0, local copies, waits for them, and re-layouts: 35 us -> none  [local(): jnp.sqrt(series_re * series_re + series_im * series_im)]
    unnamed x1 -> x0, blocking collectives: 33.9 us -> none
    pad x2 -> x0, local copies, waits for them, and re-layouts: 26.3 us -> none  [the longest x1 13.3 us: local(): jnp.pad(coef_re, widths)]
    sin x2 -> x0, other arithmetic: 17.9 us -> none  [angle_table(): return (jnp.cos(angles), jnp.sin(angles))]
  transfers between devices with their start and end apart: 4 -> 13, of which waited for: 1 -> 5; matrix products, arithmetic and copies ran while one was open for 28% -> 22% of each run, Pallas kernels for 0% -> 20%
where the time goes in v1:
time: 153 us; the launch traced here: 152 us
  Pallas kernels  69.2 us (45%)
  starting transfers between devices  27.6 us (18%)
  local copies, waits for them, and re-layouts  25.2 us (16%)
  other arithmetic  16.9 us (11%)
  waiting for transfers between devices  12.7 us (8%)
    pallas_call x4, Pallas kernels, inv_call(): pl.pallas_call(inv_kernel, grid_spec=pltpu.PrefetchScalarGridSpec(num_sca...  47 us
    ppermute x11, starting transfers between devices, sent(): return lax.ppermute(v, 'tmpl', route)  15.9 us
    pallas_call x1, Pallas kernels, out_call(): pl.pallas_call(out_kernel, grid=(16,), in_specs=[pl.BlockSpec((64, 2, 8,...  10.4 us
    unnamed x30, local copies, waits for them, and re-layouts  9.2 us
    all_to_all x1, waiting for transfers between devices, local(): lax.all_to_all(sent_out, 'tmpl', split_axis=0, concat_axis=0, tiled=True)  8.74 us
    all_to_all x1, starting transfers between devices, local(): lax.all_to_all(sent_out, 'tmpl', split_axis=0, concat_axis=0, tiled=True)  7.61 us
    reshape x2, local copies, waits for them, and re-layouts, local(): g[:6].reshape(6, 8, 8, 16, 4).transpose(3, 0, 4, 2, 1).reshape(16, 12, 128)  7.28 us
    pallas_call x1, Pallas kernels, psd_call(): pl.pallas_call(psd_kernel, grid_spec=pltpu.PrefetchScalarGridSpec(num_sca...  6.51 us
  transfers between devices with their start and end apart: 13, of which 5 were waited for; matrix products, arithmetic and copies ran while one was open for 22% of the time, Pallas kernels for 20%

profile of v1, /device:TPU:1, one launch (start us, length us, event | category | flops | bytes accessed | tf_op | source)
XLA Modules:
  0.0 152.0 jit_solution(5087124350613697417)
XLA Ops:
  0.0 4.0 %collective-permute-start = (f32[256,128]{1,0:T(8,128)}, f32[256,128]{1,0:T(8,128)S(1)}, u32[]{:S(2)}, u32[]{:S(2)}) collective-permute-start(f32[256,128]{1,0:T(8,128)} %bitcast.15), channel_id=1, source_target_pairs={{0,16},{16,32},{32,48},{48,64},{64,80},{80,96},{96,112},{1,17},{17... | collective-permute-start | bytes 393224 | tf_op jit(solution)/shard_map/ppermute | solution.py:394
  4.2 0.7 iota_add_fusion
  4.9 0.7 broadcast_multiply_fusion
  5.6 1.3 and_select_fusion
  6.9 1.7 %fusion.10 = (f32[2,64,128]{2,1,0:T(8,128)}, f32[2,64,128]{2,1,0:T(8,128)}) fusion(s32[64,128]{1,0:T(8,128)S(1)} %get-tuple-element.32, s32[2]{0:T(128)} %param.19, s32[64,128]{1,0:T(8,128)S(1)} %get-tuple-element.31, s32[2]{0:T(128)} %param.18), kind=kLoop, calls=%fused_computation.30 | loop fusion | flops 262144 | bytes 196624 | tf_op jit(solution)/shard_map/cos | solution.py:380
  8.6 0.6 iota_add_fusion.7
  9.1 0.6 iota_add_fusion.5
  9.7 0.6 iota_add_fusion.13
  10.3 0.5 iota_add_fusion.10
  10.8 0.6 fusion.15
  11.4 0.5 iota_add_fusion.9
  12.0 0.6 fusion.18
  12.6 0.6 iota_add_fusion.15
  13.2 0.1 pad_add_fusion.1.b0s
  13.2 6.5 %shard_map.145 = (f32[8,4096]{1,0:T(8,128)}, f32[8,128]{1,0:T(8,128)}) custom-call(s32[1]{0:T(128)} %bitcast.me, s32[8,4096]{1,0:T(8,128)} %bins.1, f32[64,128]{1,0:T(8,128)} %bitcast.20, f32[16,8,4096]{2,1,0:T(8,128)} %constant.270.clone.amp), custom_call_target="tpu_custom_call" | custom-call | tf_op jit(solution)/shard_map/pallas_call | solution.py:105
  19.7 5.8 %reshape.194 = f32[6,8,8,16,4]{4,3,2,1,0:T(8,128)} reshape(f32[6,4096]{1,0:T(8,128)} %bitcast.19) | data formatting | bytes 196608 | tf_op jit(solution)/shard_map/reshape | solution.py:397
  25.6 5.2 %copy.21 = f32[16,6,4,8,8]{0,4,3,2,1:T(8,128)} copy(f32[16,6,4,8,8]{2,0,3,4,1:T(8,128)} %bitcast.17) | data formatting | bytes 196608 | tf_op jit(solution)/shard_map/transpose | solution.py:397
  30.8 1.4 copy.22
  32.2 1.2 slice.31
  33.4 0.7 concatenate.46.extra
  34.1 0.8 concatenate.54.b0s
  34.8 0.8 concatenate.51.b0s
  35.6 0.8 pad_add_fusion.b0s
  36.4 0.0 collective-permute-done.tail
  36.4 0.0 copy-start.2
  36.4 3.4 %copy-done.2 = f32[16,2,512,128]{3,2,1,0:T(8,128)S(1)} copy-done((f32[16,2,512,128]{3,2,1,0:T(8,128)S(1)}, f32[16,2,512,128]{3,2,1,0:T(8,128)}, u32[]{:S(2)}) %copy-start.2) | copy-done | bytes 8388632
  39.8 2.4 %shard_map.146 = f32[16,80,128]{2,1,0:T(8,128)} custom-call(s32[1]{0:T(128)} %bitcast.me, f32[256,128]{1,0:T(8,128)S(1)} %collective-permute-done.tail, f32[256,128]{1,0:T(8,128)S(1)} %bitcast.16, bf16[2,1024,512]{2,1,0:T(8,128)(2,1)S(1)} %copy-done.5, f32[2,512,128]{2,1,0:T(8,128)S(1)} %copy-done.6, bf16[768,256]{1,0:T(8,128)(2,1)S(1)} %copy-done.7, ...), custom_call_target="tpu_custom_call" | custom-call | tf_op jit(solution)/shard_map/pallas_call | solution.py:152
  42.2 7.6 %all-to-all-start = ((f32[16,80,128]{2,1,0:T(8,128)}), f32[16,80,128]{2,1,0:T(8,128)}, u32[]{:S(2)}, u32[]{:S(2)}) async-start(f32[16,80,128]{2,1,0:T(8,128)} %shard_map.146), calls=%async_computation | async-start | bytes 1310720 | tf_op jit(solution)/shard_map/all_to_all | solution.py:402
  49.8 1.0 fusion.13
  50.8 3.3 %multiply_subtract_fusion = (f32[2,64,1,48,128]{4,3,2,1,0:T(8,128)S(1)}, f32[2,64,1,48,128]{4,3,2,1,0:T(8,128)}) fusion(f32[2,64,48]{2,1,0:T(8,128)S(1)} %get-tuple-element.30, f32[2,64,128]{2,1,0:T(8,128)S(1)} %copy-done.11, f32[2,64,48]{2,1,0:T(8,128)S(1)} %get-tuple-element.29, f32[2,64,128]{2,1,0:T(8,128)S(1)} %copy-done.10), kind=kLoop, calls=%fused_computation.2 | loop fusion | flops 4718592 | bytes 6471680 | tf_op jit(solution)/shard_map/sub | solution.py:385
  54.1 8.7 %all-to-all-done = f32[16,80,128]{2,1,0:T(8,128)} async-done(((f32[16,80,128]{2,1,0:T(8,128)}), f32[16,80,128]{2,1,0:T(8,128)}, u32[]{:S(2)}, u32[]{:S(2)}) %all-to-all-start) | async-done | bytes 655392 | tf_op jit(solution)/shard_map/all_to_all | solution.py:402
  62.8 2.8 %shard_map.147 = (f32[4,96,128]{2,1,0:T(8,128)}, f32[8,128]{1,0:T(8,128)}) custom-call(f32[1280,128]{1,0:T(8,128)} %bitcast.6.p), custom_call_target="tpu_custom_call" | custom-call | tf_op jit(solution)/shard_map/pallas_call | solution.py:216
  65.6 0.7 collective-permute-start.1
  66.3 0.0 collective-permute-start.2
  66.3 2.7 %collective-permute-start.5 = (f32[4,96,128]{2,1,0:T(8,128)}, f32[4,96,128]{2,1,0:T(8,128)S(1)}, u32[]{:S(2)}, u32[]{:S(2)}) collective-permute-start(f32[4,96,128]{2,1,0:T(8,128)} %get-tuple-element.11), channel_id=1, source_target_pairs={{0,6},{1,7},{2,0},{3,1},{4,2},{5,3},{6,4},{7,5},{8,14},{9,15},{10,... | collective-permute-start | bytes 589832 | tf_op jit(solution)/shard_map/ppermute | solution.py:371
  69.0 2.6 %pad_maximum_fusion.ph = f32[2,64,2,48,128]{4,3,2,1,0:T(8,128)S(1)} fusion(f32[2,64,1,48,128]{4,3,2,1,0:T(8,128)} %get-tuple-element.24, f32[2,64,1,48,128]{4,3,2,1,0:T(8,128)S(1)} %get-tuple-element.23), kind=kLoop, calls=%fused_computation | loop fusion | flops 1572864 | bytes 12582912 | tf_op jit(solution)/shard_map/stack | solution.py:385
  71.7 0.0 copy-start.3
  71.7 0.0 copy-start.4
  71.7 1.5 collective-permute-start.11
  73.1 0.0 collective-permute-done.1
  73.1 0.2 collective-permute-done.2
  73.4 0.0 collective-permute-done.5
  73.4 1.8 %collective-permute-start.10 = (f32[12,96,128]{2,1,0:T(8,128)S(1)}, f32[12,96,128]{2,1,0:T(8,128)S(1)}, u32[]{:S(2)}, u32[]{:S(2)}) collective-permute-start(f32[12,96,128]{2,1,0:T(8,128)S(1)} %pad_maximum_fusion.3), channel_id=1, source_target_pairs={{0,1},{1,0},{2,3},{3,2},{4,5},{5,4},{6,7},{7,6},{8,9},{9,8},{10,11... | collective-permute-start | bytes 1769480 | tf_op jit(solution)/shard_map/ppermute | solution.py:371
  75.3 0.1 collective-permute-start.3
  75.3 2.7 %collective-permute-start.6 = (f32[6,96,128]{2,1,0:T(8,128)S(1)}, f32[6,96,128]{2,1,0:T(8,128)S(1)}, u32[]{:S(2)}, u32[]{:S(2)}) collective-permute-start(f32[6,96,128]{2,1,0:T(8,128)S(1)} %get-tuple-element.26), channel_id=1, source_target_pairs={{0,6},{1,7},{2,0},{3,1},{4,2},{5,3},{6,4},{7,5},{8,14},{9,15},{10,... | collective-permute-start | bytes 884744 | tf_op jit(solution)/shard_map/ppermute | solution.py:371
  78.1 0.0 collective-permute-done.11
  78.2 6.5 %shard_map.148.rest_0_ = f32[64,2,128,256]{3,2,1,0:T(8,128)} custom-call(s32[8]{0:T(128)S(1)} %pad_add_fusion.1.b0s, f32[8,96,128]{2,1,0:T(8,128)S(1)} %pad_maximum_fusion.5.w, f32[2,64,2,48,128]{4,3,2,1,0:T(8,128)S(1)} %pad_maximum_fusion.ph, f32[64,256,128]{2,1,0:T(8,128)S(1)} %bitcast.14, f32[64,128,128]{2,1,0:T(8,128)S(1)} %copy-done.1, ...), custom_call_target="tpu_custom_call" | custom-call | flops 2400000000 | bytes 5600000 | tf_op jit(solution)/shard_map/pallas_call | solution.py:268
  84.7 0.5 collective-permute-done.3
  85.2 0.0 collective-permute-done.6
  85.3 2.5 %collective-permute-start.7 = (f32[2,96,128]{2,1,0:T(8,128)S(1)}, f32[2,96,128]{2,1,0:T(8,128)S(1)}, u32[]{:S(2)}, u32[]{:S(2)}) collective-permute-start(f32[2,96,128]{2,1,0:T(8,128)S(1)} %get-tuple-element.22), channel_id=1, source_target_pairs={{0,6},{1,7},{2,0},{3,1},{4,2},{5,3},{6,4},{7,5},{8,14},{9,15},{10,... | collective-permute-start | bytes 294920 | tf_op jit(solution)/shard_map/ppermute | solution.py:371
  87.8 0.0 collective-permute-start.4
  87.9 1.4 collective-permute-start.9
  89.3 0.2 collective-permute-done.7
  89.5 3.0 %collective-permute-done.4 = f32[2,96,128]{2,1,0:T(8,128)S(1)} collective-permute-done((f32[2,96,128]{2,1,0:T(8,128)S(1)}, f32[2,96,128]{2,1,0:T(8,128)S(1)}, u32[]{:S(2)}, u32[]{:S(2)}) %collective-permute-start.4) | collective-permute-done | bytes 98336 | tf_op jit(solution)/shard_map/ppermute | solution.py:371
  92.5 2.6 %collective-permute-start.8 = (f32[4,96,128]{2,1,0:T(8,128)S(1)}, f32[4,96,128]{2,1,0:T(8,128)S(1)}, u32[]{:S(2)}, u32[]{:S(2)}) collective-permute-start(f32[4,96,128]{2,1,0:T(8,128)S(1)} %pad_maximum_fusion.8), channel_id=1, source_target_pairs={{0,1},{1,0},{2,3},{3,2},{4,5},{5,4},{6,7},{7,6},{8,9},{9,8},{10,11... | collective-permute-start | bytes 589832 | tf_op jit(solution)/shard_map/ppermute | solution.py:371
  95.1 0.0 collective-permute-done.10
  95.1 0.1 pad_maximum_fusion.1.w
  95.2 17.1 %shard_map.149.rest_0_ = f32[64,2,128,256]{3,2,1,0:T(8,128)} custom-call(s32[24]{0:T(128)S(1)} %concatenate.54.b0s, f32[24,96,128]{2,1,0:T(8,128)S(1)} %pad_maximum_fusion.1.w, f32[2,64,2,48,128]{4,3,2,1,0:T(8,128)S(1)} %pad_maximum_fusion.ph, f32[64,256,128]{2,1,0:T(8,128)S(1)} %bitcast.14, ...), custom_call_target="tpu_custom_call", output_to_operand_aliasing={{}: (7, {})} | custom-call | flops 7200000000 | bytes 16800000 | tf_op jit(solution)/shard_map/pallas_call | solution.py:268
  112.2 0.0 collective-permute-done.8
  112.3 0.0 collective-permute-done.9
  112.3 17.0 %shard_map.150.rest_0_ = f32[64,2,128,256]{3,2,1,0:T(8,128)} custom-call(s32[24]{0:T(128)S(1)} %concatenate.51.b0s, f32[24,96,128]{2,1,0:T(8,128)S(1)} %constant_dynamic-update-slice_fusion.w, f32[2,64,2,48,128]{4,3,2,1,0:T(8,128)S(1)} %pad_maximum_fusion.ph, f32[64,256,128]{2,1,0:T(8,128)S(1)} %bitcast.14, ...), custom_call_target="tpu_custom_call", output_to_operand_aliasing={{}: (7, {})} | custom-call | flops 7200000000 | bytes 16800000 | tf_op jit(solution)/shard_map/pallas_call | solution.py:268
  129.4 6.5 %shard_map.151.h = f32[64,2,128,256]{3,2,1,0:T(8,128)} custom-call(s32[8]{0:T(128)S(1)} %pad_add_fusion.b0s, f32[8,96,128]{2,1,0:T(8,128)S(1)} %pad_maximum_fusion.4.w, f32[2,64,2,48,128]{4,3,2,1,0:T(8,128)S(1)} %pad_maximum_fusion.ph, f32[64,256,128]{2,1,0:T(8,128)S(1)} %bitcast.14, f32[64,128,128]{2,1,0:T(8,128)S(1)} %copy-done.1, ...), custom_call_target="tpu_custom_call", output_to_operand_aliasing={{}: (7, {})} | custom-call | flops 2400000000 | bytes 5600000 | tf_op jit(solution)/shard_map/pallas_call | solution.py:268
  135.8 5.8 %copy-done = f32[64,2,128,256]{3,2,1,0:T(8,128)S(1)} copy-done((f32[64,2,128,256]{3,2,1,0:T(8,128)S(1)}, f32[64,2,128,256]{3,2,1,0:T(8,128)}, u32[]{:S(2)}) %copy-start) | copy-done | bytes 16777240
  141.6 10.4 %shard_map.152 = f32[32,256,128]{2,1,0:T(8,128)} custom-call(f32[64,2,128,256]{3,2,1,0:T(8,128)S(1)} %copy-done, f32[8,128]{1,0:T(8,128)S(1)} %copy-done.9), custom_call_target="tpu_custom_call" | custom-call | tf_op jit(solution)/shard_map/pallas_call | solution.py:346
  (41 shorter events, 0.4 us)
Async XLA Ops:
  0.0 36.4 %collective-permute-start = (f32[256,128]{1,0:T(8,128)}, f32[256,128]{1,0:T(8,128)S(1)}, u32[]{:S(2)}, u32[]{:S(2)}) collective-permute-start(f32[256,128]{1,0:T(8,128)} %bitcast.15), channel_id=1, source_target_pairs={{0,16},{16,32},{32,48},{48,64},{64,80},{80,96},{96,112},{1,17},{17... | collective-permute-start | bytes 393224 | tf_op jit(solution)/shard_map/ppermute | solution.py:394
  25.6 10.8 %copy-start.5 = (bf16[2,1024,512]{2,1,0:T(8,128)(2,1)S(1)}, bf16[2,1024,512]{2,1,0:T(8,128)(2,1)}, u32[]{:S(2)}) copy-start(bf16[2,1024,512]{2,1,0:T(8,128)(2,1)} %constant.262.clone.l1) | copy-start | bytes 6291460
  25.6 10.8 %copy-start.6 = (f32[2,512,128]{2,1,0:T(8,128)S(1)}, f32[2,512,128]{2,1,0:T(8,128)}, u32[]{:S(2)}) copy-start(f32[2,512,128]{2,1,0:T(8,128)} %constant.263.clone.tw1) | copy-start | bytes 1572868
  25.6 10.8 %copy-start.7 = (bf16[768,256]{1,0:T(8,128)(2,1)S(1)}, bf16[768,256]{1,0:T(8,128)(2,1)}, u32[]{:S(2)}) copy-start(bf16[768,256]{1,0:T(8,128)(2,1)} %constant.264.clone.m2) | copy-start | bytes 1179652
  25.6 10.8 %copy-start.8 = (f32[1,32768]{1,0:T(1,128)S(1)}, f32[1,32768]{1,0:T(1,128)}, u32[]{:S(2)}) copy-start(f32[1,32768]{1,0:T(1,128)} %param.15) | copy-start | bytes 393220
  36.4 3.4 %copy-start.2 = (f32[16,2,512,128]{3,2,1,0:T(8,128)S(1)}, f32[16,2,512,128]{3,2,1,0:T(8,128)}, u32[]{:S(2)}) copy-start(f32[16,2,512,128]{3,2,1,0:T(8,128)} %constant.265.clone.tj) | copy-start | bytes 25165828
  39.8 11.0 %copy-start.10 = (f32[2,64,128]{2,1,0:T(8,128)S(1)}, f32[2,64,128]{2,1,0:T(8,128)}, u32[]{:S(2)}) copy-start(f32[2,64,128]{2,1,0:T(8,128)} %get-tuple-element.27) | copy-start | bytes 196612
  39.8 11.0 %copy-start.11 = (f32[2,64,128]{2,1,0:T(8,128)S(1)}, f32[2,64,128]{2,1,0:T(8,128)}, u32[]{:S(2)}) copy-start(f32[2,64,128]{2,1,0:T(8,128)} %get-tuple-element.28) | copy-start | bytes 196612
  42.2 20.6 %all-to-all-start = ((f32[16,80,128]{2,1,0:T(8,128)}), f32[16,80,128]{2,1,0:T(8,128)}, u32[]{:S(2)}, u32[]{:S(2)}) async-start(f32[16,80,128]{2,1,0:T(8,128)} %shard_map.146), calls=%async_computation | async-start | bytes 1310720 | tf_op jit(solution)/shard_map/all_to_all | solution.py:402
  65.6 7.5 %collective-permute-start.1 = (f32[4,96,128]{2,1,0:T(8,128)}, f32[4,96,128]{2,1,0:T(8,128)S(1)}, u32[]{:S(2)}, u32[]{:S(2)}) collective-permute-start(f32[4,96,128]{2,1,0:T(8,128)} %get-tuple-element.11), channel_id=1, source_target_pairs={{0,8},{1,9},{2,10},{3,11},{4,12},{5,13},{6,14},{7,15},{8,0},{9,1},... | collective-permute-start | bytes 589832 | tf_op jit(solution)/shard_map/ppermute | solution.py:371
  66.3 7.0 %collective-permute-start.2 = (f32[4,96,128]{2,1,0:T(8,128)}, f32[4,96,128]{2,1,0:T(8,128)S(1)}, u32[]{:S(2)}, u32[]{:S(2)}) collective-permute-start(f32[4,96,128]{2,1,0:T(8,128)} %get-tuple-element.11), channel_id=1, source_target_pairs={{0,2},{1,3},{2,4},{3,5},{4,6},{5,7},{6,0},{7,1},{8,10},{9,11},{10,... | collective-permute-start | bytes 589832 | tf_op jit(solution)/shard_map/ppermute | solution.py:371
  66.3 7.0 %collective-permute-start.5 = (f32[4,96,128]{2,1,0:T(8,128)}, f32[4,96,128]{2,1,0:T(8,128)S(1)}, u32[]{:S(2)}, u32[]{:S(2)}) collective-permute-start(f32[4,96,128]{2,1,0:T(8,128)} %get-tuple-element.11), channel_id=1, source_target_pairs={{0,6},{1,7},{2,0},{3,1},{4,2},{5,3},{6,4},{7,5},{8,14},{9,15},{10,... | collective-permute-start | bytes 589832 | tf_op jit(solution)/shard_map/ppermute | solution.py:371
  69.0 9.1 %slice-start = ((s8[8388608]{0:T(1024)(128)(4,1)}), s8[4194304]{0:T(1024)(128)(4,1)S(1)}, s32[]{:S(2)}) async-start(s8[8388608]{0:T(1024)(128)(4,1)} %bitcast.13), calls=%async_computation.1 | async-start | bytes 8388608
  69.0 9.1 %copy-start.12 = (f32[4,96,128]{2,1,0:T(8,128)S(1)}, f32[4,96,128]{2,1,0:T(8,128)}, u32[]{:S(2)}) copy-start(f32[4,96,128]{2,1,0:T(8,128)} %get-tuple-element.11) | copy-start | bytes 589828
  69.0 9.1 %slice-start.1 = ((s8[8388608]{0:T(1024)(128)(4,1)}), s8[4194304]{0:T(1024)(128)(4,1)S(1)}, s32[]{:S(2)}) async-start(s8[8388608]{0:T(1024)(128)(4,1)} %bitcast.13), calls=%async_computation.2 | async-start | bytes 8388608
  69.0 9.1 %copy-start.1 = (f32[64,128,128]{2,1,0:T(8,128)S(1)}, f32[64,128,128]{2,1,0:T(8,128)}, u32[]{:S(2)}) copy-start(f32[64,128,128]{2,1,0:T(8,128)} %constant.269.clone.tw3) | copy-start | bytes 12582916
  71.7 6.5 %copy-start.3 = (bf16[256,768]{1,0:T(8,128)(2,1)S(1)}, bf16[256,768]{1,0:T(8,128)(2,1)}, u32[]{:S(2)}) copy-start(bf16[256,768]{1,0:T(8,128)(2,1)} %constant.267.clone.e2) | copy-start | bytes 1179652
  71.7 6.5 %copy-start.4 = (bf16[288,256]{1,0:T(8,128)(2,1)S(1)}, bf16[288,256]{1,0:T(8,128)(2,1)}, u32[]{:S(2)}) copy-start(bf16[288,256]{1,0:T(8,128)(2,1)} %constant.266.clone.e1) | copy-start | bytes 442372
  71.7 6.4 %collective-permute-start.11 = (f32[4,96,128]{2,1,0:T(8,128)}, f32[4,96,128]{2,1,0:T(8,128)S(1)}, u32[]{:S(2)}, u32[]{:S(2)}) collective-permute-start(f32[4,96,128]{2,1,0:T(8,128)} %get-tuple-element.11), channel_id=1, source_target_pairs={{0,1},{1,0},{2,3},{3,2},{4,5},{5,4},{6,7},{7,6},{8,9},{9,8},{10,11... | collective-permute-start | bytes 589832 | tf_op jit(solution)/shard_map/ppermute | solution.py:371
  73.4 21.7 %collective-permute-start.10 = (f32[12,96,128]{2,1,0:T(8,128)S(1)}, f32[12,96,128]{2,1,0:T(8,128)S(1)}, u32[]{:S(2)}, u32[]{:S(2)}) collective-permute-start(f32[12,96,128]{2,1,0:T(8,128)S(1)} %pad_maximum_fusion.3), channel_id=1, source_target_pairs={{0,1},{1,0},{2,3},{3,2},{4,5},{5,4},{6,7},{7,6},{8,9},{9,8},{10,11... | collective-permute-start | bytes 1769480 | tf_op jit(solution)/shard_map/ppermute | solution.py:371
  75.3 9.9 %collective-permute-start.3 = (f32[6,96,128]{2,1,0:T(8,128)S(1)}, f32[6,96,128]{2,1,0:T(8,128)S(1)}, u32[]{:S(2)}, u32[]{:S(2)}) collective-permute-start(f32[6,96,128]{2,1,0:T(8,128)S(1)} %get-tuple-element.25), channel_id=1, source_target_pairs={{0,2},{1,3},{2,4},{3,5},{4,6},{5,7},{6,0},{7,1},{8,10},{9,11},{10,... | collective-permute-start | bytes 884744 | tf_op jit(solution)/shard_map/ppermute | solution.py:371
  75.3 9.8 %collective-permute-start.6 = (f32[6,96,128]{2,1,0:T(8,128)S(1)}, f32[6,96,128]{2,1,0:T(8,128)S(1)}, u32[]{:S(2)}, u32[]{:S(2)}) collective-permute-start(f32[6,96,128]{2,1,0:T(8,128)S(1)} %get-tuple-element.26), channel_id=1, source_target_pairs={{0,6},{1,7},{2,0},{3,1},{4,2},{5,3},{6,4},{7,5},{8,14},{9,15},{10,... | collective-permute-start | bytes 884744 | tf_op jit(solution)/shard_map/ppermute | solution.py:371
  85.3 4.2 %collective-permute-start.7 = (f32[2,96,128]{2,1,0:T(8,128)S(1)}, f32[2,96,128]{2,1,0:T(8,128)S(1)}, u32[]{:S(2)}, u32[]{:S(2)}) collective-permute-start(f32[2,96,128]{2,1,0:T(8,128)S(1)} %get-tuple-element.22), channel_id=1, source_target_pairs={{0,6},{1,7},{2,0},{3,1},{4,2},{5,3},{6,4},{7,5},{8,14},{9,15},{10,... | collective-permute-start | bytes 294920 | tf_op jit(solution)/shard_map/ppermute | solution.py:371
  87.8 4.7 %collective-permute-start.4 = (f32[2,96,128]{2,1,0:T(8,128)S(1)}, f32[2,96,128]{2,1,0:T(8,128)S(1)}, u32[]{:S(2)}, u32[]{:S(2)}) collective-permute-start(f32[2,96,128]{2,1,0:T(8,128)S(1)} %get-tuple-element.19), channel_id=1, source_target_pairs={{0,2},{1,3},{2,4},{3,5},{4,6},{5,7},{6,0},{7,1},{8,10},{9,11},{10,... | collective-permute-start | bytes 294920 | tf_op jit(solution)/shard_map/ppermute | solution.py:371
  87.9 24.4 %collective-permute-start.9 = (f32[12,96,128]{2,1,0:T(8,128)S(1)}, f32[12,96,128]{2,1,0:T(8,128)S(1)}, u32[]{:S(2)}, u32[]{:S(2)}) collective-permute-start(f32[12,96,128]{2,1,0:T(8,128)S(1)} %pad_maximum_fusion.2), channel_id=1, source_target_pairs={{0,1},{1,0},{2,3},{3,2},{4,5},{5,4},{6,7},{7,6},{8,9},{9,8},{10,11... | collective-permute-start | bytes 1769480 | tf_op jit(solution)/shard_map/ppermute | solution.py:371
  92.5 19.7 %collective-permute-start.8 = (f32[4,96,128]{2,1,0:T(8,128)S(1)}, f32[4,96,128]{2,1,0:T(8,128)S(1)}, u32[]{:S(2)}, u32[]{:S(2)}) collective-permute-start(f32[4,96,128]{2,1,0:T(8,128)S(1)} %pad_maximum_fusion.8), channel_id=1, source_target_pairs={{0,1},{1,0},{2,3},{3,2},{4,5},{5,4},{6,7},{7,6},{8,9},{9,8},{10,11... | collective-permute-start | bytes 589832 | tf_op jit(solution)/shard_map/ppermute | solution.py:371
  129.4 6.5 %copy-start.9 = (f32[8,128]{1,0:T(8,128)S(1)}, f32[8,128]{1,0:T(8,128)}, u32[]{:S(2)}) copy-start(f32[8,128]{1,0:T(8,128)} %get-tuple-element.12.sig) | copy-start | bytes 12292
  135.8 5.8 %copy-start = (f32[64,2,128,256]{3,2,1,0:T(8,128)S(1)}, f32[64,2,128,256]{3,2,1,0:T(8,128)}, u32[]{:S(2)}) copy-start(f32[64,2,128,256]{3,2,1,0:T(8,128)} %shard_map.151.h) | copy-start | bytes 50331652

commit v2 on v1

--- a/solution.py
+++ b/solution.py
@@ -29,7 +29,17 @@
 
 
 LANE = np.arange(128)
-B1 = 64 * (LANE // 64) + 8 * (LANE % 8) + (LANE // 8) % 8
+
+
+def bits(x, *order):
+    out = 0 * x
+    for b in order:
+        out = 2 * out + (x >> b & 1)
+    return out
+
+
+B1 = bits(LANE, 2, 1, 6, 5, 4, 3, 0)
+SWAP = (0, 3, 4)
 
 
 @functools.lru_cache(None)
@@ -42,8 +52,7 @@
     t["l1"] = np.stack([hi, lo])
     c, s = unit(low[:, None] * LANE[None, :], 65536, -1)
     t["tw1"] = np.stack([c, s]).astype(np.float32)
-    h, al, bh = LANE // 64, (LANE // 8) % 8, LANE % 8
-    top = 16 * al + 8 * h + bh
+    top = 16 * bits(LANE, 4, 3, 0) + (B1 >> 3)
     c, s = unit(LANE[:, None] * top[None, :], 128, -1)
     hi, lo = halves(np.block([[c, s], [-s, c]]))
     t["m2"] = np.concatenate([hi, hi, lo])
@@ -81,24 +90,39 @@
     return jnp.dot(a, b, preferred_element_type=F32)
 
 
-def psd_kernel(me, bins, vals, amp, g_out, sig_out):
+def psd_kernel(me, bins, vals, amp, out, g):
+    width = 512
+
     def tile(i, total):
-        at = pl.multiple_of(i * 128, 128)
-        idx = bins[:, pl.ds(at, 128)]
-        hi, lo = idx >> 7, idx & 127
-        acc = jnp.ones((8, 128), F32)
+        at = pl.multiple_of(i * width, width)
+        idx = bins[:, pl.ds(at, width)]
+        parts = [idx[:, 128 * q : 128 * q + 128] for q in range(width // 128)]
+        hi, lo = [v >> 7 for v in parts], [v & 127 for v in parts]
+        acc = [jnp.ones((8, 128), F32) for _ in parts]
         for h in range(64):
             row = jnp.broadcast_to(vals[h : h + 1, :], (8, 128))
-            got = jnp.take_along_axis(row, lo, axis=1)
-            acc = jnp.where(hi == h, got, acc)
-        inv = 1.0 / acc
-        a = amp[0, :, pl.ds(at, 128)]
-        g = inv * a
-        g_out[:, pl.ds(at, 128)] = g * (1.0 / 1024.0)
-        return total + g * a
-
-    total = lax.fori_loop(0, 32, tile, jnp.zeros((8, 128), F32))
-    sig_out[...] = jnp.broadcast_to(jnp.sum(total, keepdims=True), (8, 128))
+            for q in range(len(parts)):
+                got = jnp.take_along_axis(row, lo[q], axis=1)
+                acc[q] = jnp.where(hi[q] == h, got, acc[q])
+        for q in range(len(parts)):
+            pos = pl.multiple_of(at + 128 * q, 128)
+            a = amp[0, :, pl.ds(pos, 128)]
+            f = a / acc[q]
+            total = total + f * a
+            row8 = pl.multiple_of(i * (width // 16) + 8 * q, 8)
+            g[pl.ds(row8, 8), :] = f * (1.0 / 1024.0)
+        return total
+
+    total = lax.fori_loop(0, 4096 // width, tile, jnp.zeros((8, 128), F32))
+    share = jnp.broadcast_to(jnp.sum(total, keepdims=True), (256, 128))
+    row = lax.broadcasted_iota(jnp.int32, (256, 128), 0) & 7
+    full = jnp.where(row >= 6, share, g[...])
+    for half in range(2):
+        tr = full[128 * half : 128 * half + 128].T
+        for low in range(2):
+            for d in range(16):
+                at = 8 * half + 4 * low
+                out[d, at : at + 4, :] = tr[64 * low + 4 * d : 64 * low + 4 * d + 4]
 
 
 def psd_call(me, bins, vals, amp):
@@ -112,15 +136,11 @@
                 pl.BlockSpec((64, 128), lambda i, m: (0, 0)),
                 pl.BlockSpec((1, 8, 4096), lambda i, m: (m[0], 0, 0)),
             ],
-            out_specs=[
-                pl.BlockSpec((8, 4096), lambda i, m: (0, 0)),
-                pl.BlockSpec((8, 128), lambda i, m: (0, 0)),
-            ],
+            out_specs=pl.BlockSpec((16, 16, 128), lambda i, m: (0, 0, 0)),
+            scratch_shapes=[pltpu.VMEM((256, 128), F32)],
         ),
-        out_shape=[
-            jax.ShapeDtypeStruct((8, 4096), F32),
-            jax.ShapeDtypeStruct((8, 128), F32),
-        ],
+        out_shape=jax.ShapeDtypeStruct((16, 16, 128), F32),
+        compiler_params=pltpu.CompilerParams(vmem_limit_bytes=50 << 20),
     )(me, bins, vals, amp)
 
 
@@ -166,7 +186,7 @@
             out_specs=pl.BlockSpec((16, 80, 128), lambda i, m: (0, 0, 0)),
         ),
         out_shape=jax.ShapeDtypeStruct((16, 80, 128), F32),
-        compiler_params=pltpu.CompilerParams(vmem_limit_bytes=40 << 20),
+        compiler_params=pltpu.CompilerParams(vmem_limit_bytes=50 << 20),
     )(me, tail, own, l1, tw1, m2, tj, extra)
 
 
@@ -175,16 +195,33 @@
     lane = lax.broadcasted_iota(jnp.int32, x.shape, 1)
     n = x.shape[0]
     for t in range(3):
-        d, w = 1 << t, 8 << t
-        rb, lb = (row >> t) & 1, (lane >> (3 + t)) & 1
+        d, w = 1 << t, 1 << SWAP[t]
+        rb, lb = (row >> t) & 1, (lane >> SWAP[t]) & 1
         up = pltpu.roll(pltpu.roll(x, d, 0), 128 - w, 1)
         dn = pltpu.roll(pltpu.roll(x, n - d, 0), w, 1)
         x = jnp.where(rb == lb, x, jnp.where(rb == 1, up, dn))
     return x
 
 
+def swap_low_bits(v):
+    lane = lax.broadcasted_iota(jnp.int32, v[0].shape, 1)
+    v = list(v)
+    for t in range(3):
+        w = 1 << t
+        clear = (lane >> t) & 1 == 0
+        for i in range(8):
+            if not i & w:
+                p, q = v[i], v[i | w]
+                v[i] = jnp.where(clear, p, pltpu.roll(q, w, 1))
+                v[i | w] = jnp.where(clear, pltpu.roll(p, 128 - w, 1), q)
+    return v
+
+
 def mix_kernel(p, w_out, sig_out):
-    lane = lax.broadcasted_iota(jnp.int32, (8, 128), 1)
+    g = []
+    for b in range(4):
+        rows = [64 + 80 * (i >> 2) + 4 * (i & 3) + b for i in range(8)]
+        g.append(swap_low_bits([p[pl.ds(r, 8, stride=160), :] for r in rows]))
     for ah in range(6):
         re = jnp.zeros((32, 128), F32)
         im = jnp.zeros((32, 128), F32)
@@ -196,19 +233,11 @@
             re = re + (pr * c - pi * s)
             im = im + (pr * s + pi * c)
         re, im = swap_groups(re), swap_groups(im)
-        for pair in range(2):
-            row = 64 + 2 * ah + pair
-            g0 = p[pl.ds(row, 8, stride=160), :]
-            g1 = p[pl.ds(row + 80, 8, stride=160), :]
-            g = (
-                jnp.where(lane < 64, g0, pltpu.roll(g1, 64, 1)),
-                jnp.where(lane < 64, pltpu.roll(g0, 64, 1), g1),
-            )
-            for odd in range(2):
-                b = 2 * pair + odd
-                w_out[b, 8 * ah : 8 * ah + 8, :] = re[8 * b : 8 * b + 8] * g[odd]
-                w_out[b, 48 + 8 * ah : 56 + 8 * ah, :] = im[8 * b : 8 * b + 8] * g[odd]
-    sig = jnp.sum(p[pl.ds(76, 16, stride=80), :], axis=0, keepdims=True)
+        for b in range(4):
+            at = slice(8 * b, 8 * b + 8)
+            w_out[b, 8 * ah : 8 * ah + 8, :] = re[at] * g[b][ah]
+            w_out[b, 48 + 8 * ah : 56 + 8 * ah, :] = im[at] * g[b][ah]
+    sig = jnp.sum(g[0][6], keepdims=True) * (1.0 / 64.0)
     sig_out[...] = jnp.broadcast_to(lax.rsqrt(sig), (8, 128))
 
 
@@ -222,62 +251,77 @@
     )(p)
 
 
-def inv_kernel(b0s, w, ph, tw, tw3, e1, e2, *rest):
+def inv_kernel(me, w, phc, phs, tw, tw3, e1, e2, *rest):
     h_out = rest[-1]
-    wr, wi = w[0, 0:48, :], w[0, 48:96, :]
-    zr, zi = [], []
-    for m in range(2):
-        c, s = ph[m, 0, 0], ph[m, 0, 1]
-        v = jnp.concatenate([wr * c - wi * s, wr * s + wi * c])
-        vh, vl = split2(v)
+    core = me[0] & 1
+    for u in range(8):
+        at = (u // 4 ^ core) * 4 + u % 4
+        wr, wi = w[0, at, 0:48, :], w[0, at, 48:96, :]
+        v = []
+        for m in range(2):
+            c, s = phc[m, u], phs[m, u]
+            v.append(jnp.concatenate([wr * c - wi * s, wr * s + wi * c]))
+        vh, vl = split2(jnp.concatenate(v, 1))
         g = lax.dot_general(
             jnp.concatenate([vh, vl, vh]),
             e1[...],
             (((0,), (0,)), ((), ())),
             preferred_element_type=F32,
         )
-        gr, gi = g[:, :128], g[:, 128:]
-        c, s = tw[0, :128], tw[0, 128:]
-        zr.append(gr * c - gi * s)
-        zi.append(gr * s + gi * c)
-    z = jnp.concatenate([jnp.concatenate(zr, 1), jnp.concatenate(zi, 1)], 0)
-    zh, zl = split2(z)
-    h = dot(e2[...], jnp.concatenate([zh, zl, zh], 0))
-    c, s = tw3[0, :, 0:1], tw3[0, :, 1:2]
-    hr, hi = h[:128], h[128:]
-    h_out[0, 0] = hr * c - hi * s
-    h_out[0, 1] = hr * s + hi * c
-
-
-def inv_call(b0s, w, ph, tw, tw3, e1, e2, prev):
-    count = w.shape[0]
+        c, s = tw[u, :128], tw[u, 128:]
+        zr, zi = [], []
+        for m in range(2):
+            gr, gi = g[128 * m : 128 * m + 128, :128], g[128 * m : 128 * m + 128, 128:]
+            zr.append(gr * c - gi * s)
+            zi.append(gr * s + gi * c)
+        z = jnp.concatenate([jnp.concatenate(zr, 1), jnp.concatenate(zi, 1)], 0)
+        zh, zl = split2(z)
+        h = dot(e2[...], jnp.concatenate([zh, zl, zh], 0))
+        c, s = tw3[u, :, 0:1], tw3[u, :, 1:2]
+        hr, hi = h[:128], h[128:]
+        h_out[u, 0] = hr * c - hi * s
+        h_out[u, 1] = hr * s + hi * c
+
+
+def inv_call(me, w, chips, ph, tw, tw3, e1, e2, prev):
+    count = len(chips)
+
+    def chip(i, m):
+        y, x = m[0] >> 3, (m[0] >> 1) & 3
+        dy, dx = chips[0]
+        for n in range(1, count):
+            dy = jnp.where(i == n, chips[n][0], dy)
+            dx = jnp.where(i == n, chips[n][1], dx)
+        return ((y + dy) & 1) * 4 + ((x + dx) & 3)
+
     in_specs = [
-        pl.BlockSpec((1, 96, 128), lambda i, b: (i, 0, 0)),
-        pl.BlockSpec((2, 1, 2, 48, 128), lambda i, b: (0, b[i], 0, 0, 0)),
-        pl.BlockSpec((1, 256, 128), lambda i, b: (b[i], 0, 0)),
-        pl.BlockSpec((1, 128, 128), lambda i, b: (b[i], 0, 0)),
-        pl.BlockSpec((288, 256), lambda i, b: (0, 0)),
-        pl.BlockSpec((256, 768), lambda i, b: (0, 0)),
+        pl.BlockSpec((1, 8, 96, 128), lambda i, m: (i, 0, 0, 0)),
+        pl.BlockSpec((2, 8, 48, 128), lambda i, m: (0, chip(i, m), 0, 0)),
+        pl.BlockSpec((2, 8, 48, 128), lambda i, m: (0, chip(i, m), 0, 0)),
+        pl.BlockSpec((8, 256, 128), lambda i, m: (chip(i, m), 0, 0)),
+        pl.BlockSpec((8, 128, 128), lambda i, m: (chip(i, m), 0, 0)),
+        pl.BlockSpec((288, 256), lambda i, m: (0, 0)),
+        pl.BlockSpec((256, 768), lambda i, m: (0, 0)),
     ]
-    args = [b0s, w, ph, tw, tw3, e1, e2]
+    args = [me, w, *ph, tw, tw3, e1, e2]
     alias = {}
     if prev is not None:
         in_specs.append(pl.BlockSpec(memory_space=pl.ANY))
         args.append(prev)
-        alias = {7: 0}
+        alias = {8: 0}
     return pl.pallas_call(
         inv_kernel,
         grid_spec=pltpu.PrefetchScalarGridSpec(
             num_scalar_prefetch=1,
             grid=(count,),
             in_specs=in_specs,
-            out_specs=pl.BlockSpec((1, 2, 128, 256), lambda i, b: (b[i], 0, 0, 0)),
+            out_specs=pl.BlockSpec((8, 2, 128, 256), lambda i, m: (chip(i, m), 0, 0, 0)),
         ),
         out_shape=jax.ShapeDtypeStruct((64, 2, 128, 256), F32),
         input_output_aliases=alias,
-        compiler_params=pltpu.CompilerParams(vmem_limit_bytes=32 << 20),
+        compiler_params=pltpu.CompilerParams(vmem_limit_bytes=50 << 20),
         cost_estimate=pl.CostEstimate(
-            flops=count * 300_000_000, bytes_accessed=count * 700_000, transcendentals=0
+            flops=count * 1_500_000_000, bytes_accessed=count * 6_000_000, transcendentals=0
         ),
     )(*args)
 
@@ -338,7 +382,8 @@
             ev, od = fft4(x[0::2]), fft4(x[1::2])
             for f in range(4):
                 v = sub(ev[f], cmul(od[f], f, 8))
-                mag = jnp.sqrt(v[0] * v[0] + v[1] * v[1]) * scale
+                power = v[0] * v[0] + v[1] * v[1]
+                mag = power * lax.rsqrt(jnp.maximum(power, 1e-37)) * scale
                 out[f2 + 8 * f, pl.ds(m, 8, stride=2), :] = mag
 
 
@@ -353,7 +398,7 @@
         out_specs=pl.BlockSpec((32, 16, 128), lambda i: (0, i, 0)),
         out_shape=jax.ShapeDtypeStruct((32, 256, 128), F32),
         scratch_shapes=[pltpu.VMEM((8, 8, 2, 8, 128), F32)],
-        compiler_params=pltpu.CompilerParams(vmem_limit_bytes=32 << 20),
+        compiler_params=pltpu.CompilerParams(vmem_limit_bytes=58 << 20),
     )(h, sig)
 
 
@@ -382,7 +427,7 @@
     p = a[None, None, :] * ((s + 2 * c * b0[None, :, None]) % 128) % 128
     ang = p.astype(F32) * (2 * math.pi / 128)
     qc, qs = jnp.cos(ang)[:, :, :, None], jnp.sin(ang)[:, :, :, None]
-    return jnp.stack([pc * qc - ps * qs, pc * qs + ps * qc], 2)
+    return pc * qc - ps * qs, pc * qs + ps * qc
 
 
 def local(strain, psd_bins, psd_values, chirp_slope, chirp_curve):
@@ -393,52 +438,33 @@
     count = lax.axis_size("tm")
     tail = lax.ppermute(own, "tm", [(i, i + 1) for i in range(count - 1)])
 
-    g, sig = psd_call(me, psd_bins, psd_values.reshape(64, 128), t["amp"])
-    g = g[:6].reshape(6, 8, 8, 16, 4).transpose(3, 0, 4, 2, 1).reshape(16, 12, 128)
-    sig = jnp.broadcast_to(sig[0, 0], (16, 4, 128))
-    extra = jnp.concatenate([g, sig], 1)
-
+    extra = psd_call(me, psd_bins, psd_values.reshape(64, 128), t["amp"])
     sent_out = fwd_call(me, tail, own, t["l1"], t["tw1"], t["m2"], t["tj"], extra)
+    sent_out, chirp_slope, chirp_curve = lax.optimization_barrier(
+        (sent_out, chirp_slope, chirp_curve)
+    )
     parts = lax.all_to_all(sent_out, "tmpl", split_axis=0, concat_axis=0, tiled=True)
+    ph = phases(chirp_slope, chirp_curve)
     w, scale = mix_call(parts.reshape(1280, 128))
 
-    ph = phases(chirp_slope, chirp_curve)
-    y, x, c = member // 8, member // 2 % 4, member % 2
-
-    def ids(dy, dx, dc, rows):
-        d = ((y + dy) % 2 * 4 + (x + dx) % 4) * 2 + (c + dc) % 2
-        return (4 * d + jnp.arange(rows.start, rows.stop)).astype(jnp.int32)
-
-    def work(blocks, prev):
-        mine = jnp.concatenate([v for v, *_ in blocks])
-        other = sent(mine, 0, 0, 1)
-        both = jnp.concatenate([mine, other])
-        order = [ids(dy, dx, 0, rows) for _, dy, dx, rows in blocks]
-        order += [ids(dy, dx, 1, rows) for _, dy, dx, rows in blocks]
-        return inv_call(
-            jnp.concatenate(order), both, ph, t["tw"], t["tw3"], t["e1"], t["e2"], prev
-        )
-
-    full, first, last = slice(0, 4), slice(0, 2), slice(2, 4)
+    def work(blocks, chips, prev):
+        mine = jnp.stack(blocks)
+        both = jnp.concatenate([mine, sent(mine, 0, 0, 1)], 1)
+        return inv_call(me, both, chips, ph, t["tw"], t["tw3"], t["e1"], t["e2"], prev)
+
     up = sent(w, 1, 0, 0)
     right = sent(w, 0, 1, 0)
     left = sent(w, 0, -1, 0)
-    h = work([(w, 0, 0, full)], None)
+    h = work([w], [(0, 0)], None)
     right2 = sent(jnp.concatenate([up, right[:2]]), 0, 1, 0)
     left2 = sent(jnp.concatenate([up, left[2:]]), 0, -1, 0)
-    h = work([(up, 1, 0, full), (right, 0, -1, full), (left, 0, 1, full)], h)
+    h = work([up, right, left], [(1, 0), (0, -1), (0, 1)], h)
+    right2, left2, h = lax.optimization_barrier((right2, left2, h))
     right3 = sent(right2[:2], 0, 1, 0)
     left3 = sent(left2[2:4], 0, -1, 0)
-    h = work(
-        [
-            (right2[:4], 1, -1, full),
-            (left2[:4], 1, 1, full),
-            (right2[4:], 0, -2, first),
-            (left2[4:], 0, 2, last),
-        ],
-        h,
-    )
-    h = work([(right3, 1, -2, first), (left3, 1, 2, last)], h)
+    far = jnp.concatenate([right2[4:], left2[4:]])
+    h = work([right2[:4], left2[:4], far], [(1, -1), (1, 1), (0, 2)], h)
+    h = work([jnp.concatenate([right3, left3])], [(1, 2)], h)
     out = out_call(h, scale)
     return out.reshape(4096, 2, 128).transpose(1, 0, 2).reshape(2, 4096 * 128)
 

time: 153 us -> 123 us (0.80)
  local copies, waits for them, and re-layouts: 25.2 us -> 7.12 us
  other arithmetic: 16.9 us -> 5.07 us
  waiting for transfers between devices: 12.7 us -> 23.6 us
  Pallas kernels: 69.2 us -> 61.5 us
  starting transfers between devices: 27.6 us -> 24.2 us
    pallas_call x4, Pallas kernels: 47 us -> 32.6 us  [inv_call(): pl.pallas_call(inv_kernel, grid_spec=pltpu.PrefetchScalarGridSpec(num_sca...]
    reshape x2 -> x0, local copies, waits for them, and re-layouts: 7.28 us -> none  [local(): g[:6].reshape(6, 8, 8, 16, 4).transpose(3, 0, 4, 2, 1).reshape(16, 12, 128)]
    ppermute x11, waiting for transfers between devices: 3.95 us -> 11.1 us  [sent(): return lax.ppermute(v, 'tmpl', route)]
    pallas_call x1, Pallas kernels: 10.4 us -> 15.7 us  [out_call(): pl.pallas_call(out_kernel, grid=(16,), in_specs=[pl.BlockSpec((64, 2, 8,...]
    transpose x1 -> x0, local copies, waits for them, and re-layouts: 5.16 us -> none  [local(): g[:6].reshape(6, 8, 8, 16, 4).transpose(3, 0, 4, 2, 1).reshape(16, 12, 128)]
    all_to_all x1, waiting for transfers between devices: 8.74 us -> 12.5 us  [local(): lax.all_to_all(sent_out, 'tmpl', split_axis=0, concat_axis=0, tiled=True)]
    ppermute x11, starting transfers between devices: 15.9 us -> 12.4 us  [sent(): return lax.ppermute(v, 'tmpl', route)]
    sub x1 -> x0, other arithmetic: 3.26 us -> none  [phases(): return jnp.stack([pc * qc - ps * qs, pc * qs + ps * qc], 2)]
  transfers between devices with their start and end apart: 13 -> 13, of which waited for: 5 -> 6; matrix products, arithmetic and copies ran while one was open for 22% -> 4% of each run, Pallas kernels for 20% -> 19%
where the time goes in v2:
time: 123 us; the launch traced here: 122 us
  Pallas kernels  61.5 us (50%)
  starting transfers between devices  24.2 us (20%)
  waiting for transfers between devices  23.6 us (19%)
  local copies, waits for them, and re-layouts  7.12 us (6%)
  other arithmetic  5.07 us (4%)
    pallas_call x4, Pallas kernels, inv_call(): pl.pallas_call(inv_kernel, grid_spec=pltpu.PrefetchScalarGridSpec(num_sca...  32.6 us
    pallas_call x1, Pallas kernels, out_call(): pl.pallas_call(out_kernel, grid=(16,), in_specs=[pl.BlockSpec((64, 2, 8,...  15.7 us
    all_to_all x1, waiting for transfers between devices, local(): lax.all_to_all(sent_out, 'tmpl', split_axis=0, concat_axis=0, tiled=True)  12.5 us
    ppermute x11, starting transfers between devices, sent(): return lax.ppermute(v, 'tmpl', route)  12.4 us
    ppermute x11, waiting for transfers between devices, sent(): return lax.ppermute(v, 'tmpl', route)  11.1 us
    all_to_all x1, starting transfers between devices, local(): lax.all_to_all(sent_out, 'tmpl', split_axis=0, concat_axis=0, tiled=True)  7.6 us
    unnamed x30, local copies, waits for them, and re-layouts  7.05 us
    pallas_call x1, Pallas kernels, psd_call(): pl.pallas_call(psd_kernel, grid_spec=pltpu.PrefetchScalarGridSpec(num_sca...  6.51 us
  transfers between devices with their start and end apart: 13, of which 6 were waited for; matrix products, arithmetic and copies ran while one was open for 4% of the time, Pallas kernels for 19%

profile of v2, /device:TPU:1, one launch (start us, length us, event | category | flops | bytes accessed | tf_op | source)
XLA Modules:
  0.0 121.8 jit_solution(4103018698609560844)
XLA Ops:
  0.0 0.0 copy-start.4
  0.0 4.2 %collective-permute-start = (f32[256,128]{1,0:T(8,128)}, f32[256,128]{1,0:T(8,128)S(1)}, u32[]{:S(2)}, u32[]{:S(2)}) collective-permute-start(f32[256,128]{1,0:T(8,128)} %bitcast.21), channel_id=1, source_target_pairs={{0,16},{16,32},{32,48},{48,64},{64,80},{80,96},{96,112},{1,17},{17... | collective-permute-start | bytes 393224 | tf_op jit(solution)/shard_map/ppermute | solution.py:439
  4.2 0.0 copy-start.5
  4.2 1.6 %copy-done.5 = f32[16,8,4096]{2,1,0:T(8,128)S(1)} copy-done((f32[16,8,4096]{2,1,0:T(8,128)S(1)}, f32[16,8,4096]{2,1,0:T(8,128)}, u32[]{:S(2)}) %copy-start.5) | copy-done | bytes 2097176
  5.8 0.0 copy-start.9
  5.8 0.9 copy-done.9
  6.7 0.0 copy-start.10
  6.7 0.8 copy-done.10
  7.4 6.5 %shard_map.145.extra = f32[16,16,128]{2,1,0:T(8,128)S(1)} custom-call(s32[1]{0:T(128)} %bitcast.me, s32[8,4096]{1,0:T(8,128)S(1)} %copy-done.9, f32[64,128]{1,0:T(8,128)S(1)} %bitcast.23, f32[16,8,4096]{2,1,0:T(8,128)S(1)} %copy-done.5), custom_call_target="tpu_custom_call" | custom-call | tf_op jit(solution)/shard_map/pallas_call | solution.py:129
  14.0 0.7 iota_add_fusion
  14.6 0.0 collective-permute-done.tail
  14.6 0.0 copy-done.4
  14.7 0.0 copy-start.6
  14.7 1.0 copy-done.6
  15.7 0.0 copy-start.7
  15.7 1.0 copy-done.7
  16.7 0.9 copy-done.8
  17.6 3.5 %shard_map.146 = f32[16,80,128]{2,1,0:T(8,128)} custom-call(s32[1]{0:T(128)} %bitcast.me, f32[256,128]{1,0:T(8,128)S(1)} %collective-permute-done.tail, f32[256,128]{1,0:T(8,128)S(1)} %bitcast.22, bf16[2,1024,512]{2,1,0:T(8,128)(2,1)S(1)} %copy-done.4, f32[2,512,128]{2,1,0:T(8,128)S(1)} %copy-done.6, bf16[768,256]{1,0:T(8,128)(2,1)S(1)} %copy-done.7, ...), custom_call_target="tpu_custom_call" | custom-call | tf_op jit(solution)/shard_map/pallas_call | solution.py:172
  21.1 7.6 %all-to-all-start = ((f32[16,80,128]{2,1,0:T(8,128)}), f32[16,80,128]{2,1,0:T(8,128)S(1)}, u32[]{:S(2)}, u32[]{:S(2)}) async-start(f32[16,80,128]{2,1,0:T(8,128)} %shard_map.146), calls=%async_computation | async-start | bytes 1310720 | tf_op jit(solution)/shard_map/all_to_all | solution.py:446
  28.7 0.0 copy-done.14
  28.7 0.0 copy-done.13
  28.7 0.1 and_select_fusion
  28.8 0.3 fusion.10
  29.2 12.5 %all-to-all-done = f32[16,80,128]{2,1,0:T(8,128)S(1)} async-done(((f32[16,80,128]{2,1,0:T(8,128)}), f32[16,80,128]{2,1,0:T(8,128)S(1)}, u32[]{:S(2)}, u32[]{:S(2)}) %all-to-all-start) | async-done | bytes 655392 | tf_op jit(solution)/shard_map/all_to_all | solution.py:446
  41.6 0.8 copy-done.11
  42.5 3.3 %shard_map.147 = (f32[4,96,128]{2,1,0:T(8,128)}, f32[8,128]{1,0:T(8,128)}) custom-call(f32[1280,128]{1,0:T(8,128)} %bitcast.24), custom_call_target="tpu_custom_call" | custom-call | tf_op jit(solution)/shard_map/pallas_call | solution.py:245
  45.7 1.0 collective-permute-start.4
  46.7 0.5 collective-permute-start.2
  47.2 0.7 collective-permute-start.1
  47.9 0.3 fusion.13
  48.2 1.5 %collective-permute-start.7 = (f32[1,4,96,128]{3,2,1,0:T(8,128)}, f32[1,4,96,128]{3,2,1,0:T(8,128)S(1)}, u32[]{:S(2)}, u32[]{:S(2)}) collective-permute-start(f32[1,4,96,128]{3,2,1,0:T(8,128)} %bitcast.31), channel_id=1, source_target_pairs={{0,1},{1,0},{2,3},{3,2},{4,5},{5,4},{6,7},{7,6},{8,9},{9,8},{10,11... | collective-permute-start | bytes 589832 | tf_op jit(solution)/shard_map/ppermute | solution.py:416
  49.7 1.8 %collective-permute-done.4 = f32[4,96,128]{2,1,0:T(8,128)S(1)} collective-permute-done((f32[4,96,128]{2,1,0:T(8,128)}, f32[4,96,128]{2,1,0:T(8,128)S(1)}, u32[]{:S(2)}, u32[]{:S(2)}) %collective-permute-start.4) | collective-permute-done | bytes 196640 | tf_op jit(solution)/shard_map/ppermute | solution.py:416
  51.5 3.0 %collective-permute-done.2 = f32[4,96,128]{2,1,0:T(8,128)S(1)} collective-permute-done((f32[4,96,128]{2,1,0:T(8,128)}, f32[4,96,128]{2,1,0:T(8,128)S(1)}, u32[]{:S(2)}, u32[]{:S(2)}) %collective-permute-start.2) | collective-permute-done | bytes 196640 | tf_op jit(solution)/shard_map/ppermute | solution.py:416
  54.5 0.0 collective-permute-done.1
  54.5 1.8 %collective-permute-start.6 = (f32[3,4,96,128]{3,2,1,0:T(8,128)S(1)}, f32[3,4,96,128]{3,2,1,0:T(8,128)S(1)}, u32[]{:S(2)}, u32[]{:S(2)}) collective-permute-start(f32[3,4,96,128]{3,2,1,0:T(8,128)S(1)} %pad_maximum_fusion.2), channel_id=1, source_target_pairs={{0,1},{1,0},{2,3},{3,2},{4,5},{5,4},{6,7},{7,6},{8,9},{9,8},{10,11... | collective-permute-start | bytes 1769480 | tf_op jit(solution)/shard_map/ppermute | solution.py:416
  56.3 3.2 %multiply_add_fusion = (f32[2,64,48,128]{3,2,1,0:T(8,128)}, f32[2,64,48,128]{3,2,1,0:T(8,128)S(1)}) fusion(f32[2,64,48]{2,1,0:T(8,128)S(1)} %get-tuple-element.32, f32[2,64,128]{2,1,0:T(8,128)S(1)} %get-tuple-element.30, f32[2,64,48]{2,1,0:T(8,128)S(1)} %get-tuple-element.31, f32[2,64,128]{2,1,0:T(8,128)S(1)} %get-tuple-element.29), kind=kLoop, calls=%fused_computation | loop fusion | flops 4718592 | bytes 6471680 | tf_op jit(solution)/shard_map/add | solution.py:430
  59.7 2.3 %collective-permute-start.5 = (f32[6,96,128]{2,1,0:T(8,128)S(1)}, f32[6,96,128]{2,1,0:T(8,128)S(1)}, u32[]{:S(2)}, u32[]{:S(2)}) collective-permute-start(f32[6,96,128]{2,1,0:T(8,128)S(1)} %get-tuple-element.27), channel_id=1, source_target_pairs={{0,6},{1,7},{2,0},{3,1},{4,2},{5,3},{6,4},{7,5},{8,14},{9,15},{10,... | collective-permute-start | bytes 884744 | tf_op jit(solution)/shard_map/ppermute | solution.py:416
  61.9 0.0 collective-permute-start.3
  62.0 0.0 collective-permute-done.7
  62.0 0.0 copy-done.12
  62.0 0.0 copy-done.2
  62.0 0.0 copy-done.3
  62.0 5.4 %shard_map.148.rest_0_ = f32[64,2,128,256]{3,2,1,0:T(8,128)} custom-call(s32[1]{0:T(128)} %bitcast.me, f32[1,8,96,128]{3,2,1,0:T(8,128)S(1)} %pad_maximum_fusion.4.w, f32[2,64,48,128]{3,2,1,0:T(8,128)S(1)} %get-tuple-element.26.phc, f32[2,64,48,128]{3,2,1,0:T(8,128)} %get-tuple-element.25.phs, f32[64,256,128]{2,1,0:T(8,128)} %constant.83.clone.tw, ...), custom_call_target="tpu_custom_call" | custom-call | flops 1500000000 | bytes 6000000 | tf_op jit(solution)/shard_map/pallas_call | solution.py:312
  67.4 0.0 copy-done
  67.4 0.0 collective-permute-done.6
  67.4 0.1 pad_maximum_fusion.w
  67.5 10.8 %shard_map.149.rest_0_ = f32[64,2,128,256]{3,2,1,0:T(8,128)} custom-call(s32[1]{0:T(128)} %bitcast.me, f32[3,8,96,128]{3,2,1,0:T(8,128)S(1)} %pad_maximum_fusion.w, f32[2,64,48,128]{3,2,1,0:T(8,128)} %copy-done, f32[2,64,48,128]{3,2,1,0:T(8,128)} %get-tuple-element.25.phs, f32[64,256,128]{2,1,0:T(8,128)} %constant.83.clone.tw, ...), custom_call_target="tpu_custom_call", output_to_operand_aliasing={{}: (8, {})} | custom-call | flops 4499999744 | bytes 18000000 | tf_op jit(solution)/shard_map/pallas_call | solution.py:312
  78.3 0.0 collective-permute-done.5
  78.3 0.0 collective-permute-done.3
  78.5 0.1 pad_maximum_fusion.3
  78.5 0.4 collective-permute-start.11
  78.9 3.0 %collective-permute-start.9 = (f32[2,96,128]{2,1,0:T(8,128)S(1)}, f32[2,96,128]{2,1,0:T(8,128)S(1)}, u32[]{:S(2)}, u32[]{:S(2)}) collective-permute-start(f32[2,96,128]{2,1,0:T(8,128)S(1)} %get-tuple-element.24), channel_id=1, source_target_pairs={{0,6},{1,7},{2,0},{3,1},{4,2},{5,3},{6,4},{7,5},{8,14},{9,15},{10,... | collective-permute-start | bytes 294920 | tf_op jit(solution)/shard_map/ppermute | solution.py:416
  82.0 0.0 collective-permute-start.8
  82.0 2.1 %collective-permute-done.9 = f32[2,96,128]{2,1,0:T(8,128)S(1)} collective-permute-done((f32[2,96,128]{2,1,0:T(8,128)S(1)}, f32[2,96,128]{2,1,0:T(8,128)S(1)}, u32[]{:S(2)}, u32[]{:S(2)}) %collective-permute-start.9) | collective-permute-done | bytes 98336 | tf_op jit(solution)/shard_map/ppermute | solution.py:416
  84.1 3.1 %collective-permute-done.8 = f32[2,96,128]{2,1,0:T(8,128)S(1)} collective-permute-done((f32[2,96,128]{2,1,0:T(8,128)S(1)}, f32[2,96,128]{2,1,0:T(8,128)S(1)}, u32[]{:S(2)}, u32[]{:S(2)}) %collective-permute-start.8) | collective-permute-done | bytes 98336 | tf_op jit(solution)/shard_map/ppermute | solution.py:416
  87.2 1.3 %collective-permute-start.10 = (f32[1,4,96,128]{3,2,1,0:T(8,128)S(1)}, f32[1,4,96,128]{3,2,1,0:T(8,128)S(1)}, u32[]{:S(2)}, u32[]{:S(2)}) collective-permute-start(f32[1,4,96,128]{3,2,1,0:T(8,128)S(1)} %maximum_bitcast_fusion), channel_id=1, source_target_pairs={{0,1},{1,0},{2,3},{3,2},{4,5},{5,4},{6,7},{7,6},{8,9},{9,8},{10,11... | collective-permute-start | bytes 589832 | tf_op jit(solution)/shard_map/ppermute | solution.py:416
  88.5 1.1 collective-permute-done.10
  89.6 0.0 collective-permute-done.11
  89.6 0.1 pad_maximum_fusion.1.w
  89.7 0.0 copy-start.1
  89.7 11.0 %shard_map.150.rest_0_ = f32[64,2,128,256]{3,2,1,0:T(8,128)} custom-call(s32[1]{0:T(128)} %bitcast.me, f32[3,8,96,128]{3,2,1,0:T(8,128)S(1)} %pad_maximum_fusion.1.w, f32[2,64,48,128]{3,2,1,0:T(8,128)} %copy-done, f32[2,64,48,128]{3,2,1,0:T(8,128)} %get-tuple-element.25.phs, f32[64,256,128]{2,1,0:T(8,128)} %constant.83.clone.tw, ...), custom_call_target="tpu_custom_call", output_to_operand_aliasing={{}: (8, {})} | custom-call | flops 4499999744 | bytes 18000000 | tf_op jit(solution)/shard_map/pallas_call | solution.py:312
  100.7 0.0 copy-done.1
  100.7 5.4 %shard_map.151.h = f32[64,2,128,256]{3,2,1,0:T(8,128)} custom-call(s32[1]{0:T(128)} %bitcast.me, f32[1,8,96,128]{3,2,1,0:T(8,128)S(1)} %pad_maximum_fusion.5.w, f32[2,64,48,128]{3,2,1,0:T(8,128)S(1)} %copy-done.1, f32[2,64,48,128]{3,2,1,0:T(8,128)} %get-tuple-element.25.phs, f32[64,256,128]{2,1,0:T(8,128)} %constant.83.clone.tw, ...), custom_call_target="tpu_custom_call", output_to_operand_aliasing={{}: (8, {})} | custom-call | flops 1500000000 | bytes 6000000 | tf_op jit(solution)/shard_map/pallas_call | solution.py:312
  106.1 15.7 %shard_map.152 = f32[32,256,128]{2,1,0:T(8,128)} custom-call(f32[64,2,128,256]{3,2,1,0:T(8,128)} %shard_map.151.h, f32[8,128]{1,0:T(8,128)} %get-tuple-element.20.sig), custom_call_target="tpu_custom_call" | custom-call | tf_op jit(solution)/shard_map/pallas_call | solution.py:391
  (20 shorter events, 0.3 us)
Async XLA Ops:
  0.0 14.6 %copy-start.4 = (bf16[2,1024,512]{2,1,0:T(8,128)(2,1)S(1)}, bf16[2,1024,512]{2,1,0:T(8,128)(2,1)}, u32[]{:S(2)}) copy-start(bf16[2,1024,512]{2,1,0:T(8,128)(2,1)} %constant.77.clone.l1) | copy-start | bytes 6291460
  0.0 14.6 %collective-permute-start = (f32[256,128]{1,0:T(8,128)}, f32[256,128]{1,0:T(8,128)S(1)}, u32[]{:S(2)}, u32[]{:S(2)}) collective-permute-start(f32[256,128]{1,0:T(8,128)} %bitcast.21), channel_id=1, source_target_pairs={{0,16},{16,32},{32,48},{48,64},{64,80},{80,96},{96,112},{1,17},{17... | collective-permute-start | bytes 393224 | tf_op jit(solution)/shard_map/ppermute | solution.py:439
  4.2 1.6 %copy-start.5 = (f32[16,8,4096]{2,1,0:T(8,128)S(1)}, f32[16,8,4096]{2,1,0:T(8,128)}, u32[]{:S(2)}) copy-start(f32[16,8,4096]{2,1,0:T(8,128)} %constant.85.clone.amp) | copy-start | bytes 6291460
  5.8 0.9 copy-start.9
  6.7 0.8 copy-start.10
  14.7 1.0 copy-start.6
  15.7 1.0 copy-start.7
  16.7 0.9 copy-start.8
  17.6 11.1 %copy-start.14 = (s32[2]{0:T(128)S(1)}, s32[2]{0:T(128)}, u32[]{:S(2)}) copy-start(s32[2]{0:T(128)} %param.19) | copy-start | bytes 28
  17.6 11.1 %copy-start.13 = (s32[2]{0:T(128)S(1)}, s32[2]{0:T(128)}, u32[]{:S(2)}) copy-start(s32[2]{0:T(128)} %param.18) | copy-start | bytes 28
  21.1 20.5 %all-to-all-start = ((f32[16,80,128]{2,1,0:T(8,128)}), f32[16,80,128]{2,1,0:T(8,128)S(1)}, u32[]{:S(2)}, u32[]{:S(2)}) async-start(f32[16,80,128]{2,1,0:T(8,128)} %shard_map.146), calls=%async_computation | async-start | bytes 1310720 | tf_op jit(solution)/shard_map/all_to_all | solution.py:446
  41.6 0.8 copy-start.11
  45.7 5.8 %collective-permute-start.4 = (f32[4,96,128]{2,1,0:T(8,128)}, f32[4,96,128]{2,1,0:T(8,128)S(1)}, u32[]{:S(2)}, u32[]{:S(2)}) collective-permute-start(f32[4,96,128]{2,1,0:T(8,128)} %get-tuple-element.14), channel_id=1, source_target_pairs={{0,6},{1,7},{2,0},{3,1},{4,2},{5,3},{6,4},{7,5},{8,14},{9,15},{10,... | collective-permute-start | bytes 589832 | tf_op jit(solution)/shard_map/ppermute | solution.py:416
  46.7 7.7 %collective-permute-start.2 = (f32[4,96,128]{2,1,0:T(8,128)}, f32[4,96,128]{2,1,0:T(8,128)S(1)}, u32[]{:S(2)}, u32[]{:S(2)}) collective-permute-start(f32[4,96,128]{2,1,0:T(8,128)} %get-tuple-element.14), channel_id=1, source_target_pairs={{0,2},{1,3},{2,4},{3,5},{4,6},{5,7},{6,0},{7,1},{8,10},{9,11},{10,... | collective-permute-start | bytes 589832 | tf_op jit(solution)/shard_map/ppermute | solution.py:416
  47.2 7.3 %collective-permute-start.1 = (f32[4,96,128]{2,1,0:T(8,128)}, f32[4,96,128]{2,1,0:T(8,128)S(1)}, u32[]{:S(2)}, u32[]{:S(2)}) collective-permute-start(f32[4,96,128]{2,1,0:T(8,128)} %get-tuple-element.14), channel_id=1, source_target_pairs={{0,8},{1,9},{2,10},{3,11},{4,12},{5,13},{6,14},{7,15},{8,0},{9,1},... | collective-permute-start | bytes 589832 | tf_op jit(solution)/shard_map/ppermute | solution.py:416
  48.2 13.7 %collective-permute-start.7 = (f32[1,4,96,128]{3,2,1,0:T(8,128)}, f32[1,4,96,128]{3,2,1,0:T(8,128)S(1)}, u32[]{:S(2)}, u32[]{:S(2)}) collective-permute-start(f32[1,4,96,128]{3,2,1,0:T(8,128)} %bitcast.31), channel_id=1, source_target_pairs={{0,1},{1,0},{2,3},{3,2},{4,5},{5,4},{6,7},{7,6},{8,9},{9,8},{10,11... | collective-permute-start | bytes 589832 | tf_op jit(solution)/shard_map/ppermute | solution.py:416
  54.5 12.9 %collective-permute-start.6 = (f32[3,4,96,128]{3,2,1,0:T(8,128)S(1)}, f32[3,4,96,128]{3,2,1,0:T(8,128)S(1)}, u32[]{:S(2)}, u32[]{:S(2)}) collective-permute-start(f32[3,4,96,128]{3,2,1,0:T(8,128)S(1)} %pad_maximum_fusion.2), channel_id=1, source_target_pairs={{0,1},{1,0},{2,3},{3,2},{4,5},{5,4},{6,7},{7,6},{8,9},{9,8},{10,11... | collective-permute-start | bytes 1769480 | tf_op jit(solution)/shard_map/ppermute | solution.py:416
  56.3 5.6 %copy-start.12 = (f32[4,96,128]{2,1,0:T(8,128)S(1)}, f32[4,96,128]{2,1,0:T(8,128)}, u32[]{:S(2)}) copy-start(f32[4,96,128]{2,1,0:T(8,128)} %get-tuple-element.14) | copy-start | bytes 589828
  56.3 5.7 %copy-start.2 = (bf16[256,768]{1,0:T(8,128)(2,1)S(1)}, bf16[256,768]{1,0:T(8,128)(2,1)}, u32[]{:S(2)}) copy-start(bf16[256,768]{1,0:T(8,128)(2,1)} %constant.82.clone.e2) | copy-start | bytes 1179652
  56.3 5.7 %copy-start.3 = (bf16[288,256]{1,0:T(8,128)(2,1)S(1)}, bf16[288,256]{1,0:T(8,128)(2,1)}, u32[]{:S(2)}) copy-start(bf16[288,256]{1,0:T(8,128)(2,1)} %constant.81.clone.e1) | copy-start | bytes 442372
  59.6 7.9 %copy-start = (f32[2,64,48,128]{3,2,1,0:T(8,128)}, f32[2,64,48,128]{3,2,1,0:T(8,128)S(1)}, u32[]{:S(2)}) copy-start(f32[2,64,48,128]{3,2,1,0:T(8,128)S(1)} %get-tuple-element.26.phc) | copy-start | bytes 9437188
  59.7 18.7 %collective-permute-start.5 = (f32[6,96,128]{2,1,0:T(8,128)S(1)}, f32[6,96,128]{2,1,0:T(8,128)S(1)}, u32[]{:S(2)}, u32[]{:S(2)}) collective-permute-start(f32[6,96,128]{2,1,0:T(8,128)S(1)} %get-tuple-element.27), channel_id=1, source_target_pairs={{0,6},{1,7},{2,0},{3,1},{4,2},{5,3},{6,4},{7,5},{8,14},{9,15},{10,... | collective-permute-start | bytes 884744 | tf_op jit(solution)/shard_map/ppermute | solution.py:416
  61.9 16.4 %collective-permute-start.3 = (f32[6,96,128]{2,1,0:T(8,128)S(1)}, f32[6,96,128]{2,1,0:T(8,128)S(1)}, u32[]{:S(2)}, u32[]{:S(2)}) collective-permute-start(f32[6,96,128]{2,1,0:T(8,128)S(1)} %get-tuple-element.28), channel_id=1, source_target_pairs={{0,2},{1,3},{2,4},{3,5},{4,6},{5,7},{6,0},{7,1},{8,10},{9,11},{10,... | collective-permute-start | bytes 884744 | tf_op jit(solution)/shard_map/ppermute | solution.py:416
  78.5 11.1 %collective-permute-start.11 = (f32[3,4,96,128]{3,2,1,0:T(8,128)S(1)}, f32[3,4,96,128]{3,2,1,0:T(8,128)S(1)}, u32[]{:S(2)}, u32[]{:S(2)}) collective-permute-start(f32[3,4,96,128]{3,2,1,0:T(8,128)S(1)} %pad_maximum_fusion.3), channel_id=1, source_target_pairs={{0,1},{1,0},{2,3},{3,2},{4,5},{5,4},{6,7},{7,6},{8,9},{9,8},{10,11... | collective-permute-start | bytes 1769480 | tf_op jit(solution)/shard_map/ppermute | solution.py:416
  78.9 5.2 %collective-permute-start.9 = (f32[2,96,128]{2,1,0:T(8,128)S(1)}, f32[2,96,128]{2,1,0:T(8,128)S(1)}, u32[]{:S(2)}, u32[]{:S(2)}) collective-permute-start(f32[2,96,128]{2,1,0:T(8,128)S(1)} %get-tuple-element.24), channel_id=1, source_target_pairs={{0,6},{1,7},{2,0},{3,1},{4,2},{5,3},{6,4},{7,5},{8,14},{9,15},{10,... | collective-permute-start | bytes 294920 | tf_op jit(solution)/shard_map/ppermute | solution.py:416
  82.0 5.2 %collective-permute-start.8 = (f32[2,96,128]{2,1,0:T(8,128)S(1)}, f32[2,96,128]{2,1,0:T(8,128)S(1)}, u32[]{:S(2)}, u32[]{:S(2)}) collective-permute-start(f32[2,96,128]{2,1,0:T(8,128)S(1)} %get-tuple-element.22), channel_id=1, source_target_pairs={{0,2},{1,3},{2,4},{3,5},{4,6},{5,7},{6,0},{7,1},{8,10},{9,11},{10,... | collective-permute-start | bytes 294920 | tf_op jit(solution)/shard_map/ppermute | solution.py:416
  87.2 2.3 %collective-permute-start.10 = (f32[1,4,96,128]{3,2,1,0:T(8,128)S(1)}, f32[1,4,96,128]{3,2,1,0:T(8,128)S(1)}, u32[]{:S(2)}, u32[]{:S(2)}) collective-permute-start(f32[1,4,96,128]{3,2,1,0:T(8,128)S(1)} %maximum_bitcast_fusion), channel_id=1, source_target_pairs={{0,1},{1,0},{2,3},{3,2},{4,5},{5,4},{6,7},{7,6},{8,9},{9,8},{10,11... | collective-permute-start | bytes 589832 | tf_op jit(solution)/shard_map/ppermute | solution.py:416
  89.7 11.0 %copy-start.1 = (f32[2,64,48,128]{3,2,1,0:T(8,128)S(1)}, f32[2,64,48,128]{3,2,1,0:T(8,128)}, u32[]{:S(2)}) copy-start(f32[2,64,48,128]{3,2,1,0:T(8,128)} %copy-done) | copy-start | bytes 9437188

commit v3 on v2

--- a/solution.py
+++ b/solution.py
@@ -14,6 +14,8 @@
 K_LOW = N // 200
 BF = jnp.bfloat16
 F32 = jnp.float32
+INV_VMEM = 24 << 20
+OUT_VMEM = 24 << 20
 
 
 def halves(x):
@@ -66,12 +68,14 @@
     c, s = unit(LANE[:, None] * B1[None, :], 128, 1)
     hi, lo = halves(np.block([[c, -s], [s, c]]))
     t["e2"] = np.concatenate([hi, hi, lo], 1)
-    b = 64 * B1[None, :] + np.arange(64)[:, None]
-    c, s = unit(b[:, :, None] * LANE[None, None, :], N, 1)
-    t["tw"] = np.concatenate([c, s], 1).astype(np.float32)
+    c, s = unit(64 * B1[:, None] * LANE[None, :], N, 1)
+    t["tw"] = np.stack([c, s]).astype(np.float32)
+    c, s = unit(np.arange(64)[:, None] * LANE[None, :], N, 1)
+    t["twb"] = np.stack([c, s], 1).astype(np.float32)
     c, s = unit(np.arange(64)[:, None] * LANE[None, :], 8192, 1)
-    t3 = np.zeros((64, 128, 128), np.float32)
-    t3[:, :, 0], t3[:, :, 1] = c, s
+    t3 = np.zeros((8, 128, 128), np.float32)
+    t3[:, :, 0:8] = c.reshape(8, 8, 128).transpose(0, 2, 1)
+    t3[:, :, 8:16] = s.reshape(8, 8, 128).transpose(0, 2, 1)
     t["tw3"] = t3
     k = np.arange(6)[:, None] * 65536 + np.arange(65536)[None, :]
     amp = np.where(k >= K_LOW, (np.maximum(k, 1) / K_LOW) ** (-7.0 / 6.0), 0.0)
@@ -251,7 +255,7 @@
     )(p)
 
 
-def inv_kernel(me, w, phc, phs, tw, tw3, e1, e2, *rest):
+def inv_kernel(me, w, phi, psi, tw, twb, tw3, e1, e2, *rest):
     h_out = rest[-1]
     core = me[0] & 1
     for u in range(8):
@@ -259,7 +263,10 @@
         wr, wi = w[0, at, 0:48, :], w[0, at, 48:96, :]
         v = []
         for m in range(2):
-            c, s = phc[m, u], phs[m, u]
+            pc, ps = phi[0, u, 2 * m : 2 * m + 1, :], phi[0, u, 2 * m + 1 : 2 * m + 2, :]
+            lane = 16 * m + u
+            qc, qs = psi[0, :, lane : lane + 1], psi[0, :, lane + 8 : lane + 9]
+            c, s = pc * qc - ps * qs, pc * qs + ps * qc
             v.append(jnp.concatenate([wr * c - wi * s, wr * s + wi * c]))
         vh, vl = split2(jnp.concatenate(v, 1))
         g = lax.dot_general(
@@ -268,7 +275,8 @@
             (((0,), (0,)), ((), ())),
             preferred_element_type=F32,
         )
-        c, s = tw[u, :128], tw[u, 128:]
+        fc, fs, bc, bs = tw[0], tw[1], twb[u, 0:1, :], twb[u, 1:2, :]
+        c, s = fc * bc - fs * bs, fc * bs + fs * bc
         zr, zi = [], []
         for m in range(2):
             gr, gi = g[128 * m : 128 * m + 128, :128], g[128 * m : 128 * m + 128, 128:]
@@ -277,13 +285,13 @@
         z = jnp.concatenate([jnp.concatenate(zr, 1), jnp.concatenate(zi, 1)], 0)
         zh, zl = split2(z)
         h = dot(e2[...], jnp.concatenate([zh, zl, zh], 0))
-        c, s = tw3[u, :, 0:1], tw3[u, :, 1:2]
+        c, s = tw3[0, :, u : u + 1], tw3[0, :, u + 8 : u + 9]
         hr, hi = h[:128], h[128:]
-        h_out[u, 0] = hr * c - hi * s
-        h_out[u, 1] = hr * s + hi * c
-
-
-def inv_call(me, w, chips, ph, tw, tw3, e1, e2, prev):
+        h_out[:, u, 0] = (hr * c - hi * s).reshape(16, 8, 256)
+        h_out[:, u, 1] = (hr * s + hi * c).reshape(16, 8, 256)
+
+
+def inv_call(me, w, chips, ph, t, prev):
     count = len(chips)
 
     def chip(i, m):
@@ -296,32 +304,35 @@
 
     in_specs = [
         pl.BlockSpec((1, 8, 96, 128), lambda i, m: (i, 0, 0, 0)),
-        pl.BlockSpec((2, 8, 48, 128), lambda i, m: (0, chip(i, m), 0, 0)),
-        pl.BlockSpec((2, 8, 48, 128), lambda i, m: (0, chip(i, m), 0, 0)),
-        pl.BlockSpec((8, 256, 128), lambda i, m: (chip(i, m), 0, 0)),
-        pl.BlockSpec((8, 128, 128), lambda i, m: (chip(i, m), 0, 0)),
+        pl.BlockSpec((1, 8, 4, 128), lambda i, m: (chip(i, m), 0, 0, 0)),
+        pl.BlockSpec((1, 48, 128), lambda i, m: (chip(i, m), 0, 0)),
+        pl.BlockSpec((2, 128, 128), lambda i, m: (0, 0, 0)),
+        pl.BlockSpec((8, 2, 128), lambda i, m: (chip(i, m), 0, 0)),
+        pl.BlockSpec((1, 128, 128), lambda i, m: (chip(i, m), 0, 0)),
         pl.BlockSpec((288, 256), lambda i, m: (0, 0)),
         pl.BlockSpec((256, 768), lambda i, m: (0, 0)),
     ]
-    args = [me, w, *ph, tw, tw3, e1, e2]
+    args = [me, w, *ph, t["tw"], t["twb"], t["tw3"], t["e1"], t["e2"]]
     alias = {}
     if prev is not None:
         in_specs.append(pl.BlockSpec(memory_space=pl.ANY))
         args.append(prev)
-        alias = {8: 0}
+        alias = {9: 0}
     return pl.pallas_call(
         inv_kernel,
         grid_spec=pltpu.PrefetchScalarGridSpec(
             num_scalar_prefetch=1,
             grid=(count,),
             in_specs=in_specs,
-            out_specs=pl.BlockSpec((8, 2, 128, 256), lambda i, m: (chip(i, m), 0, 0, 0)),
+            out_specs=pl.BlockSpec(
+                (16, 8, 2, 8, 256), lambda i, m: (0, chip(i, m), 0, 0, 0)
+            ),
         ),
-        out_shape=jax.ShapeDtypeStruct((64, 2, 128, 256), F32),
+        out_shape=jax.ShapeDtypeStruct((16, 64, 2, 8, 256), F32),
         input_output_aliases=alias,
-        compiler_params=pltpu.CompilerParams(vmem_limit_bytes=50 << 20),
+        compiler_params=pltpu.CompilerParams(vmem_limit_bytes=INV_VMEM),
         cost_estimate=pl.CostEstimate(
-            flops=count * 1_500_000_000, bytes_accessed=count * 6_000_000, transcendentals=0
+            flops=count * 1_500_000_000, bytes_accessed=count * 3_000_000, transcendentals=0
         ),
     )(*args)
 
@@ -369,7 +380,7 @@
     for m in range(2):
         at = slice(128 * m, 128 * m + 128)
         for lo in range(8):
-            x = [(h[8 * hi + lo, 0, :, at], h[8 * hi + lo, 1, :, at]) for hi in range(8)]
+            x = [(h[0, 8 * hi + lo, 0, :, at], h[0, 8 * hi + lo, 1, :, at]) for hi in range(8)]
             ev, od = fft4(x[0::2]), fft4(x[1::2])
             for f in range(4):
                 o = cmul(od[f], f, 8)
@@ -392,13 +403,13 @@
         out_kernel,
         grid=(16,),
         in_specs=[
-            pl.BlockSpec((64, 2, 8, 256), lambda i: (0, 0, i, 0)),
+            pl.BlockSpec((1, 64, 2, 8, 256), lambda i: (i, 0, 0, 0, 0)),
             pl.BlockSpec((8, 128), lambda i: (0, 0)),
         ],
         out_specs=pl.BlockSpec((32, 16, 128), lambda i: (0, i, 0)),
         out_shape=jax.ShapeDtypeStruct((32, 256, 128), F32),
         scratch_shapes=[pltpu.VMEM((8, 8, 2, 8, 128), F32)],
-        compiler_params=pltpu.CompilerParams(vmem_limit_bytes=58 << 20),
+        compiler_params=pltpu.CompilerParams(vmem_limit_bytes=OUT_VMEM),
     )(h, sig)
 
 
@@ -417,17 +428,21 @@
 
 
 def phases(chirp_slope, chirp_curve):
-    s, c = chirp_slope[:, None, None], chirp_curve[:, None, None]
-    b0 = jnp.arange(64, dtype=jnp.int32)
-    b = 64 * jnp.asarray(B1, jnp.int32)[None, :] + b0[:, None]
-    p = (s * b[None] + c * (b * b % N)[None]) % N
-    ang = p.astype(F32) * (2 * math.pi / N)
-    pc, ps = jnp.cos(ang)[:, :, None, :], jnp.sin(ang)[:, :, None, :]
-    a = jnp.arange(48, dtype=jnp.int32)
-    p = a[None, None, :] * ((s + 2 * c * b0[None, :, None]) % 128) % 128
-    ang = p.astype(F32) * (2 * math.pi / 128)
-    qc, qs = jnp.cos(ang)[:, :, :, None], jnp.sin(ang)[:, :, :, None]
-    return pc * qc - ps * qs, pc * qs + ps * qc
+    row = jnp.arange(4, dtype=jnp.int32)[None, :, None]
+    s = jnp.where(row < 2, chirp_slope[0], chirp_slope[1])
+    c = jnp.where(row < 2, chirp_curve[0], chirp_curve[1])
+    b0 = jnp.arange(64, dtype=jnp.int32)[:, None, None]
+    b = 64 * jnp.asarray(B1, jnp.int32)[None, None, :] + b0
+    p = (s * b + c * (b * b % N) - (N // 4) * (row % 2)) % N
+    phi = jnp.cos(p.astype(F32) * (2 * math.pi / N))
+    lane = jnp.arange(128, dtype=jnp.int32)[None, None, :]
+    s = jnp.where(lane < 16, chirp_slope[0], chirp_slope[1])
+    c = jnp.where(lane < 16, chirp_curve[0], chirp_curve[1])
+    b0 = 8 * jnp.arange(8, dtype=jnp.int32)[:, None, None] + lane % 8
+    a = jnp.arange(48, dtype=jnp.int32)[None, :, None]
+    p = (a * ((s + 2 * c * b0) % 128) - 32 * (lane // 8 % 2)) % 128
+    psi = jnp.cos(p.astype(F32) * (2 * math.pi / 128))
+    return phi.reshape(8, 8, 4, 128), psi
 
 
 def local(strain, psd_bins, psd_values, chirp_slope, chirp_curve):
@@ -445,12 +460,13 @@
     )
     parts = lax.all_to_all(sent_out, "tmpl", split_axis=0, concat_axis=0, tiled=True)
     ph = phases(chirp_slope, chirp_curve)
+    parts, *ph = lax.optimization_barrier((parts, *ph))
     w, scale = mix_call(parts.reshape(1280, 128))
 
     def work(blocks, chips, prev):
         mine = jnp.stack(blocks)
         both = jnp.concatenate([mine, sent(mine, 0, 0, 1)], 1)
-        return inv_call(me, both, chips, ph, t["tw"], t["tw3"], t["e1"], t["e2"], prev)
+        return inv_call(me, both, chips, ph, t, prev)
 
     up = sent(w, 1, 0, 0)
     right = sent(w, 0, 1, 0)

time: 123 us -> 100 us (0.81)
  Pallas kernels: 61.5 us -> 45.7 us
  waiting for transfers between devices: 23.6 us -> 16 us
  other arithmetic: 5.07 us -> 8.07 us
  starting transfers between devices: 24.2 us -> 22.6 us
    pallas_call x4, Pallas kernels: 32.6 us -> 23.1 us  [inv_call(): pl.pallas_call(inv_kernel, grid_spec=pltpu.PrefetchScalarGridSpec(num_sca...]
    all_to_all x1, waiting for transfers between devices: 12.5 us -> 5.27 us  [local(): lax.all_to_all(sent_out, 'tmpl', split_axis=0, concat_axis=0, tiled=True)]
    pallas_call x1, Pallas kernels: 15.7 us -> 9.33 us  [out_call(): pl.pallas_call(out_kernel, grid=(16,), in_specs=[pl.BlockSpec((1, 64, 2,...]
    select_n x1 -> x5, other arithmetic: 0.08 us -> 3.97 us  [the longest x1 1.35 us: phases(): s = jnp.where(lane < 16, chirp_slope[0], chirp_slope[1])]
    add x2, other arithmetic: 3.91 us -> 0.75 us  [phases(): b = 64 * jnp.asarray(B1, jnp.int32)[None, None, :] + b0]
    ppermute x11, starting transfers between devices: 12.4 us -> 10.9 us  [sent(): return lax.ppermute(v, 'tmpl', route)]
    unnamed x30 -> x34, local copies, waits for them, and re-layouts: 7.05 us -> 6.17 us
  transfers between devices with their start and end apart: 13 -> 13, of which waited for: 6 -> 5; matrix products, arithmetic and copies ran while one was open for 4% -> 9% of each run, Pallas kernels for 19% -> 18%
where the time goes in v3:
time: 100 us; the launch traced here: 99.7 us
  Pallas kernels  45.7 us (46%)
  starting transfers between devices  22.6 us (23%)
  waiting for transfers between devices  16 us (16%)
  other arithmetic  8.07 us (8%)
  local copies, waits for them, and re-layouts  6.9 us (7%)
    pallas_call x4, Pallas kernels, inv_call(): pl.pallas_call(inv_kernel, grid_spec=pltpu.PrefetchScalarGridSpec(num_sca...  23.1 us
    ppermute x11, starting transfers between devices, sent(): return lax.ppermute(v, 'tmpl', route)  10.9 us
    ppermute x11, waiting for transfers between devices, sent(): return lax.ppermute(v, 'tmpl', route)  10.7 us
    pallas_call x1, Pallas kernels, out_call(): pl.pallas_call(out_kernel, grid=(16,), in_specs=[pl.BlockSpec((1, 64, 2,...  9.33 us
    all_to_all x1, starting transfers between devices, local(): lax.all_to_all(sent_out, 'tmpl', split_axis=0, concat_axis=0, tiled=True)  7.74 us
    pallas_call x1, Pallas kernels, psd_call(): pl.pallas_call(psd_kernel, grid_spec=pltpu.PrefetchScalarGridSpec(num_sca...  6.51 us
    unnamed x34, local copies, waits for them, and re-layouts  6.17 us
    all_to_all x1, waiting for transfers between devices, local(): lax.all_to_all(sent_out, 'tmpl', split_axis=0, concat_axis=0, tiled=True)  5.27 us
  transfers between devices with their start and end apart: 13, of which 5 were waited for; matrix products, arithmetic and copies ran while one was open for 9% of the time, Pallas kernels for 18%

profile of v3, /device:TPU:1, one launch (start us, length us, event | category | flops | bytes accessed | tf_op | source)
XLA Modules:
  0.0 99.7 jit_solution(3983367590763572112)
XLA Ops:
  0.0 4.0 %collective-permute-start = (f32[256,128]{1,0:T(8,128)}, f32[256,128]{1,0:T(8,128)S(1)}, u32[]{:S(2)}, u32[]{:S(2)}) collective-permute-start(f32[256,128]{1,0:T(8,128)} %bitcast.25), channel_id=1, source_target_pairs={{0,16},{16,32},{32,48},{48,64},{64,80},{80,96},{96,112},{1,17},{17... | collective-permute-start | bytes 393224 | tf_op jit(solution)/shard_map/ppermute | solution.py:454
  4.1 0.7 broadcast_add_fusion
  4.8 0.0 copy-start.5
  4.8 1.6 %copy-done.5 = f32[16,8,4096]{2,1,0:T(8,128)S(1)} copy-done((f32[16,8,4096]{2,1,0:T(8,128)S(1)}, f32[16,8,4096]{2,1,0:T(8,128)}, u32[]{:S(2)}) %copy-start.5) | copy-done | bytes 2097176
  6.4 0.9 copy-done.10
  7.3 0.8 copy-done.11
  8.1 6.5 %shard_map.154.extra = f32[16,16,128]{2,1,0:T(8,128)S(1)} custom-call(s32[1]{0:T(128)} %bitcast.me, s32[8,4096]{1,0:T(8,128)S(1)} %copy-done.10, f32[64,128]{1,0:T(8,128)S(1)} %bitcast.27, f32[16,8,4096]{2,1,0:T(8,128)S(1)} %copy-done.5), custom_call_target="tpu_custom_call" | custom-call | tf_op jit(solution)/shard_map/pallas_call | solution.py:133
  14.6 0.0 collective-permute-done.tail
  14.6 0.0 copy-done.4
  14.6 0.0 copy-done.9
  14.7 0.0 copy-start.7
  14.7 1.0 %copy-done.7 = f32[2,512,128]{2,1,0:T(8,128)S(1)} copy-done((f32[2,512,128]{2,1,0:T(8,128)S(1)}, f32[2,512,128]{2,1,0:T(8,128)}, u32[]{:S(2)}) %copy-start.7) | copy-done | bytes 524312
  15.7 1.0 copy-done.8
  16.7 3.5 %shard_map.155 = f32[16,80,128]{2,1,0:T(8,128)} custom-call(s32[1]{0:T(128)} %bitcast.me, f32[256,128]{1,0:T(8,128)S(1)} %collective-permute-done.tail, f32[256,128]{1,0:T(8,128)S(1)} %bitcast.26, bf16[2,1024,512]{2,1,0:T(8,128)(2,1)S(1)} %copy-done.4, f32[2,512,128]{2,1,0:T(8,128)S(1)} %copy-done.7, bf16[768,256]{1,0:T(8,128)(2,1)S(1)} %copy-done.8, ...), custom_call_target="tpu_custom_call" | custom-call | tf_op jit(solution)/shard_map/pallas_call | solution.py:176
  20.2 7.7 %all-to-all-start = ((f32[16,80,128]{2,1,0:T(8,128)}), f32[16,80,128]{2,1,0:T(8,128)S(1)}, u32[]{:S(2)}, u32[]{:S(2)}) async-start(f32[16,80,128]{2,1,0:T(8,128)} %shard_map.155), calls=%async_computation | async-start | bytes 1310720 | tf_op jit(solution)/shard_map/all_to_all | solution.py:461
  27.9 0.0 copy-done.15
  27.9 0.0 copy-done.16
  27.9 0.7 fusion.16
  28.6 1.4 %compare_select_fusion.3 = s32[128]{0:T(128)S(1)} fusion(s32[]{:T(128)} %bitcast.4, s32[]{:T(128)} %bitcast.3), kind=kLoop, calls=%fused_computation.43 | loop fusion | flops 256 | bytes 520 | tf_op jit(solution)/shard_map/jit(_where)/select_n | solution.py:439
  29.9 1.2 %fusion.10 = s32[128]{0:T(128)S(1)} fusion(s32[]{:T(128)} %bitcast.6, s32[]{:T(128)} %bitcast.5), kind=kLoop, calls=%fused_computation.48 | loop fusion | flops 384 | bytes 520 | tf_op jit(solution)/shard_map/mul | solution.py:443
  31.1 0.1 add_select_fusion.3
  31.2 1.4 %compare_select_fusion.5 = s32[4]{0:T(128)S(1)} fusion(s32[]{:T(128)} %bitcast.4, s32[]{:T(128)} %bitcast.3), kind=kLoop, calls=%fused_computation.45 | loop fusion | flops 8 | bytes 24 | tf_op jit(solution)/shard_map/jit(_where)/select_n | solution.py:432
  32.6 1.2 %compare_select_fusion.4 = s32[4]{0:T(128)S(1)} fusion(s32[]{:T(128)} %bitcast.6, s32[]{:T(128)} %bitcast.5), kind=kLoop, calls=%fused_computation.44 | loop fusion | flops 8 | bytes 24 | tf_op jit(solution)/shard_map/jit(_where)/select_n | solution.py:433
  33.8 1.1 %fusion.7.phi = f32[8,8,4,128]{3,2,1,0:T(4,128)S(1)} fusion(s32[4]{0:T(128)S(1)} %fusion.11, s32[8,8,128]{2,1,0:T(8,128)S(1)} %get-tuple-element.34, s32[4]{0:T(128)S(1)} %compare_select_fusion.4, s32[8,8,128]{2,1,0:T(8,128)S(1)} %get-tuple-element.33, s32[4]{0:T(128)S(1)} %compare_select_fusion.5), kind=kLoop, calls=%fused_computation.25 | loop fusion | flops 557056 | bytes 196656 | tf_op jit(solution)/shard_map/cos | solution.py:437
  34.8 0.7 fusion.3.psi
  35.6 5.3 %all-to-all-done = f32[16,80,128]{2,1,0:T(8,128)S(1)} async-done(((f32[16,80,128]{2,1,0:T(8,128)}), f32[16,80,128]{2,1,0:T(8,128)S(1)}, u32[]{:S(2)}, u32[]{:S(2)}) %all-to-all-start) | async-done | bytes 655392 | tf_op jit(solution)/shard_map/all_to_all | solution.py:461
  40.8 0.8 copy-done.13
  41.7 3.3 %shard_map.156 = (f32[4,96,128]{2,1,0:T(8,128)}, f32[8,128]{1,0:T(8,128)}) custom-call(f32[1280,128]{1,0:T(8,128)} %bitcast.28), custom_call_target="tpu_custom_call" | custom-call | tf_op jit(solution)/shard_map/pallas_call | solution.py:249
  44.9 1.0 %collective-permute-start.4 = (f32[4,96,128]{2,1,0:T(8,128)}, f32[4,96,128]{2,1,0:T(8,128)S(1)}, u32[]{:S(2)}, u32[]{:S(2)}) collective-permute-start(f32[4,96,128]{2,1,0:T(8,128)} %get-tuple-element.20), channel_id=1, source_target_pairs={{0,6},{1,7},{2,0},{3,1},{4,2},{5,3},{6,4},{7,5},{8,14},{9,15},{10,... | collective-permute-start | bytes 589832 | tf_op jit(solution)/shard_map/ppermute | solution.py:427
  45.9 0.5 collective-permute-start.2
  46.4 0.7 collective-permute-start.1
  47.1 3.6 %collective-permute-done.4 = f32[4,96,128]{2,1,0:T(8,128)S(1)} collective-permute-done((f32[4,96,128]{2,1,0:T(8,128)}, f32[4,96,128]{2,1,0:T(8,128)S(1)}, u32[]{:S(2)}, u32[]{:S(2)}) %collective-permute-start.4) | collective-permute-done | bytes 196640 | tf_op jit(solution)/shard_map/ppermute | solution.py:427
  50.7 3.0 %collective-permute-done.2 = f32[4,96,128]{2,1,0:T(8,128)S(1)} collective-permute-done((f32[4,96,128]{2,1,0:T(8,128)}, f32[4,96,128]{2,1,0:T(8,128)S(1)}, u32[]{:S(2)}, u32[]{:S(2)}) %collective-permute-start.2) | collective-permute-done | bytes 196640 | tf_op jit(solution)/shard_map/ppermute | solution.py:427
  53.7 0.0 collective-permute-done.1
  53.7 0.0 copy-start
  53.7 0.0 copy-start.1
  53.7 0.0 copy-start.2
  53.8 0.0 copy-start.3
  53.8 0.0 copy-start.6
  53.8 1.8 %collective-permute-start.6 = (f32[3,4,96,128]{3,2,1,0:T(8,128)S(1)}, f32[3,4,96,128]{3,2,1,0:T(8,128)S(1)}, u32[]{:S(2)}, u32[]{:S(2)}) collective-permute-start(f32[3,4,96,128]{3,2,1,0:T(8,128)S(1)} %pad_maximum_fusion.2), channel_id=1, source_target_pairs={{0,1},{1,0},{2,3},{3,2},{4,5},{5,4},{6,7},{7,6},{8,9},{9,8},{10,11... | collective-permute-start | bytes 1769480 | tf_op jit(solution)/shard_map/ppermute | solution.py:427
  55.6 0.0 copy-done.14
  55.6 0.1 collective-permute-start.7
  55.8 2.3 %collective-permute-start.5 = (f32[6,96,128]{2,1,0:T(8,128)S(1)}, f32[6,96,128]{2,1,0:T(8,128)S(1)}, u32[]{:S(2)}, u32[]{:S(2)}) collective-permute-start(f32[6,96,128]{2,1,0:T(8,128)S(1)} %get-tuple-element.31), channel_id=1, source_target_pairs={{0,6},{1,7},{2,0},{3,1},{4,2},{5,3},{6,4},{7,5},{8,14},{9,15},{10,... | collective-permute-start | bytes 884744 | tf_op jit(solution)/shard_map/ppermute | solution.py:427
  58.1 0.0 collective-permute-start.3
  58.1 0.0 collective-permute-done.7
  58.1 0.0 copy-done
  58.2 2.8 %shard_map.157.rest_0_ = f32[16,64,2,8,256]{4,3,2,1,0:T(8,128)S(1)} custom-call(s32[1]{0:T(128)} %bitcast.me, f32[1,8,96,128]{3,2,1,0:T(8,128)S(1)} %pad_maximum_fusion.4.w, f32[8,8,4,128]{3,2,1,0:T(4,128)S(1)} %fusion.7.phi, f32[8,48,128]{2,1,0:T(8,128)S(1)} %fusion.3.psi, f32[2,128,128]{2,1,0:T(8,128)S(1)} %copy-done.3, f32[64,2,128]{2,1,0:T(2,128)S(1)} %copy-done.6, ...), custom_call_target="tpu_custom_call" | custom-call | flops 1500000000 | bytes 3000000 | tf_op jit(solution)/shard_map/pallas_call | solution.py:321
  60.9 0.0 collective-permute-done.6
  60.9 0.1 pad_maximum_fusion.w
  61.0 8.8 %shard_map.158.rest_0_ = f32[16,64,2,8,256]{4,3,2,1,0:T(8,128)S(1)} custom-call(s32[1]{0:T(128)} %bitcast.me, f32[3,8,96,128]{3,2,1,0:T(8,128)S(1)} %pad_maximum_fusion.w, f32[8,8,4,128]{3,2,1,0:T(4,128)S(1)} %fusion.7.phi, f32[8,48,128]{2,1,0:T(8,128)S(1)} %fusion.3.psi, f32[2,128,128]{2,1,0:T(8,128)S(1)} %copy-done.3, ...), custom_call_target="tpu_custom_call", output_to_operand_aliasing={{}: (9, {})} | custom-call | flops 4499999744 | bytes 9000000 | tf_op jit(solution)/shard_map/pallas_call | solution.py:321
  69.8 0.0 collective-permute-done.5
  69.8 0.0 collective-permute-done.3
  70.0 0.8 collective-permute-start.11
  70.8 0.0 collective-permute-start.8
  70.8 3.0 %collective-permute-start.9 = (f32[2,96,128]{2,1,0:T(8,128)S(1)}, f32[2,96,128]{2,1,0:T(8,128)S(1)}, u32[]{:S(2)}, u32[]{:S(2)}) collective-permute-start(f32[2,96,128]{2,1,0:T(8,128)S(1)} %get-tuple-element.30), channel_id=1, source_target_pairs={{0,6},{1,7},{2,0},{3,1},{4,2},{5,3},{6,4},{7,5},{8,14},{9,15},{10,... | collective-permute-start | bytes 294920 | tf_op jit(solution)/shard_map/ppermute | solution.py:427
  73.7 3.1 %collective-permute-done.8 = f32[2,96,128]{2,1,0:T(8,128)S(1)} collective-permute-done((f32[2,96,128]{2,1,0:T(8,128)S(1)}, f32[2,96,128]{2,1,0:T(8,128)S(1)}, u32[]{:S(2)}, u32[]{:S(2)}) %collective-permute-start.8) | collective-permute-done | bytes 98336 | tf_op jit(solution)/shard_map/ppermute | solution.py:427
  76.8 0.0 collective-permute-done.9
  76.8 0.7 collective-permute-start.10
  77.6 1.1 %collective-permute-done.10 = f32[1,4,96,128]{3,2,1,0:T(8,128)S(1)} collective-permute-done((f32[1,4,96,128]{3,2,1,0:T(8,128)S(1)}, f32[1,4,96,128]{3,2,1,0:T(8,128)S(1)}, u32[]{:S(2)}, u32[]{:S(2)}) %collective-permute-start.10) | collective-permute-done | bytes 196640 | tf_op jit(solution)/shard_map/ppermute | solution.py:427
  78.7 0.0 collective-permute-done.11
  78.7 0.1 pad_maximum_fusion.1.w
  78.8 8.8 %shard_map.159.rest_0_ = f32[16,64,2,8,256]{4,3,2,1,0:T(8,128)S(1)} custom-call(s32[1]{0:T(128)} %bitcast.me, f32[3,8,96,128]{3,2,1,0:T(8,128)S(1)} %pad_maximum_fusion.1.w, f32[8,8,4,128]{3,2,1,0:T(4,128)S(1)} %fusion.7.phi, f32[8,48,128]{2,1,0:T(8,128)S(1)} %fusion.3.psi, f32[2,128,128]{2,1,0:T(8,128)S(1)} %copy-done.3, ...), custom_call_target="tpu_custom_call", output_to_operand_aliasing={{}: (9, {})} | custom-call | flops 4499999744 | bytes 9000000 | tf_op jit(solution)/shard_map/pallas_call | solution.py:321
  87.6 2.8 %shard_map.160.h = f32[16,64,2,8,256]{4,3,2,1,0:T(8,128)S(1)} custom-call(s32[1]{0:T(128)} %bitcast.me, f32[1,8,96,128]{3,2,1,0:T(8,128)S(1)} %pad_maximum_fusion.5.w, f32[8,8,4,128]{3,2,1,0:T(4,128)S(1)} %fusion.7.phi, f32[8,48,128]{2,1,0:T(8,128)S(1)} %fusion.3.psi, f32[2,128,128]{2,1,0:T(8,128)S(1)} %copy-done.3, ...), custom_call_target="tpu_custom_call", output_to_operand_aliasing={{}: (9, {})} | custom-call | flops 1500000000 | bytes 3000000 | tf_op jit(solution)/shard_map/pallas_call | solution.py:321
  90.4 9.3 %shard_map.161 = f32[32,256,128]{2,1,0:T(8,128)} custom-call(f32[16,64,2,8,256]{4,3,2,1,0:T(8,128)S(1)} %shard_map.160.h, f32[8,128]{1,0:T(8,128)S(1)} %copy-done.12), custom_call_target="tpu_custom_call" | custom-call | tf_op jit(solution)/shard_map/pallas_call | solution.py:402
  (33 shorter events, 0.3 us)
Async XLA Ops:
  0.0 14.6 %collective-permute-start = (f32[256,128]{1,0:T(8,128)}, f32[256,128]{1,0:T(8,128)S(1)}, u32[]{:S(2)}, u32[]{:S(2)}) collective-permute-start(f32[256,128]{1,0:T(8,128)} %bitcast.25), channel_id=1, source_target_pairs={{0,16},{16,32},{32,48},{48,64},{64,80},{80,96},{96,112},{1,17},{17... | collective-permute-start | bytes 393224 | tf_op jit(solution)/shard_map/ppermute | solution.py:454
  4.8 1.6 %copy-start.5 = (f32[16,8,4096]{2,1,0:T(8,128)S(1)}, f32[16,8,4096]{2,1,0:T(8,128)}, u32[]{:S(2)}) copy-start(f32[16,8,4096]{2,1,0:T(8,128)} %constant.146.clone.amp) | copy-start | bytes 6291460
  6.4 0.9 copy-start.10
  7.3 0.8 copy-start.11
  8.1 6.5 %copy-start.4 = (bf16[2,1024,512]{2,1,0:T(8,128)(2,1)S(1)}, bf16[2,1024,512]{2,1,0:T(8,128)(2,1)}, u32[]{:S(2)}) copy-start(bf16[2,1024,512]{2,1,0:T(8,128)(2,1)} %constant.137.clone.l1) | copy-start | bytes 6291460
  8.1 6.6 %copy-start.9 = (f32[1,32768]{1,0:T(1,128)S(1)}, f32[1,32768]{1,0:T(1,128)}, u32[]{:S(2)}) copy-start(f32[1,32768]{1,0:T(1,128)} %param.16) | copy-start | bytes 393220
  14.7 1.0 %copy-start.7 = (f32[2,512,128]{2,1,0:T(8,128)S(1)}, f32[2,512,128]{2,1,0:T(8,128)}, u32[]{:S(2)}) copy-start(f32[2,512,128]{2,1,0:T(8,128)} %constant.138.clone.tw1) | copy-start | bytes 1572868
  15.7 1.0 copy-start.8
  20.2 7.7 %copy-start.15 = (s32[2]{0:T(128)S(1)}, s32[2]{0:T(128)}, u32[]{:S(2)}) copy-start(s32[2]{0:T(128)} %param.19) | copy-start | bytes 28
  20.2 7.7 %copy-start.16 = (s32[2]{0:T(128)S(1)}, s32[2]{0:T(128)}, u32[]{:S(2)}) copy-start(s32[2]{0:T(128)} %param.20) | copy-start | bytes 28
  20.2 20.7 %all-to-all-start = ((f32[16,80,128]{2,1,0:T(8,128)}), f32[16,80,128]{2,1,0:T(8,128)S(1)}, u32[]{:S(2)}, u32[]{:S(2)}) async-start(f32[16,80,128]{2,1,0:T(8,128)} %shard_map.155), calls=%async_computation | async-start | bytes 1310720 | tf_op jit(solution)/shard_map/all_to_all | solution.py:461
  40.8 0.8 copy-start.13
  44.9 10.7 %copy-start.14 = (f32[4,96,128]{2,1,0:T(8,128)S(1)}, f32[4,96,128]{2,1,0:T(8,128)}, u32[]{:S(2)}) copy-start(f32[4,96,128]{2,1,0:T(8,128)} %get-tuple-element.20) | copy-start | bytes 589828
  44.9 5.8 %collective-permute-start.4 = (f32[4,96,128]{2,1,0:T(8,128)}, f32[4,96,128]{2,1,0:T(8,128)S(1)}, u32[]{:S(2)}, u32[]{:S(2)}) collective-permute-start(f32[4,96,128]{2,1,0:T(8,128)} %get-tuple-element.20), channel_id=1, source_target_pairs={{0,6},{1,7},{2,0},{3,1},{4,2},{5,3},{6,4},{7,5},{8,14},{9,15},{10,... | collective-permute-start | bytes 589832 | tf_op jit(solution)/shard_map/ppermute | solution.py:427
  45.9 7.7 %collective-permute-start.2 = (f32[4,96,128]{2,1,0:T(8,128)}, f32[4,96,128]{2,1,0:T(8,128)S(1)}, u32[]{:S(2)}, u32[]{:S(2)}) collective-permute-start(f32[4,96,128]{2,1,0:T(8,128)} %get-tuple-element.20), channel_id=1, source_target_pairs={{0,2},{1,3},{2,4},{3,5},{4,6},{5,7},{6,0},{7,1},{8,10},{9,11},{10,... | collective-permute-start | bytes 589832 | tf_op jit(solution)/shard_map/ppermute | solution.py:427
  46.4 7.3 %collective-permute-start.1 = (f32[4,96,128]{2,1,0:T(8,128)}, f32[4,96,128]{2,1,0:T(8,128)S(1)}, u32[]{:S(2)}, u32[]{:S(2)}) collective-permute-start(f32[4,96,128]{2,1,0:T(8,128)} %get-tuple-element.20), channel_id=1, source_target_pairs={{0,8},{1,9},{2,10},{3,11},{4,12},{5,13},{6,14},{7,15},{8,0},{9,1},... | collective-permute-start | bytes 589832 | tf_op jit(solution)/shard_map/ppermute | solution.py:427
  53.7 4.4 %copy-start = (f32[8,128,128]{2,1,0:T(8,128)S(1)}, f32[8,128,128]{2,1,0:T(8,128)}, u32[]{:S(2)}) copy-start(f32[8,128,128]{2,1,0:T(8,128)} %constant.145.clone.tw3) | copy-start | bytes 1572868
  53.7 4.4 %copy-start.1 = (bf16[256,768]{1,0:T(8,128)(2,1)S(1)}, bf16[256,768]{1,0:T(8,128)(2,1)}, u32[]{:S(2)}) copy-start(bf16[256,768]{1,0:T(8,128)(2,1)} %constant.142.clone.e2) | copy-start | bytes 1179652
  53.7 4.4 %copy-start.2 = (bf16[288,256]{1,0:T(8,128)(2,1)S(1)}, bf16[288,256]{1,0:T(8,128)(2,1)}, u32[]{:S(2)}) copy-start(bf16[288,256]{1,0:T(8,128)(2,1)} %constant.141.clone.e1) | copy-start | bytes 442372
  53.8 4.4 %copy-start.3 = (f32[2,128,128]{2,1,0:T(8,128)S(1)}, f32[2,128,128]{2,1,0:T(8,128)}, u32[]{:S(2)}) copy-start(f32[2,128,128]{2,1,0:T(8,128)} %constant.143.clone.tw) | copy-start | bytes 393220
  53.8 4.4 %copy-start.6 = (f32[64,2,128]{2,1,0:T(2,128)S(1)}, f32[64,2,128]{2,1,0:T(2,128)}, u32[]{:S(2)}) copy-start(f32[64,2,128]{2,1,0:T(2,128)} %constant.144.clone.twb) | copy-start | bytes 196612
  53.8 7.1 %collective-permute-start.6 = (f32[3,4,96,128]{3,2,1,0:T(8,128)S(1)}, f32[3,4,96,128]{3,2,1,0:T(8,128)S(1)}, u32[]{:S(2)}, u32[]{:S(2)}) collective-permute-start(f32[3,4,96,128]{3,2,1,0:T(8,128)S(1)} %pad_maximum_fusion.2), channel_id=1, source_target_pairs={{0,1},{1,0},{2,3},{3,2},{4,5},{5,4},{6,7},{7,6},{8,9},{9,8},{10,11... | collective-permute-start | bytes 1769480 | tf_op jit(solution)/shard_map/ppermute | solution.py:427
  55.6 2.5 %collective-permute-start.7 = (f32[1,4,96,128]{3,2,1,0:T(8,128)S(1)}, f32[1,4,96,128]{3,2,1,0:T(8,128)S(1)}, u32[]{:S(2)}, u32[]{:S(2)}) collective-permute-start(f32[1,4,96,128]{3,2,1,0:T(8,128)S(1)} %bitcast.35), channel_id=1, source_target_pairs={{0,1},{1,0},{2,3},{3,2},{4,5},{5,4},{6,7},{7,6},{8,9},{9,8},{10,11... | collective-permute-start | bytes 589832 | tf_op jit(solution)/shard_map/ppermute | solution.py:427
  55.8 14.0 %collective-permute-start.5 = (f32[6,96,128]{2,1,0:T(8,128)S(1)}, f32[6,96,128]{2,1,0:T(8,128)S(1)}, u32[]{:S(2)}, u32[]{:S(2)}) collective-permute-start(f32[6,96,128]{2,1,0:T(8,128)S(1)} %get-tuple-element.31), channel_id=1, source_target_pairs={{0,6},{1,7},{2,0},{3,1},{4,2},{5,3},{6,4},{7,5},{8,14},{9,15},{10,... | collective-permute-start | bytes 884744 | tf_op jit(solution)/shard_map/ppermute | solution.py:427
  58.1 11.8 %collective-permute-start.3 = (f32[6,96,128]{2,1,0:T(8,128)S(1)}, f32[6,96,128]{2,1,0:T(8,128)S(1)}, u32[]{:S(2)}, u32[]{:S(2)}) collective-permute-start(f32[6,96,128]{2,1,0:T(8,128)S(1)} %get-tuple-element.32), channel_id=1, source_target_pairs={{0,2},{1,3},{2,4},{3,5},{4,6},{5,7},{6,0},{7,1},{8,10},{9,11},{10,... | collective-permute-start | bytes 884744 | tf_op jit(solution)/shard_map/ppermute | solution.py:427
  70.0 8.7 %collective-permute-start.11 = (f32[3,4,96,128]{3,2,1,0:T(8,128)S(1)}, f32[3,4,96,128]{3,2,1,0:T(8,128)S(1)}, u32[]{:S(2)}, u32[]{:S(2)}) collective-permute-start(f32[3,4,96,128]{3,2,1,0:T(8,128)S(1)} %pad_maximum_fusion.3), channel_id=1, source_target_pairs={{0,1},{1,0},{2,3},{3,2},{4,5},{5,4},{6,7},{7,6},{8,9},{9,8},{10,11... | collective-permute-start | bytes 1769480 | tf_op jit(solution)/shard_map/ppermute | solution.py:427
  70.8 6.1 %collective-permute-start.8 = (f32[2,96,128]{2,1,0:T(8,128)S(1)}, f32[2,96,128]{2,1,0:T(8,128)S(1)}, u32[]{:S(2)}, u32[]{:S(2)}) collective-permute-start(f32[2,96,128]{2,1,0:T(8,128)S(1)} %get-tuple-element.28), channel_id=1, source_target_pairs={{0,2},{1,3},{2,4},{3,5},{4,6},{5,7},{6,0},{7,1},{8,10},{9,11},{10,... | collective-permute-start | bytes 294920 | tf_op jit(solution)/shard_map/ppermute | solution.py:427
  70.8 6.1 %collective-permute-start.9 = (f32[2,96,128]{2,1,0:T(8,128)S(1)}, f32[2,96,128]{2,1,0:T(8,128)S(1)}, u32[]{:S(2)}, u32[]{:S(2)}) collective-permute-start(f32[2,96,128]{2,1,0:T(8,128)S(1)} %get-tuple-element.30), channel_id=1, source_target_pairs={{0,6},{1,7},{2,0},{3,1},{4,2},{5,3},{6,4},{7,5},{8,14},{9,15},{10,... | collective-permute-start | bytes 294920 | tf_op jit(solution)/shard_map/ppermute | solution.py:427
  76.8 1.8 %collective-permute-start.10 = (f32[1,4,96,128]{3,2,1,0:T(8,128)S(1)}, f32[1,4,96,128]{3,2,1,0:T(8,128)S(1)}, u32[]{:S(2)}, u32[]{:S(2)}) collective-permute-start(f32[1,4,96,128]{3,2,1,0:T(8,128)S(1)} %maximum_bitcast_fusion), channel_id=1, source_target_pairs={{0,1},{1,0},{2,3},{3,2},{4,5},{5,4},{6,7},{7,6},{8,9},{9,8},{10,11... | collective-permute-start | bytes 589832 | tf_op jit(solution)/shard_map/ppermute | solution.py:427
  87.6 2.8 %copy-start.12 = (f32[8,128]{1,0:T(8,128)S(1)}, f32[8,128]{1,0:T(8,128)}, u32[]{:S(2)}) copy-start(f32[8,128]{1,0:T(8,128)} %get-tuple-element.26.sig) | copy-start | bytes 12292

commit v4 on v3

--- a/solution.py
+++ b/solution.py
@@ -15,6 +15,7 @@
 BF = jnp.bfloat16
 F32 = jnp.float32
 INV_VMEM = 24 << 20
+FWD_VMEM = 58 << 20
 OUT_VMEM = 24 << 20
 
 
@@ -77,10 +78,6 @@
     t3[:, :, 0:8] = c.reshape(8, 8, 128).transpose(0, 2, 1)
     t3[:, :, 8:16] = s.reshape(8, 8, 128).transpose(0, 2, 1)
     t["tw3"] = t3
-    k = np.arange(6)[:, None] * 65536 + np.arange(65536)[None, :]
-    amp = np.where(k >= K_LOW, (np.maximum(k, 1) / K_LOW) ** (-7.0 / 6.0), 0.0)
-    amp = np.concatenate([amp, np.zeros((2, 65536))])
-    t["amp"] = amp.reshape(8, 16, 4096).transpose(1, 0, 2).astype(np.float32)
     return t
 
 
@@ -94,58 +91,77 @@
     return jnp.dot(a, b, preferred_element_type=F32)
 
 
-def psd_kernel(me, bins, vals, amp, out, g):
+def psd_kernel(me, bins_hbm, vals_hbm, out, g, tr, bins, vals, sems):
+    fetch = [
+        pltpu.make_async_copy(bins_hbm, bins, sems.at[0]),
+        pltpu.make_async_copy(vals_hbm, vals, sems.at[1]),
+    ]
+    for copy in fetch:
+        copy.start()
+    row = lax.broadcasted_iota(jnp.int32, (256, 128), 0)
+    lane = lax.broadcasted_iota(jnp.int32, (256, 128), 1)
+    k = (row & 7) * 65536 + me[0] * 4096 + (row >> 3) * 128 + lane
+    ratio = jnp.maximum(k.astype(F32) / K_LOW, 1.0)
+    amp = jnp.where(k >= K_LOW, jnp.exp(jnp.log(ratio) * (-7.0 / 6.0)), 0.0)
+    for copy in fetch:
+        copy.wait()
+    v0 = vals[...]
+    p0 = v0.astype(BF)
+    v1 = v0 - p0.astype(F32)
+    p1 = v1.astype(BF)
+    p2 = (v1 - p1.astype(F32)).astype(BF)
+    parts = jnp.concatenate([p0, p1, p2])
     width = 512
-
-    def tile(i, total):
+    low = lax.broadcasted_iota(jnp.int32, (128, width), 0)
+    high = lax.broadcasted_iota(jnp.int32, (64, width), 0)
+    g[...] = jnp.ones((256, 128), F32)
+
+    def chunk(i, carry):
         at = pl.multiple_of(i * width, width)
         idx = bins[:, pl.ds(at, width)]
-        parts = [idx[:, 128 * q : 128 * q + 128] for q in range(width // 128)]
-        hi, lo = [v >> 7 for v in parts], [v & 127 for v in parts]
-        acc = [jnp.ones((8, 128), F32) for _ in parts]
-        for h in range(64):
-            row = jnp.broadcast_to(vals[h : h + 1, :], (8, 128))
-            for q in range(len(parts)):
-                got = jnp.take_along_axis(row, lo[q], axis=1)
-                acc[q] = jnp.where(hi[q] == h, got, acc[q])
-        for q in range(len(parts)):
-            pos = pl.multiple_of(at + 128 * q, 128)
-            a = amp[0, :, pl.ds(pos, 128)]
-            f = a / acc[q]
-            total = total + f * a
-            row8 = pl.multiple_of(i * (width // 16) + 8 * q, 8)
-            g[pl.ds(row8, 8), :] = f * (1.0 / 1024.0)
-        return total
-
-    total = lax.fori_loop(0, 4096 // width, tile, jnp.zeros((8, 128), F32))
-    share = jnp.broadcast_to(jnp.sum(total, keepdims=True), (256, 128))
-    row = lax.broadcasted_iota(jnp.int32, (256, 128), 0) & 7
-    full = jnp.where(row >= 6, share, g[...])
+        for ah in range(6):
+            one = idx[ah : ah + 1]
+            hot = jnp.where((one & 127) == low, 1.0, 0.0).astype(BF)
+            got = dot(parts, hot)
+            got = got[:64] + got[64:128] + got[128:]
+            got = jnp.sum(jnp.where((one >> 7) == high, got, 0.0), axis=0, keepdims=True)
+            for q in range(width // 128):
+                g[pl.ds(i * (width // 16) + 8 * q + ah, 1), :] = got[:, 128 * q : 128 * q + 128]
+        return carry
+
+    lax.fori_loop(0, 4096 // width, chunk, 0)
+    f = amp / g[...]
+    rows = (row & 7) < 6
+    share = jnp.sum(jnp.where(rows, f * amp, 0.0), keepdims=True)
+    full = jnp.where(rows, f * (1.0 / 1024.0), jnp.broadcast_to(share, (256, 128)))
     for half in range(2):
-        tr = full[128 * half : 128 * half + 128].T
-        for low in range(2):
+        tr[...] = full[128 * half : 128 * half + 128].T
+        for low_bit in range(2):
             for d in range(16):
-                at = 8 * half + 4 * low
-                out[d, at : at + 4, :] = tr[64 * low + 4 * d : 64 * low + 4 * d + 4]
-
-
-def psd_call(me, bins, vals, amp):
+                at = 8 * half + 4 * low_bit
+                src = 64 * low_bit + 4 * d
+                out[d, at : at + 4, :] = tr[src : src + 4, :]
+
+
+def psd_call(me, bins, vals):
     return pl.pallas_call(
         psd_kernel,
         grid_spec=pltpu.PrefetchScalarGridSpec(
             num_scalar_prefetch=1,
             grid=(1,),
-            in_specs=[
-                pl.BlockSpec((8, 4096), lambda i, m: (0, 0)),
-                pl.BlockSpec((64, 128), lambda i, m: (0, 0)),
-                pl.BlockSpec((1, 8, 4096), lambda i, m: (m[0], 0, 0)),
+            in_specs=[pl.BlockSpec(memory_space=pl.ANY)] * 2,
+            out_specs=pl.BlockSpec((16, 16, 128), lambda i, m: (0, 0, 0)),
+            scratch_shapes=[
+                pltpu.VMEM((256, 128), F32),
+                pltpu.VMEM((128, 128), F32),
+                pltpu.VMEM((8, 4096), jnp.int32),
+                pltpu.VMEM((64, 128), F32),
+                pltpu.SemaphoreType.DMA((2,)),
             ],
-            out_specs=pl.BlockSpec((16, 16, 128), lambda i, m: (0, 0, 0)),
-            scratch_shapes=[pltpu.VMEM((256, 128), F32)],
         ),
         out_shape=jax.ShapeDtypeStruct((16, 16, 128), F32),
-        compiler_params=pltpu.CompilerParams(vmem_limit_bytes=50 << 20),
-    )(me, bins, vals, amp)
+        compiler_params=pltpu.CompilerParams(vmem_limit_bytes=16 << 20),
+    )(me, bins, vals)
 
 
 def fwd_kernel(me, tail, own, l1, tw1, m2, tj, extra, out):
@@ -190,7 +206,7 @@
             out_specs=pl.BlockSpec((16, 80, 128), lambda i, m: (0, 0, 0)),
         ),
         out_shape=jax.ShapeDtypeStruct((16, 80, 128), F32),
-        compiler_params=pltpu.CompilerParams(vmem_limit_bytes=50 << 20),
+        compiler_params=pltpu.CompilerParams(vmem_limit_bytes=FWD_VMEM),
     )(me, tail, own, l1, tw1, m2, tj, extra)
 
 
@@ -226,16 +242,13 @@
     for b in range(4):
         rows = [64 + 80 * (i >> 2) + 4 * (i & 3) + b for i in range(8)]
         g.append(swap_low_bits([p[pl.ds(r, 8, stride=160), :] for r in rows]))
+    quarters = []
+    for n in range(4):
+        rows = [80 * (n + 4 * q) for q in range(4)]
+        quarters.append(fft4([(p[i + 32 : i + 64, :], p[i : i + 32, :]) for i in rows]))
     for ah in range(6):
-        re = jnp.zeros((32, 128), F32)
-        im = jnp.zeros((32, 128), F32)
-        for j in range(16):
-            c = math.cos(2 * math.pi * (j * ah % 16) / 16)
-            s = -math.sin(2 * math.pi * (j * ah % 16) / 16)
-            pr = p[80 * j : 80 * j + 32, :]
-            pi = p[80 * j + 32 : 80 * j + 64, :]
-            re = re + (pr * c - pi * s)
-            im = im + (pr * s + pi * c)
+        z = [cmul(quarters[n][ah % 4], n * ah, 16) for n in range(4)]
+        im, re = add(add(z[0], z[1]), add(z[2], z[3]))
         re, im = swap_groups(re), swap_groups(im)
         for b in range(4):
             at = slice(8 * b, 8 * b + 8)
@@ -252,6 +265,7 @@
             jax.ShapeDtypeStruct((4, 96, 128), F32),
             jax.ShapeDtypeStruct((8, 128), F32),
         ],
+        compiler_params=pltpu.CompilerParams(vmem_limit_bytes=16 << 20),
     )(p)
 
 
@@ -453,7 +467,7 @@
     count = lax.axis_size("tm")
     tail = lax.ppermute(own, "tm", [(i, i + 1) for i in range(count - 1)])
 
-    extra = psd_call(me, psd_bins, psd_values.reshape(64, 128), t["amp"])
+    extra = psd_call(me, psd_bins, psd_values.reshape(64, 128))
     sent_out = fwd_call(me, tail, own, t["l1"], t["tw1"], t["m2"], t["tj"], extra)
     sent_out, chirp_slope, chirp_curve = lax.optimization_barrier(
         (sent_out, chirp_slope, chirp_curve)
@@ -472,6 +486,7 @@
     right = sent(w, 0, 1, 0)
     left = sent(w, 0, -1, 0)
     h = work([w], [(0, 0)], None)
+    up, right, left, h = lax.optimization_barrier((up, right, left, h))
     right2 = sent(jnp.concatenate([up, right[:2]]), 0, 1, 0)
     left2 = sent(jnp.concatenate([up, left[2:]]), 0, -1, 0)
     h = work([up, right, left], [(1, 0), (0, -1), (0, 1)], h)
@@ -480,6 +495,7 @@
     left3 = sent(left2[2:4], 0, -1, 0)
     far = jnp.concatenate([right2[4:], left2[4:]])
     h = work([right2[:4], left2[:4], far], [(1, -1), (1, 1), (0, 2)], h)
+    right3, left3, h = lax.optimization_barrier((right3, left3, h))
     h = work([jnp.concatenate([right3, left3])], [(1, 2)], h)
     out = out_call(h, scale)
     return out.reshape(4096, 2, 128).transpose(1, 0, 2).reshape(2, 4096 * 128)

time: 100 us -> 88.8 us (0.89)
  waiting for transfers between devices: 16 us -> 11.2 us
  local copies, waits for them, and re-layouts: 6.9 us -> 3.73 us
  Pallas kernels: 45.7 us -> 42.8 us
    ppermute x11, waiting for transfers between devices: 10.7 us -> 5.95 us  [sent(): return lax.ppermute(v, 'tmpl', route)]
    unnamed x34 -> x22, local copies, waits for them, and re-layouts: 6.17 us -> 2.99 us
    pallas_call x1, Pallas kernels: 6.51 us -> 4.73 us  [psd_call(): pl.pallas_call(psd_kernel, grid_spec=pltpu.PrefetchScalarGridSpec(num_sca...]
    pallas_call x1, Pallas kernels: 3.26 us -> 1.56 us  [mix_call(): pl.pallas_call(mix_kernel, out_shape=[jax.ShapeDtypeStruct((4, 96, 128),...]
    pallas_call x1, Pallas kernels: 3.46 us -> 4.49 us  [fwd_call(): pl.pallas_call(fwd_kernel, grid_spec=pltpu.PrefetchScalarGridSpec(num_sca...]
  transfers between devices with their start and end apart: 13 -> 13, of which waited for: 5 -> 6; matrix products, arithmetic and copies ran while one was open for 9% -> 10% of each run, Pallas kernels for 18% -> 28%
where the time goes in v4:
time: 88.8 us; the launch traced here: 88.4 us
  Pallas kernels  42.8 us (48%)
  starting transfers between devices  22.2 us (25%)
  waiting for transfers between devices  11.2 us (13%)
  other arithmetic  8 us (9%)
  local copies, waits for them, and re-layouts  3.73 us (4%)
    pallas_call x4, Pallas kernels, inv_call(): pl.pallas_call(inv_kernel, grid_spec=pltpu.PrefetchScalarGridSpec(num_sca...  22.7 us
    ppermute x11, starting transfers between devices, sent(): return lax.ppermute(v, 'tmpl', route)  10.5 us
    pallas_call x1, Pallas kernels, out_call(): pl.pallas_call(out_kernel, grid=(16,), in_specs=[pl.BlockSpec((1, 64, 2,...  9.33 us
    all_to_all x1, starting transfers between devices, local(): lax.all_to_all(sent_out, 'tmpl', split_axis=0, concat_axis=0, tiled=True)  7.72 us
    ppermute x11, waiting for transfers between devices, sent(): return lax.ppermute(v, 'tmpl', route)  5.95 us
    all_to_all x1, waiting for transfers between devices, local(): lax.all_to_all(sent_out, 'tmpl', split_axis=0, concat_axis=0, tiled=True)  5.26 us
    pallas_call x1, Pallas kernels, psd_call(): pl.pallas_call(psd_kernel, grid_spec=pltpu.PrefetchScalarGridSpec(num_sca...  4.73 us
    pallas_call x1, Pallas kernels, fwd_call(): pl.pallas_call(fwd_kernel, grid_spec=pltpu.PrefetchScalarGridSpec(num_sca...  4.49 us
  transfers between devices with their start and end apart: 13, of which 6 were waited for; matrix products, arithmetic and copies ran while one was open for 10% of the time, Pallas kernels for 28%

profile of v4, /device:TPU:1, one launch (start us, length us, event | category | flops | bytes accessed | tf_op | source)
XLA Modules:
  0.0 88.4 jit_solution(883726812053852565)
XLA Ops:
  0.0 4.0 %collective-permute-start = (f32[256,128]{1,0:T(8,128)}, f32[256,128]{1,0:T(8,128)S(1)}, u32[]{:S(2)}, u32[]{:S(2)}) collective-permute-start(f32[256,128]{1,0:T(8,128)} %bitcast.35), channel_id=1, source_target_pairs={{0,16},{16,32},{32,48},{48,64},{64,80},{80,96},{96,112},{1,17},{17... | collective-permute-start | bytes 393224 | tf_op jit(solution)/shard_map/ppermute | solution.py:468
  4.1 0.7 broadcast_add_fusion
  4.8 0.0 copy-start.6
  4.8 0.9 %copy-done.6 = s32[8,4096]{1,0:T(8,128)S(1)} copy-done((s32[8,4096]{1,0:T(8,128)S(1)}, s32[8,4096]{1,0:T(8,128)}, u32[]{:S(2)}) %copy-start.6) | copy-done | bytes 131096
  5.7 0.0 copy-start.7
  5.7 0.8 copy-done.7
  6.5 4.7 %shard_map.145.extra = f32[16,16,128]{2,1,0:T(8,128)S(1)} custom-call(s32[1]{0:T(128)} %bitcast.me, s32[8,4096]{1,0:T(8,128)S(1)} %copy-done.6, f32[64,128]{1,0:T(8,128)S(1)} %bitcast.28), custom_call_target="tpu_custom_call" | custom-call | tf_op jit(solution)/shard_map/pallas_call | solution.py:147
  11.2 0.0 copy-start.5
  11.3 0.6 copy-done.5
  11.9 0.0 collective-permute-done.tail
  11.9 0.6 copy-done.8
  12.5 4.5 %shard_map.146 = f32[16,80,128]{2,1,0:T(8,128)} custom-call(s32[1]{0:T(128)} %bitcast.me, f32[256,128]{1,0:T(8,128)} %copy-done.8, f32[256,128]{1,0:T(8,128)} %bitcast.36, bf16[2,1024,512]{2,1,0:T(8,128)(2,1)} %constant.135.clone.l1, f32[2,512,128]{2,1,0:T(8,128)} %constant.136.clone.tw1, bf16[768,256]{1,0:T(8,128)(2,1)} %constant.137.clone.m2, ...), custom_call_target="tpu_custom_call" | custom-call | tf_op jit(solution)/shard_map/pallas_call | solution.py:192
  17.0 7.7 %all-to-all-start = ((f32[16,80,128]{2,1,0:T(8,128)}), f32[16,80,128]{2,1,0:T(8,128)S(1)}, u32[]{:S(2)}, u32[]{:S(2)}) async-start(f32[16,80,128]{2,1,0:T(8,128)} %shard_map.146), calls=%async_computation | async-start | bytes 1310720 | tf_op jit(solution)/shard_map/all_to_all | solution.py:475
  24.8 0.0 copy-done.9
  24.8 0.0 copy-done.10
  24.8 0.0 copy-start
  24.8 0.0 copy-start.1
  24.8 0.0 copy-start.2
  24.8 0.0 copy-start.3
  24.8 0.0 copy-start.4
  24.8 0.7 fusion.16
  25.5 1.3 %compare_select_fusion.3 = s32[128]{0:T(128)S(1)} fusion(s32[]{:T(128)} %bitcast.4, s32[]{:T(128)} %bitcast.3), kind=kLoop, calls=%fused_computation.43 | loop fusion | flops 256 | bytes 520 | tf_op jit(solution)/shard_map/jit(_where)/select_n | solution.py:453
  26.8 1.2 %fusion.10 = s32[128]{0:T(128)S(1)} fusion(s32[]{:T(128)} %bitcast.6, s32[]{:T(128)} %bitcast.5), kind=kLoop, calls=%fused_computation.48 | loop fusion | flops 384 | bytes 520 | tf_op jit(solution)/shard_map/mul | solution.py:457
  28.0 0.1 add_select_fusion.3
  28.1 1.3 %compare_select_fusion.5 = s32[4]{0:T(128)S(1)} fusion(s32[]{:T(128)} %bitcast.4, s32[]{:T(128)} %bitcast.3), kind=kLoop, calls=%fused_computation.45 | loop fusion | flops 8 | bytes 24 | tf_op jit(solution)/shard_map/jit(_where)/select_n | solution.py:446
  29.4 1.2 %compare_select_fusion.4 = s32[4]{0:T(128)S(1)} fusion(s32[]{:T(128)} %bitcast.6, s32[]{:T(128)} %bitcast.5), kind=kLoop, calls=%fused_computation.44 | loop fusion | flops 8 | bytes 24 | tf_op jit(solution)/shard_map/jit(_where)/select_n | solution.py:447
  30.6 1.1 %fusion.7.phi = f32[8,8,4,128]{3,2,1,0:T(4,128)S(1)} fusion(s32[4]{0:T(128)S(1)} %fusion.11, s32[8,8,128]{2,1,0:T(8,128)S(1)} %get-tuple-element.48, s32[4]{0:T(128)S(1)} %compare_select_fusion.4, s32[8,8,128]{2,1,0:T(8,128)S(1)} %get-tuple-element.47, s32[4]{0:T(128)S(1)} %compare_select_fusion.5), kind=kLoop, calls=%fused_computation.25 | loop fusion | flops 557056 | bytes 196656 | tf_op jit(solution)/shard_map/cos | solution.py:451
  31.7 0.7 fusion.3.psi
  32.4 5.3 %all-to-all-done = f32[16,80,128]{2,1,0:T(8,128)S(1)} async-done(((f32[16,80,128]{2,1,0:T(8,128)}), f32[16,80,128]{2,1,0:T(8,128)S(1)}, u32[]{:S(2)}, u32[]{:S(2)}) %all-to-all-start) | async-done | bytes 655392 | tf_op jit(solution)/shard_map/all_to_all | solution.py:475
  37.7 1.6 %shard_map.147 = (f32[4,96,128]{2,1,0:T(8,128)S(1)}, f32[8,128]{1,0:T(8,128)S(1)}) custom-call(f32[1280,128]{1,0:T(8,128)S(1)} %bitcast.25), custom_call_target="tpu_custom_call" | custom-call | tf_op jit(solution)/shard_map/pallas_call | solution.py:262
  39.2 1.0 %collective-permute-start.4 = (f32[1,4,96,128]{3,2,1,0:T(8,128)S(1)}, f32[1,4,96,128]{3,2,1,0:T(8,128)S(1)}, u32[]{:S(2)}, u32[]{:S(2)}) collective-permute-start(f32[1,4,96,128]{3,2,1,0:T(8,128)S(1)} %bitcast.26), channel_id=1, source_target_pairs={{0,1},{1,0},{2,3},{3,2},{4,5},{5,4},{6,7},{7,6},{8,9},{9,8},{10,11... | collective-permute-start | bytes 589832 | tf_op jit(solution)/shard_map/ppermute | solution.py:441
  40.3 0.1 collective-permute-start.3
  40.4 1.3 %collective-permute-start.2 = (f32[4,96,128]{2,1,0:T(8,128)S(1)}, f32[4,96,128]{2,1,0:T(8,128)S(1)}, u32[]{:S(2)}, u32[]{:S(2)}) collective-permute-start(f32[4,96,128]{2,1,0:T(8,128)S(1)} %get-tuple-element.27), channel_id=1, source_target_pairs={{0,2},{1,3},{2,4},{3,5},{4,6},{5,7},{6,0},{7,1},{8,10},{9,11},{10,... | collective-permute-start | bytes 589832 | tf_op jit(solution)/shard_map/ppermute | solution.py:441
  41.8 0.3 collective-permute-start.1
  42.0 0.0 collective-permute-done.4
  42.1 0.0 copy-done
  42.1 0.0 copy-done.1
  42.1 0.0 copy-done.2
  42.1 0.0 copy-done.3
  42.1 0.0 copy-done.4
  42.1 2.7 %shard_map.148.rest_0_ = f32[16,64,2,8,256]{4,3,2,1,0:T(8,128)S(1)} custom-call(s32[1]{0:T(128)} %bitcast.me, f32[1,8,96,128]{3,2,1,0:T(8,128)S(1)} %pad_maximum_fusion.4.w, f32[8,8,4,128]{3,2,1,0:T(4,128)S(1)} %fusion.7.phi, f32[8,48,128]{2,1,0:T(8,128)S(1)} %fusion.3.psi, f32[2,128,128]{2,1,0:T(8,128)S(1)} %copy-done.3, f32[64,2,128]{2,1,0:T(2,128)S(1)} %copy-done.4, ...), custom_call_target="tpu_custom_call" | custom-call | flops 1500000000 | bytes 3000000 | tf_op jit(solution)/shard_map/pallas_call | solution.py:335
  44.9 1.9 %collective-permute-done.3 = f32[4,96,128]{2,1,0:T(8,128)S(1)} collective-permute-done((f32[4,96,128]{2,1,0:T(8,128)S(1)}, f32[4,96,128]{2,1,0:T(8,128)S(1)}, u32[]{:S(2)}, u32[]{:S(2)}) %collective-permute-start.3) | collective-permute-done | bytes 196640 | tf_op jit(solution)/shard_map/ppermute | solution.py:441
  46.7 0.6 collective-permute-done.2
  47.4 1.7 %collective-permute-done.1 = f32[4,96,128]{2,1,0:T(8,128)S(1)} collective-permute-done((f32[4,96,128]{2,1,0:T(8,128)S(1)}, f32[4,96,128]{2,1,0:T(8,128)S(1)}, u32[]{:S(2)}, u32[]{:S(2)}) %collective-permute-start.1) | collective-permute-done | bytes 196640 | tf_op jit(solution)/shard_map/ppermute | solution.py:441
  49.1 1.6 %collective-permute-start.7 = (f32[3,4,96,128]{3,2,1,0:T(8,128)S(1)}, f32[3,4,96,128]{3,2,1,0:T(8,128)S(1)}, u32[]{:S(2)}, u32[]{:S(2)}) collective-permute-start(f32[3,4,96,128]{3,2,1,0:T(8,128)S(1)} %pad_maximum_fusion.2), channel_id=1, source_target_pairs={{0,1},{1,0},{2,3},{3,2},{4,5},{5,4},{6,7},{7,6},{8,9},{9,8},{10,11... | collective-permute-start | bytes 1769480 | tf_op jit(solution)/shard_map/ppermute | solution.py:441
  50.8 1.4 %collective-permute-start.6 = (f32[6,96,128]{2,1,0:T(8,128)S(1)}, f32[6,96,128]{2,1,0:T(8,128)S(1)}, u32[]{:S(2)}, u32[]{:S(2)}) collective-permute-start(f32[6,96,128]{2,1,0:T(8,128)S(1)} %get-tuple-element.45), channel_id=1, source_target_pairs={{0,6},{1,7},{2,0},{3,1},{4,2},{5,3},{6,4},{7,5},{8,14},{9,15},{10,... | collective-permute-start | bytes 884744 | tf_op jit(solution)/shard_map/ppermute | solution.py:441
  52.2 0.1 collective-permute-start.5
  52.3 0.0 collective-permute-done.7
  52.3 0.1 pad_maximum_fusion.w
  52.4 8.6 %shard_map.149.rest_0_ = f32[16,64,2,8,256]{4,3,2,1,0:T(8,128)S(1)} custom-call(s32[1]{0:T(128)} %bitcast.me, f32[3,8,96,128]{3,2,1,0:T(8,128)S(1)} %pad_maximum_fusion.w, f32[8,8,4,128]{3,2,1,0:T(4,128)S(1)} %fusion.7.phi, f32[8,48,128]{2,1,0:T(8,128)S(1)} %fusion.3.psi, f32[2,128,128]{2,1,0:T(8,128)S(1)} %copy-done.3, ...), custom_call_target="tpu_custom_call", output_to_operand_aliasing={{}: (9, {})} | custom-call | flops 4499999744 | bytes 9000000 | tf_op jit(solution)/shard_map/pallas_call | solution.py:335
  61.1 0.0 collective-permute-done.6
  61.1 0.6 collective-permute-done.5
  61.8 1.2 %collective-permute-start.10 = (f32[3,4,96,128]{3,2,1,0:T(8,128)S(1)}, f32[3,4,96,128]{3,2,1,0:T(8,128)S(1)}, u32[]{:S(2)}, u32[]{:S(2)}) collective-permute-start(f32[3,4,96,128]{3,2,1,0:T(8,128)S(1)} %pad_maximum_fusion.3), channel_id=1, source_target_pairs={{0,1},{1,0},{2,3},{3,2},{4,5},{5,4},{6,7},{7,6},{8,9},{9,8},{10,11... | collective-permute-start | bytes 1769480 | tf_op jit(solution)/shard_map/ppermute | solution.py:441
  63.0 0.0 collective-permute-start.8
  63.1 2.7 %collective-permute-start.9 = (f32[2,96,128]{2,1,0:T(8,128)S(1)}, f32[2,96,128]{2,1,0:T(8,128)S(1)}, u32[]{:S(2)}, u32[]{:S(2)}) collective-permute-start(f32[2,96,128]{2,1,0:T(8,128)S(1)} %get-tuple-element.44), channel_id=1, source_target_pairs={{0,6},{1,7},{2,0},{3,1},{4,2},{5,3},{6,4},{7,5},{8,14},{9,15},{10,... | collective-permute-start | bytes 294920 | tf_op jit(solution)/shard_map/ppermute | solution.py:441
  65.7 0.0 collective-permute-done.10
  65.7 0.1 pad_maximum_fusion.1.w
  65.8 8.6 %shard_map.150.rest_0_ = f32[16,64,2,8,256]{4,3,2,1,0:T(8,128)S(1)} custom-call(s32[1]{0:T(128)} %bitcast.me, f32[3,8,96,128]{3,2,1,0:T(8,128)S(1)} %pad_maximum_fusion.1.w, f32[8,8,4,128]{3,2,1,0:T(4,128)S(1)} %fusion.7.phi, f32[8,48,128]{2,1,0:T(8,128)S(1)} %fusion.3.psi, f32[2,128,128]{2,1,0:T(8,128)S(1)} %copy-done.3, ...), custom_call_target="tpu_custom_call", output_to_operand_aliasing={{}: (9, {})} | custom-call | flops 4499999744 | bytes 9000000 | tf_op jit(solution)/shard_map/pallas_call | solution.py:335
  74.5 0.0 collective-permute-done.8
  74.5 0.0 collective-permute-done.9
  74.5 0.7 collective-permute-start.11
  75.2 1.1 %collective-permute-done.11 = f32[1,4,96,128]{3,2,1,0:T(8,128)S(1)} collective-permute-done((f32[1,4,96,128]{3,2,1,0:T(8,128)S(1)}, f32[1,4,96,128]{3,2,1,0:T(8,128)S(1)}, u32[]{:S(2)}, u32[]{:S(2)}) %collective-permute-start.11) | collective-permute-done | bytes 196640 | tf_op jit(solution)/shard_map/ppermute | solution.py:441
  76.3 2.7 %shard_map.151.h = f32[16,64,2,8,256]{4,3,2,1,0:T(8,128)S(1)} custom-call(s32[1]{0:T(128)} %bitcast.me, f32[1,8,96,128]{3,2,1,0:T(8,128)S(1)} %pad_maximum_fusion.5.w, f32[8,8,4,128]{3,2,1,0:T(4,128)S(1)} %fusion.7.phi, f32[8,48,128]{2,1,0:T(8,128)S(1)} %fusion.3.psi, f32[2,128,128]{2,1,0:T(8,128)S(1)} %copy-done.3, ...), custom_call_target="tpu_custom_call", output_to_operand_aliasing={{}: (9, {})} | custom-call | flops 1500000000 | bytes 3000000 | tf_op jit(solution)/shard_map/pallas_call | solution.py:335
  79.0 9.3 %shard_map.152 = f32[32,256,128]{2,1,0:T(8,128)} custom-call(f32[16,64,2,8,256]{4,3,2,1,0:T(8,128)S(1)} %shard_map.151.h, f32[8,128]{1,0:T(8,128)S(1)} %get-tuple-element.40.sig), custom_call_target="tpu_custom_call" | custom-call | tf_op jit(solution)/shard_map/pallas_call | solution.py:416
  (21 shorter events, 0.3 us)
Async XLA Ops:
  0.0 11.9 %collective-permute-start = (f32[256,128]{1,0:T(8,128)}, f32[256,128]{1,0:T(8,128)S(1)}, u32[]{:S(2)}, u32[]{:S(2)}) collective-permute-start(f32[256,128]{1,0:T(8,128)} %bitcast.35), channel_id=1, source_target_pairs={{0,16},{16,32},{32,48},{48,64},{64,80},{80,96},{96,112},{1,17},{17... | collective-permute-start | bytes 393224 | tf_op jit(solution)/shard_map/ppermute | solution.py:468
  4.8 0.9 %copy-start.6 = (s32[8,4096]{1,0:T(8,128)S(1)}, s32[8,4096]{1,0:T(8,128)}, u32[]{:S(2)}) copy-start(s32[8,4096]{1,0:T(8,128)} %bins_hbm.1) | copy-start | bytes 393220
  5.7 0.8 copy-start.7
  11.2 0.6 copy-start.5
  11.9 0.7 copy-start.8
  17.0 7.7 %copy-start.9 = (s32[2]{0:T(128)S(1)}, s32[2]{0:T(128)}, u32[]{:S(2)}) copy-start(s32[2]{0:T(128)} %param.18) | copy-start | bytes 28
  17.0 7.7 %copy-start.10 = (s32[2]{0:T(128)S(1)}, s32[2]{0:T(128)}, u32[]{:S(2)}) copy-start(s32[2]{0:T(128)} %param.19) | copy-start | bytes 28
  17.0 20.6 %all-to-all-start = ((f32[16,80,128]{2,1,0:T(8,128)}), f32[16,80,128]{2,1,0:T(8,128)S(1)}, u32[]{:S(2)}, u32[]{:S(2)}) async-start(f32[16,80,128]{2,1,0:T(8,128)} %shard_map.146), calls=%async_computation | async-start | bytes 1310720 | tf_op jit(solution)/shard_map/all_to_all | solution.py:475
  24.8 17.3 %copy-start = (f32[8,128,128]{2,1,0:T(8,128)S(1)}, f32[8,128,128]{2,1,0:T(8,128)}, u32[]{:S(2)}) copy-start(f32[8,128,128]{2,1,0:T(8,128)} %constant.143.clone.tw3) | copy-start | bytes 1572868
  24.8 17.3 %copy-start.1 = (bf16[256,768]{1,0:T(8,128)(2,1)S(1)}, bf16[256,768]{1,0:T(8,128)(2,1)}, u32[]{:S(2)}) copy-start(bf16[256,768]{1,0:T(8,128)(2,1)} %constant.140.clone.e2) | copy-start | bytes 1179652
  24.8 17.3 %copy-start.2 = (bf16[288,256]{1,0:T(8,128)(2,1)S(1)}, bf16[288,256]{1,0:T(8,128)(2,1)}, u32[]{:S(2)}) copy-start(bf16[288,256]{1,0:T(8,128)(2,1)} %constant.139.clone.e1) | copy-start | bytes 442372
  24.8 17.3 %copy-start.3 = (f32[2,128,128]{2,1,0:T(8,128)S(1)}, f32[2,128,128]{2,1,0:T(8,128)}, u32[]{:S(2)}) copy-start(f32[2,128,128]{2,1,0:T(8,128)} %constant.141.clone.tw) | copy-start | bytes 393220
  24.8 17.3 %copy-start.4 = (f32[64,2,128]{2,1,0:T(2,128)S(1)}, f32[64,2,128]{2,1,0:T(2,128)}, u32[]{:S(2)}) copy-start(f32[64,2,128]{2,1,0:T(2,128)} %constant.142.clone.twb) | copy-start | bytes 196612
  39.2 2.8 %collective-permute-start.4 = (f32[1,4,96,128]{3,2,1,0:T(8,128)S(1)}, f32[1,4,96,128]{3,2,1,0:T(8,128)S(1)}, u32[]{:S(2)}, u32[]{:S(2)}) collective-permute-start(f32[1,4,96,128]{3,2,1,0:T(8,128)S(1)} %bitcast.26), channel_id=1, source_target_pairs={{0,1},{1,0},{2,3},{3,2},{4,5},{5,4},{6,7},{7,6},{8,9},{9,8},{10,11... | collective-permute-start | bytes 589832 | tf_op jit(solution)/shard_map/ppermute | solution.py:441
  40.3 6.5 %collective-permute-start.3 = (f32[4,96,128]{2,1,0:T(8,128)S(1)}, f32[4,96,128]{2,1,0:T(8,128)S(1)}, u32[]{:S(2)}, u32[]{:S(2)}) collective-permute-start(f32[4,96,128]{2,1,0:T(8,128)S(1)} %get-tuple-element.27), channel_id=1, source_target_pairs={{0,6},{1,7},{2,0},{3,1},{4,2},{5,3},{6,4},{7,5},{8,14},{9,15},{10,... | collective-permute-start | bytes 589832 | tf_op jit(solution)/shard_map/ppermute | solution.py:441
  40.4 6.9 %collective-permute-start.2 = (f32[4,96,128]{2,1,0:T(8,128)S(1)}, f32[4,96,128]{2,1,0:T(8,128)S(1)}, u32[]{:S(2)}, u32[]{:S(2)}) collective-permute-start(f32[4,96,128]{2,1,0:T(8,128)S(1)} %get-tuple-element.27), channel_id=1, source_target_pairs={{0,2},{1,3},{2,4},{3,5},{4,6},{5,7},{6,0},{7,1},{8,10},{9,11},{10,... | collective-permute-start | bytes 589832 | tf_op jit(solution)/shard_map/ppermute | solution.py:441
  41.8 7.3 %collective-permute-start.1 = (f32[4,96,128]{2,1,0:T(8,128)S(1)}, f32[4,96,128]{2,1,0:T(8,128)S(1)}, u32[]{:S(2)}, u32[]{:S(2)}) collective-permute-start(f32[4,96,128]{2,1,0:T(8,128)S(1)} %get-tuple-element.27), channel_id=1, source_target_pairs={{0,8},{1,9},{2,10},{3,11},{4,12},{5,13},{6,14},{7,15},{8,0},{9,1},... | collective-permute-start | bytes 589832 | tf_op jit(solution)/shard_map/ppermute | solution.py:441
  49.1 3.2 %collective-permute-start.7 = (f32[3,4,96,128]{3,2,1,0:T(8,128)S(1)}, f32[3,4,96,128]{3,2,1,0:T(8,128)S(1)}, u32[]{:S(2)}, u32[]{:S(2)}) collective-permute-start(f32[3,4,96,128]{3,2,1,0:T(8,128)S(1)} %pad_maximum_fusion.2), channel_id=1, source_target_pairs={{0,1},{1,0},{2,3},{3,2},{4,5},{5,4},{6,7},{7,6},{8,9},{9,8},{10,11... | collective-permute-start | bytes 1769480 | tf_op jit(solution)/shard_map/ppermute | solution.py:441
  50.8 10.3 %collective-permute-start.6 = (f32[6,96,128]{2,1,0:T(8,128)S(1)}, f32[6,96,128]{2,1,0:T(8,128)S(1)}, u32[]{:S(2)}, u32[]{:S(2)}) collective-permute-start(f32[6,96,128]{2,1,0:T(8,128)S(1)} %get-tuple-element.45), channel_id=1, source_target_pairs={{0,6},{1,7},{2,0},{3,1},{4,2},{5,3},{6,4},{7,5},{8,14},{9,15},{10,... | collective-permute-start | bytes 884744 | tf_op jit(solution)/shard_map/ppermute | solution.py:441
  52.2 9.5 %collective-permute-start.5 = (f32[6,96,128]{2,1,0:T(8,128)S(1)}, f32[6,96,128]{2,1,0:T(8,128)S(1)}, u32[]{:S(2)}, u32[]{:S(2)}) collective-permute-start(f32[6,96,128]{2,1,0:T(8,128)S(1)} %get-tuple-element.46), channel_id=1, source_target_pairs={{0,2},{1,3},{2,4},{3,5},{4,6},{5,7},{6,0},{7,1},{8,10},{9,11},{10,... | collective-permute-start | bytes 884744 | tf_op jit(solution)/shard_map/ppermute | solution.py:441
  61.8 3.9 %collective-permute-start.10 = (f32[3,4,96,128]{3,2,1,0:T(8,128)S(1)}, f32[3,4,96,128]{3,2,1,0:T(8,128)S(1)}, u32[]{:S(2)}, u32[]{:S(2)}) collective-permute-start(f32[3,4,96,128]{3,2,1,0:T(8,128)S(1)} %pad_maximum_fusion.3), channel_id=1, source_target_pairs={{0,1},{1,0},{2,3},{3,2},{4,5},{5,4},{6,7},{7,6},{8,9},{9,8},{10,11... | collective-permute-start | bytes 1769480 | tf_op jit(solution)/shard_map/ppermute | solution.py:441
  63.0 11.4 %collective-permute-start.8 = (f32[2,96,128]{2,1,0:T(8,128)S(1)}, f32[2,96,128]{2,1,0:T(8,128)S(1)}, u32[]{:S(2)}, u32[]{:S(2)}) collective-permute-start(f32[2,96,128]{2,1,0:T(8,128)S(1)} %get-tuple-element.42), channel_id=1, source_target_pairs={{0,2},{1,3},{2,4},{3,5},{4,6},{5,7},{6,0},{7,1},{8,10},{9,11},{10,... | collective-permute-start | bytes 294920 | tf_op jit(solution)/shard_map/ppermute | solution.py:441
  63.1 11.4 %collective-permute-start.9 = (f32[2,96,128]{2,1,0:T(8,128)S(1)}, f32[2,96,128]{2,1,0:T(8,128)S(1)}, u32[]{:S(2)}, u32[]{:S(2)}) collective-permute-start(f32[2,96,128]{2,1,0:T(8,128)S(1)} %get-tuple-element.44), channel_id=1, source_target_pairs={{0,6},{1,7},{2,0},{3,1},{4,2},{5,3},{6,4},{7,5},{8,14},{9,15},{10,... | collective-permute-start | bytes 294920 | tf_op jit(solution)/shard_map/ppermute | solution.py:441
  74.5 1.8 %collective-permute-start.11 = (f32[1,4,96,128]{3,2,1,0:T(8,128)S(1)}, f32[1,4,96,128]{3,2,1,0:T(8,128)S(1)}, u32[]{:S(2)}, u32[]{:S(2)}) collective-permute-start(f32[1,4,96,128]{3,2,1,0:T(8,128)S(1)} %maximum_bitcast_fusion.1), channel_id=1, source_target_pairs={{0,1},{1,0},{2,3},{3,2},{4,5},{5,4},{6,7},{7,6},{8,9},{9,8},{10,11... | collective-permute-start | bytes 589832 | tf_op jit(solution)/shard_map/ppermute | solution.py:441

commit v5 on v4

--- a/solution.py
+++ b/solution.py
@@ -445,9 +445,9 @@
     row = jnp.arange(4, dtype=jnp.int32)[None, :, None]
     s = jnp.where(row < 2, chirp_slope[0], chirp_slope[1])
     c = jnp.where(row < 2, chirp_curve[0], chirp_curve[1])
-    b0 = jnp.arange(64, dtype=jnp.int32)[:, None, None]
-    b = 64 * jnp.asarray(B1, jnp.int32)[None, None, :] + b0
-    p = (s * b + c * (b * b % N) - (N // 4) * (row % 2)) % N
+    b = 64 * B1[None, None, :] + np.arange(64)[:, None, None]
+    square = jnp.asarray(b * b % N, jnp.int32)
+    p = (s * jnp.asarray(b, jnp.int32) + c * square - (N // 4) * (row % 2)) % N
     phi = jnp.cos(p.astype(F32) * (2 * math.pi / N))
     lane = jnp.arange(128, dtype=jnp.int32)[None, None, :]
     s = jnp.where(lane < 16, chirp_slope[0], chirp_slope[1])
@@ -494,8 +494,9 @@
     right3 = sent(right2[:2], 0, 1, 0)
     left3 = sent(left2[2:4], 0, -1, 0)
     far = jnp.concatenate([right2[4:], left2[4:]])
-    h = work([right2[:4], left2[:4], far], [(1, -1), (1, 1), (0, 2)], h)
+    h = work([right2[:4], left2[:4]], [(1, -1), (1, 1)], h)
     right3, left3, h = lax.optimization_barrier((right3, left3, h))
+    h = work([far], [(0, 2)], h)
     h = work([jnp.concatenate([right3, left3])], [(1, 2)], h)
     out = out_call(h, scale)
     return out.reshape(4096, 2, 128).transpose(1, 0, 2).reshape(2, 4096 * 128)

time: 88.8 us -> 87 us (0.980)
  other arithmetic: 8 us -> 6.97 us
    ppermute x11 -> x12, waiting for transfers between devices: 5.95 us -> 4.89 us  [sent(): return lax.ppermute(v, 'tmpl', route)]
    pallas_call x4 -> x5, Pallas kernels: 22.7 us -> 22.5 us  [inv_call(): pl.pallas_call(inv_kernel, grid_spec=pltpu.PrefetchScalarGridSpec(num_sca...]
    ppermute x11 -> x12, starting transfers between devices: 10.5 us -> 10.7 us  [sent(): return lax.ppermute(v, 'tmpl', route)]
    unnamed x22 -> x26, local copies, waits for them, and re-layouts: 2.99 us -> 2.99 us
  transfers between devices with their start and end apart: 13 -> 14, of which waited for: 6 -> 5; matrix products, arithmetic and copies ran while one was open for 10% -> 9% of each run, Pallas kernels for 28% -> 28%
where the time goes in v5:
time: 87 us; the launch traced here: 86.6 us
  Pallas kernels  42.6 us (49%)
  starting transfers between devices  22.4 us (26%)
  waiting for transfers between devices  10.5 us (12%)
  other arithmetic  6.97 us (8%)
  local copies, waits for them, and re-layouts  3.72 us (4%)
    pallas_call x5, Pallas kernels, inv_call(): pl.pallas_call(inv_kernel, grid_spec=pltpu.PrefetchScalarGridSpec(num_sca...  22.5 us
    ppermute x12, starting transfers between devices, sent(): return lax.ppermute(v, 'tmpl', route)  10.7 us
    pallas_call x1, Pallas kernels, out_call(): pl.pallas_call(out_kernel, grid=(16,), in_specs=[pl.BlockSpec((1, 64, 2,...  9.33 us
    all_to_all x1, starting transfers between devices, local(): lax.all_to_all(sent_out, 'tmpl', split_axis=0, concat_axis=0, tiled=True)  7.74 us
    all_to_all x1, waiting for transfers between devices, local(): lax.all_to_all(sent_out, 'tmpl', split_axis=0, concat_axis=0, tiled=True)  5.59 us
    ppermute x12, waiting for transfers between devices, sent(): return lax.ppermute(v, 'tmpl', route)  4.89 us
    pallas_call x1, Pallas kernels, psd_call(): pl.pallas_call(psd_kernel, grid_spec=pltpu.PrefetchScalarGridSpec(num_sca...  4.72 us
    pallas_call x1, Pallas kernels, fwd_call(): pl.pallas_call(fwd_kernel, grid_spec=pltpu.PrefetchScalarGridSpec(num_sca...  4.49 us
  transfers between devices with their start and end apart: 14, of which 5 were waited for; matrix products, arithmetic and copies ran while one was open for 9% of the time, Pallas kernels for 28%

profile of v5, /device:TPU:1, one launch (start us, length us, event | category | flops | bytes accessed | tf_op | source)
XLA Modules:
  0.0 86.6 jit_solution(18368107139517629105)
XLA Ops:
  0.0 4.0 %collective-permute-start = (f32[256,128]{1,0:T(8,128)}, f32[256,128]{1,0:T(8,128)S(1)}, u32[]{:S(2)}, u32[]{:S(2)}) collective-permute-start(f32[256,128]{1,0:T(8,128)} %bitcast.35), channel_id=1, source_target_pairs={{0,16},{16,32},{32,48},{48,64},{64,80},{80,96},{96,112},{1,17},{17... | collective-permute-start | bytes 393224 | tf_op jit(solution)/shard_map/ppermute | solution.py:468
  4.1 0.0 copy-start.6
  4.1 0.9 %copy-done.6 = s32[8,4096]{1,0:T(8,128)S(1)} copy-done((s32[8,4096]{1,0:T(8,128)S(1)}, s32[8,4096]{1,0:T(8,128)}, u32[]{:S(2)}) %copy-start.6) | copy-done | bytes 131096
  5.0 0.8 copy-done.7
  5.7 4.7 %shard_map.154.extra = f32[16,16,128]{2,1,0:T(8,128)S(1)} custom-call(s32[1]{0:T(128)} %bitcast.me, s32[8,4096]{1,0:T(8,128)S(1)} %copy-done.6, f32[64,128]{1,0:T(8,128)S(1)} %bitcast.28), custom_call_target="tpu_custom_call" | custom-call | tf_op jit(solution)/shard_map/pallas_call | solution.py:147
  10.5 0.0 copy-start.5
  10.5 0.6 copy-done.5
  11.1 0.0 copy-start.10
  11.1 0.0 collective-permute-done.tail
  11.2 0.0 copy-start.8
  11.2 0.6 copy-done.8
  11.8 4.5 %shard_map.155 = f32[16,80,128]{2,1,0:T(8,128)} custom-call(s32[1]{0:T(128)} %bitcast.me, f32[256,128]{1,0:T(8,128)} %copy-done.8, f32[256,128]{1,0:T(8,128)} %bitcast.36, bf16[2,1024,512]{2,1,0:T(8,128)(2,1)} %constant.125.clone.l1, f32[2,512,128]{2,1,0:T(8,128)} %constant.126.clone.tw1, bf16[768,256]{1,0:T(8,128)(2,1)} %constant.127.clone.m2, ...), custom_call_target="tpu_custom_call" | custom-call | tf_op jit(solution)/shard_map/pallas_call | solution.py:192
  16.3 0.0 copy-start.3
  16.3 0.0 copy-start.4
  16.3 7.7 %all-to-all-start = ((f32[16,80,128]{2,1,0:T(8,128)}), f32[16,80,128]{2,1,0:T(8,128)S(1)}, u32[]{:S(2)}, u32[]{:S(2)}) async-start(f32[16,80,128]{2,1,0:T(8,128)} %shard_map.155), calls=%async_computation | async-start | bytes 1310720 | tf_op jit(solution)/shard_map/all_to_all | solution.py:475
  24.1 0.0 copy-done.11
  24.1 0.0 copy-done.12
  24.1 0.7 fusion.15
  24.8 1.2 %compare_select_fusion.3 = s32[128]{0:T(128)S(1)} fusion(s32[]{:T(128)} %bitcast.4, s32[]{:T(128)} %bitcast.3), kind=kLoop, calls=%fused_computation.38 | loop fusion | flops 256 | bytes 520 | tf_op jit(solution)/shard_map/jit(_where)/select_n | solution.py:453
  26.0 1.2 %fusion.9 = s32[128]{0:T(128)S(1)} fusion(s32[]{:T(128)} %bitcast.6, s32[]{:T(128)} %bitcast.5), kind=kLoop, calls=%fused_computation.43 | loop fusion | flops 384 | bytes 520 | tf_op jit(solution)/shard_map/mul | solution.py:457
  27.1 0.1 add_select_fusion.2
  27.2 1.2 %compare_select_fusion.5 = s32[4]{0:T(128)S(1)} fusion(s32[]{:T(128)} %bitcast.4, s32[]{:T(128)} %bitcast.3), kind=kLoop, calls=%fused_computation.40 | loop fusion | flops 8 | bytes 24 | tf_op jit(solution)/shard_map/jit(_where)/select_n | solution.py:446
  28.4 1.2 %compare_select_fusion.4 = s32[4]{0:T(128)S(1)} fusion(s32[]{:T(128)} %bitcast.6, s32[]{:T(128)} %bitcast.5), kind=kLoop, calls=%fused_computation.39 | loop fusion | flops 8 | bytes 24 | tf_op jit(solution)/shard_map/jit(_where)/select_n | solution.py:447
  29.6 0.0 copy-done.9
  29.6 0.0 copy-done.10
  29.6 1.1 %fusion.7.phi = f32[8,8,4,128]{3,2,1,0:T(4,128)S(1)} fusion(s32[4]{0:T(128)S(1)} %fusion.10, s32[8,8,128]{2,1,0:T(8,128)S(1)} %copy-done.9, s32[4]{0:T(128)S(1)} %compare_select_fusion.4, s32[8,8,128]{2,1,0:T(8,128)S(1)} %copy-done.10, s32[4]{0:T(128)S(1)} %compare_select_fusion.5), kind=kLoop, calls=%fused_computation.26 | loop fusion | flops 557056 | bytes 196656 | tf_op jit(solution)/shard_map/cos | solution.py:451
  30.7 0.7 fusion.3.psi
  31.4 5.6 %all-to-all-done = f32[16,80,128]{2,1,0:T(8,128)S(1)} async-done(((f32[16,80,128]{2,1,0:T(8,128)}), f32[16,80,128]{2,1,0:T(8,128)S(1)}, u32[]{:S(2)}, u32[]{:S(2)}) %all-to-all-start) | async-done | bytes 655392 | tf_op jit(solution)/shard_map/all_to_all | solution.py:475
  37.0 1.6 %shard_map.156 = (f32[4,96,128]{2,1,0:T(8,128)S(1)}, f32[8,128]{1,0:T(8,128)S(1)}) custom-call(f32[1280,128]{1,0:T(8,128)S(1)} %bitcast.25), custom_call_target="tpu_custom_call" | custom-call | tf_op jit(solution)/shard_map/pallas_call | solution.py:262
  38.6 1.0 %collective-permute-start.4 = (f32[1,4,96,128]{3,2,1,0:T(8,128)S(1)}, f32[1,4,96,128]{3,2,1,0:T(8,128)S(1)}, u32[]{:S(2)}, u32[]{:S(2)}) collective-permute-start(f32[1,4,96,128]{3,2,1,0:T(8,128)S(1)} %bitcast.26), channel_id=1, source_target_pairs={{0,1},{1,0},{2,3},{3,2},{4,5},{5,4},{6,7},{7,6},{8,9},{9,8},{10,11... | collective-permute-start | bytes 589832 | tf_op jit(solution)/shard_map/ppermute | solution.py:441
  39.6 0.1 collective-permute-start.3
  39.7 1.3 %collective-permute-start.2 = (f32[4,96,128]{2,1,0:T(8,128)S(1)}, f32[4,96,128]{2,1,0:T(8,128)S(1)}, u32[]{:S(2)}, u32[]{:S(2)}) collective-permute-start(f32[4,96,128]{2,1,0:T(8,128)S(1)} %get-tuple-element.27), channel_id=1, source_target_pairs={{0,2},{1,3},{2,4},{3,5},{4,6},{5,7},{6,0},{7,1},{8,10},{9,11},{10,... | collective-permute-start | bytes 589832 | tf_op jit(solution)/shard_map/ppermute | solution.py:441
  41.1 0.3 collective-permute-start.1
  41.4 0.0 collective-permute-done.4
  41.4 0.0 copy-done
  41.4 0.0 copy-done.1
  41.4 0.0 copy-done.2
  41.4 2.7 %shard_map.157.rest_0_ = f32[16,64,2,8,256]{4,3,2,1,0:T(8,128)S(1)} custom-call(s32[1]{0:T(128)} %bitcast.me, f32[1,8,96,128]{3,2,1,0:T(8,128)S(1)} %pad_maximum_fusion.3.w, f32[8,8,4,128]{3,2,1,0:T(4,128)S(1)} %fusion.7.phi, f32[8,48,128]{2,1,0:T(8,128)S(1)} %fusion.3.psi, f32[2,128,128]{2,1,0:T(8,128)S(1)} %copy-done.3, f32[64,2,128]{2,1,0:T(2,128)S(1)} %copy-done.4, ...), custom_call_target="tpu_custom_call" | custom-call | flops 1500000000 | bytes 3000000 | tf_op jit(solution)/shard_map/pallas_call | solution.py:335
  44.2 1.9 %collective-permute-done.3 = f32[4,96,128]{2,1,0:T(8,128)S(1)} collective-permute-done((f32[4,96,128]{2,1,0:T(8,128)S(1)}, f32[4,96,128]{2,1,0:T(8,128)S(1)}, u32[]{:S(2)}, u32[]{:S(2)}) %collective-permute-start.3) | collective-permute-done | bytes 196640 | tf_op jit(solution)/shard_map/ppermute | solution.py:441
  46.1 0.6 collective-permute-done.2
  46.7 1.7 %collective-permute-done.1 = f32[4,96,128]{2,1,0:T(8,128)S(1)} collective-permute-done((f32[4,96,128]{2,1,0:T(8,128)S(1)}, f32[4,96,128]{2,1,0:T(8,128)S(1)}, u32[]{:S(2)}, u32[]{:S(2)}) %collective-permute-start.1) | collective-permute-done | bytes 196640 | tf_op jit(solution)/shard_map/ppermute | solution.py:441
  48.4 1.6 %collective-permute-start.7 = (f32[3,4,96,128]{3,2,1,0:T(8,128)S(1)}, f32[3,4,96,128]{3,2,1,0:T(8,128)S(1)}, u32[]{:S(2)}, u32[]{:S(2)}) collective-permute-start(f32[3,4,96,128]{3,2,1,0:T(8,128)S(1)} %pad_maximum_fusion.2), channel_id=1, source_target_pairs={{0,1},{1,0},{2,3},{3,2},{4,5},{5,4},{6,7},{7,6},{8,9},{9,8},{10,11... | collective-permute-start | bytes 1769480 | tf_op jit(solution)/shard_map/ppermute | solution.py:441
  50.1 1.4 %collective-permute-start.6 = (f32[6,96,128]{2,1,0:T(8,128)S(1)}, f32[6,96,128]{2,1,0:T(8,128)S(1)}, u32[]{:S(2)}, u32[]{:S(2)}) collective-permute-start(f32[6,96,128]{2,1,0:T(8,128)S(1)} %get-tuple-element.45), channel_id=1, source_target_pairs={{0,6},{1,7},{2,0},{3,1},{4,2},{5,3},{6,4},{7,5},{8,14},{9,15},{10,... | collective-permute-start | bytes 884744 | tf_op jit(solution)/shard_map/ppermute | solution.py:441
  51.5 0.1 collective-permute-start.5
  51.6 0.0 collective-permute-done.7
  51.7 0.1 pad_maximum_fusion.w
  51.7 8.6 %shard_map.158.rest_0_ = f32[16,64,2,8,256]{4,3,2,1,0:T(8,128)S(1)} custom-call(s32[1]{0:T(128)} %bitcast.me, f32[3,8,96,128]{3,2,1,0:T(8,128)S(1)} %pad_maximum_fusion.w, f32[8,8,4,128]{3,2,1,0:T(4,128)S(1)} %fusion.7.phi, f32[8,48,128]{2,1,0:T(8,128)S(1)} %fusion.3.psi, f32[2,128,128]{2,1,0:T(8,128)S(1)} %copy-done.3, ...), custom_call_target="tpu_custom_call", output_to_operand_aliasing={{}: (9, {})} | custom-call | flops 4499999744 | bytes 9000000 | tf_op jit(solution)/shard_map/pallas_call | solution.py:335
  60.4 0.0 collective-permute-done.6
  60.4 0.6 collective-permute-done.5
  61.1 1.2 %collective-permute-start.10 = (f32[2,4,96,128]{3,2,1,0:T(8,128)S(1)}, f32[2,4,96,128]{3,2,1,0:T(8,128)S(1)}, u32[]{:S(2)}, u32[]{:S(2)}) collective-permute-start(f32[2,4,96,128]{3,2,1,0:T(8,128)S(1)} %pad_maximum_fusion.4), channel_id=1, source_target_pairs={{0,1},{1,0},{2,3},{3,2},{4,5},{5,4},{6,7},{7,6},{8,9},{9,8},{10,11... | collective-permute-start | bytes 1179656 | tf_op jit(solution)/shard_map/ppermute | solution.py:441
  62.3 0.1 collective-permute-start.8
  62.4 2.7 %collective-permute-start.9 = (f32[2,96,128]{2,1,0:T(8,128)S(1)}, f32[2,96,128]{2,1,0:T(8,128)S(1)}, u32[]{:S(2)}, u32[]{:S(2)}) collective-permute-start(f32[2,96,128]{2,1,0:T(8,128)S(1)} %get-tuple-element.44), channel_id=1, source_target_pairs={{0,6},{1,7},{2,0},{3,1},{4,2},{5,3},{6,4},{7,5},{8,14},{9,15},{10,... | collective-permute-start | bytes 294920 | tf_op jit(solution)/shard_map/ppermute | solution.py:441
  65.2 0.7 collective-permute-start.12
  65.8 0.0 collective-permute-done.10
  65.8 0.1 pad_maximum_fusion.1.w
  65.9 5.8 %shard_map.159.rest_0_ = f32[16,64,2,8,256]{4,3,2,1,0:T(8,128)S(1)} custom-call(s32[1]{0:T(128)} %bitcast.me, f32[2,8,96,128]{3,2,1,0:T(8,128)S(1)} %pad_maximum_fusion.1.w, f32[8,8,4,128]{3,2,1,0:T(4,128)S(1)} %fusion.7.phi, f32[8,48,128]{2,1,0:T(8,128)S(1)} %fusion.3.psi, f32[2,128,128]{2,1,0:T(8,128)S(1)} %copy-done.3, ...), custom_call_target="tpu_custom_call", output_to_operand_aliasing={{}: (9, {})} | custom-call | flops 3000000000 | bytes 6000000 | tf_op jit(solution)/shard_map/pallas_call | solution.py:335
  71.6 0.0 collective-permute-done.8
  71.6 0.0 collective-permute-done.9
  71.7 0.1 collective-permute-start.11
  71.8 0.0 collective-permute-done.12
  71.8 2.7 %shard_map.160.rest_0_ = f32[16,64,2,8,256]{4,3,2,1,0:T(8,128)S(1)} custom-call(s32[1]{0:T(128)} %bitcast.me, f32[1,8,96,128]{3,2,1,0:T(8,128)S(1)} %pad_maximum_fusion.6.w, f32[8,8,4,128]{3,2,1,0:T(4,128)S(1)} %fusion.7.phi, f32[8,48,128]{2,1,0:T(8,128)S(1)} %fusion.3.psi, f32[2,128,128]{2,1,0:T(8,128)S(1)} %copy-done.3, ...), custom_call_target="tpu_custom_call", output_to_operand_aliasing={{}: (9, {})} | custom-call | flops 1500000000 | bytes 3000000 | tf_op jit(solution)/shard_map/pallas_call | solution.py:335
  74.5 0.0 collective-permute-done.11
  74.6 2.7 %shard_map.161.h = f32[16,64,2,8,256]{4,3,2,1,0:T(8,128)S(1)} custom-call(s32[1]{0:T(128)} %bitcast.me, f32[1,8,96,128]{3,2,1,0:T(8,128)S(1)} %pad_maximum_fusion.5.w, f32[8,8,4,128]{3,2,1,0:T(4,128)S(1)} %fusion.7.phi, f32[8,48,128]{2,1,0:T(8,128)S(1)} %fusion.3.psi, f32[2,128,128]{2,1,0:T(8,128)S(1)} %copy-done.3, ...), custom_call_target="tpu_custom_call", output_to_operand_aliasing={{}: (9, {})} | custom-call | flops 1500000000 | bytes 3000000 | tf_op jit(solution)/shard_map/pallas_call | solution.py:335
  77.3 9.3 %shard_map.162 = f32[32,256,128]{2,1,0:T(8,128)} custom-call(f32[16,64,2,8,256]{4,3,2,1,0:T(8,128)S(1)} %shard_map.161.h, f32[8,128]{1,0:T(8,128)S(1)} %get-tuple-element.40.sig), custom_call_target="tpu_custom_call" | custom-call | tf_op jit(solution)/shard_map/pallas_call | solution.py:416
  (27 shorter events, 0.3 us)
Async XLA Ops:
  0.0 11.2 %collective-permute-start = (f32[256,128]{1,0:T(8,128)}, f32[256,128]{1,0:T(8,128)S(1)}, u32[]{:S(2)}, u32[]{:S(2)}) collective-permute-start(f32[256,128]{1,0:T(8,128)} %bitcast.35), channel_id=1, source_target_pairs={{0,16},{16,32},{32,48},{48,64},{64,80},{80,96},{96,112},{1,17},{17... | collective-permute-start | bytes 393224 | tf_op jit(solution)/shard_map/ppermute | solution.py:468
  4.1 0.9 %copy-start.6 = (s32[8,4096]{1,0:T(8,128)S(1)}, s32[8,4096]{1,0:T(8,128)}, u32[]{:S(2)}) copy-start(s32[8,4096]{1,0:T(8,128)} %bins_hbm.1) | copy-start | bytes 393220
  5.0 0.8 copy-start.7
  10.5 0.7 copy-start.5
  11.1 13.0 %copy-start.11 = (s32[2]{0:T(128)S(1)}, s32[2]{0:T(128)}, u32[]{:S(2)}) copy-start(s32[2]{0:T(128)} %param.19) | copy-start | bytes 28
  11.1 13.0 %copy-start.12 = (s32[2]{0:T(128)S(1)}, s32[2]{0:T(128)}, u32[]{:S(2)}) copy-start(s32[2]{0:T(128)} %param.20) | copy-start | bytes 28
  11.1 18.5 %copy-start.9 = (s32[8,8,128]{2,1,0:T(8,128)S(1)}, s32[8,8,128]{2,1,0:T(8,128)}, u32[]{:S(2)}) copy-start(s32[8,8,128]{2,1,0:T(8,128)} %constant.141) | copy-start | bytes 98308
  11.1 18.5 %copy-start.10 = (s32[8,8,128]{2,1,0:T(8,128)S(1)}, s32[8,8,128]{2,1,0:T(8,128)}, u32[]{:S(2)}) copy-start(s32[8,8,128]{2,1,0:T(8,128)} %constant.140) | copy-start | bytes 98308
  11.2 0.7 copy-start.8
  16.3 25.1 %copy-start = (f32[8,128,128]{2,1,0:T(8,128)S(1)}, f32[8,128,128]{2,1,0:T(8,128)}, u32[]{:S(2)}) copy-start(f32[8,128,128]{2,1,0:T(8,128)} %constant.133.clone.tw3) | copy-start | bytes 1572868
  16.3 25.1 %copy-start.1 = (bf16[256,768]{1,0:T(8,128)(2,1)S(1)}, bf16[256,768]{1,0:T(8,128)(2,1)}, u32[]{:S(2)}) copy-start(bf16[256,768]{1,0:T(8,128)(2,1)} %constant.130.clone.e2) | copy-start | bytes 1179652
  16.3 25.1 %copy-start.2 = (bf16[288,256]{1,0:T(8,128)(2,1)S(1)}, bf16[288,256]{1,0:T(8,128)(2,1)}, u32[]{:S(2)}) copy-start(bf16[288,256]{1,0:T(8,128)(2,1)} %constant.129.clone.e1) | copy-start | bytes 442372
  16.3 25.1 %copy-start.3 = (f32[2,128,128]{2,1,0:T(8,128)S(1)}, f32[2,128,128]{2,1,0:T(8,128)}, u32[]{:S(2)}) copy-start(f32[2,128,128]{2,1,0:T(8,128)} %constant.131.clone.tw) | copy-start | bytes 393220
  16.3 25.1 %copy-start.4 = (f32[64,2,128]{2,1,0:T(2,128)S(1)}, f32[64,2,128]{2,1,0:T(2,128)}, u32[]{:S(2)}) copy-start(f32[64,2,128]{2,1,0:T(2,128)} %constant.132.clone.twb) | copy-start | bytes 196612
  16.3 20.7 %all-to-all-start = ((f32[16,80,128]{2,1,0:T(8,128)}), f32[16,80,128]{2,1,0:T(8,128)S(1)}, u32[]{:S(2)}, u32[]{:S(2)}) async-start(f32[16,80,128]{2,1,0:T(8,128)} %shard_map.155), calls=%async_computation | async-start | bytes 1310720 | tf_op jit(solution)/shard_map/all_to_all | solution.py:475
  38.6 2.8 %collective-permute-start.4 = (f32[1,4,96,128]{3,2,1,0:T(8,128)S(1)}, f32[1,4,96,128]{3,2,1,0:T(8,128)S(1)}, u32[]{:S(2)}, u32[]{:S(2)}) collective-permute-start(f32[1,4,96,128]{3,2,1,0:T(8,128)S(1)} %bitcast.26), channel_id=1, source_target_pairs={{0,1},{1,0},{2,3},{3,2},{4,5},{5,4},{6,7},{7,6},{8,9},{9,8},{10,11... | collective-permute-start | bytes 589832 | tf_op jit(solution)/shard_map/ppermute | solution.py:441
  39.6 6.5 %collective-permute-start.3 = (f32[4,96,128]{2,1,0:T(8,128)S(1)}, f32[4,96,128]{2,1,0:T(8,128)S(1)}, u32[]{:S(2)}, u32[]{:S(2)}) collective-permute-start(f32[4,96,128]{2,1,0:T(8,128)S(1)} %get-tuple-element.27), channel_id=1, source_target_pairs={{0,6},{1,7},{2,0},{3,1},{4,2},{5,3},{6,4},{7,5},{8,14},{9,15},{10,... | collective-permute-start | bytes 589832 | tf_op jit(solution)/shard_map/ppermute | solution.py:441
  39.7 6.9 %collective-permute-start.2 = (f32[4,96,128]{2,1,0:T(8,128)S(1)}, f32[4,96,128]{2,1,0:T(8,128)S(1)}, u32[]{:S(2)}, u32[]{:S(2)}) collective-permute-start(f32[4,96,128]{2,1,0:T(8,128)S(1)} %get-tuple-element.27), channel_id=1, source_target_pairs={{0,2},{1,3},{2,4},{3,5},{4,6},{5,7},{6,0},{7,1},{8,10},{9,11},{10,... | collective-permute-start | bytes 589832 | tf_op jit(solution)/shard_map/ppermute | solution.py:441
  41.1 7.3 %collective-permute-start.1 = (f32[4,96,128]{2,1,0:T(8,128)S(1)}, f32[4,96,128]{2,1,0:T(8,128)S(1)}, u32[]{:S(2)}, u32[]{:S(2)}) collective-permute-start(f32[4,96,128]{2,1,0:T(8,128)S(1)} %get-tuple-element.27), channel_id=1, source_target_pairs={{0,8},{1,9},{2,10},{3,11},{4,12},{5,13},{6,14},{7,15},{8,0},{9,1},... | collective-permute-start | bytes 589832 | tf_op jit(solution)/shard_map/ppermute | solution.py:441
  48.4 3.2 %collective-permute-start.7 = (f32[3,4,96,128]{3,2,1,0:T(8,128)S(1)}, f32[3,4,96,128]{3,2,1,0:T(8,128)S(1)}, u32[]{:S(2)}, u32[]{:S(2)}) collective-permute-start(f32[3,4,96,128]{3,2,1,0:T(8,128)S(1)} %pad_maximum_fusion.2), channel_id=1, source_target_pairs={{0,1},{1,0},{2,3},{3,2},{4,5},{5,4},{6,7},{7,6},{8,9},{9,8},{10,11... | collective-permute-start | bytes 1769480 | tf_op jit(solution)/shard_map/ppermute | solution.py:441
  50.1 10.3 %collective-permute-start.6 = (f32[6,96,128]{2,1,0:T(8,128)S(1)}, f32[6,96,128]{2,1,0:T(8,128)S(1)}, u32[]{:S(2)}, u32[]{:S(2)}) collective-permute-start(f32[6,96,128]{2,1,0:T(8,128)S(1)} %get-tuple-element.45), channel_id=1, source_target_pairs={{0,6},{1,7},{2,0},{3,1},{4,2},{5,3},{6,4},{7,5},{8,14},{9,15},{10,... | collective-permute-start | bytes 884744 | tf_op jit(solution)/shard_map/ppermute | solution.py:441
  51.5 9.5 %collective-permute-start.5 = (f32[6,96,128]{2,1,0:T(8,128)S(1)}, f32[6,96,128]{2,1,0:T(8,128)S(1)}, u32[]{:S(2)}, u32[]{:S(2)}) collective-permute-start(f32[6,96,128]{2,1,0:T(8,128)S(1)} %get-tuple-element.46), channel_id=1, source_target_pairs={{0,2},{1,3},{2,4},{3,5},{4,6},{5,7},{6,0},{7,1},{8,10},{9,11},{10,... | collective-permute-start | bytes 884744 | tf_op jit(solution)/shard_map/ppermute | solution.py:441
  61.1 4.7 %collective-permute-start.10 = (f32[2,4,96,128]{3,2,1,0:T(8,128)S(1)}, f32[2,4,96,128]{3,2,1,0:T(8,128)S(1)}, u32[]{:S(2)}, u32[]{:S(2)}) collective-permute-start(f32[2,4,96,128]{3,2,1,0:T(8,128)S(1)} %pad_maximum_fusion.4), channel_id=1, source_target_pairs={{0,1},{1,0},{2,3},{3,2},{4,5},{5,4},{6,7},{7,6},{8,9},{9,8},{10,11... | collective-permute-start | bytes 1179656 | tf_op jit(solution)/shard_map/ppermute | solution.py:441
  62.3 9.3 %collective-permute-start.8 = (f32[2,96,128]{2,1,0:T(8,128)S(1)}, f32[2,96,128]{2,1,0:T(8,128)S(1)}, u32[]{:S(2)}, u32[]{:S(2)}) collective-permute-start(f32[2,96,128]{2,1,0:T(8,128)S(1)} %get-tuple-element.42), channel_id=1, source_target_pairs={{0,2},{1,3},{2,4},{3,5},{4,6},{5,7},{6,0},{7,1},{8,10},{9,11},{10,... | collective-permute-start | bytes 294920 | tf_op jit(solution)/shard_map/ppermute | solution.py:441
  62.4 9.2 %collective-permute-start.9 = (f32[2,96,128]{2,1,0:T(8,128)S(1)}, f32[2,96,128]{2,1,0:T(8,128)S(1)}, u32[]{:S(2)}, u32[]{:S(2)}) collective-permute-start(f32[2,96,128]{2,1,0:T(8,128)S(1)} %get-tuple-element.44), channel_id=1, source_target_pairs={{0,6},{1,7},{2,0},{3,1},{4,2},{5,3},{6,4},{7,5},{8,14},{9,15},{10,... | collective-permute-start | bytes 294920 | tf_op jit(solution)/shard_map/ppermute | solution.py:441
  65.2 6.6 %collective-permute-start.12 = (f32[1,4,96,128]{3,2,1,0:T(8,128)S(1)}, f32[1,4,96,128]{3,2,1,0:T(8,128)S(1)}, u32[]{:S(2)}, u32[]{:S(2)}) collective-permute-start(f32[1,4,96,128]{3,2,1,0:T(8,128)S(1)} %maximum_bitcast_fusion.1), channel_id=1, source_target_pairs={{0,1},{1,0},{2,3},{3,2},{4,5},{5,4},{6,7},{7,6},{8,9},{9,8},{10,11... | collective-permute-start | bytes 589832 | tf_op jit(solution)/shard_map/ppermute | solution.py:441
  71.7 2.9 %collective-permute-start.11 = (f32[1,4,96,128]{3,2,1,0:T(8,128)S(1)}, f32[1,4,96,128]{3,2,1,0:T(8,128)S(1)}, u32[]{:S(2)}, u32[]{:S(2)}) collective-permute-start(f32[1,4,96,128]{3,2,1,0:T(8,128)S(1)} %maximum_bitcast_fusion), channel_id=1, source_target_pairs={{0,1},{1,0},{2,3},{3,2},{4,5},{5,4},{6,7},{7,6},{8,9},{9,8},{10,11... | collective-permute-start | bytes 589832 | tf_op jit(solution)/shard_map/ppermute | solution.py:441

commit v6 on v5

--- a/solution.py
+++ b/solution.py
@@ -160,7 +160,7 @@
             ],
         ),
         out_shape=jax.ShapeDtypeStruct((16, 16, 128), F32),
-        compiler_params=pltpu.CompilerParams(vmem_limit_bytes=16 << 20),
+        compiler_params=pltpu.CompilerParams(vmem_limit_bytes=60 << 20),
     )(me, bins, vals)
 
 

time: 87 us -> 86.2 us (level)
  local copies, waits for them, and re-layouts: 3.72 us -> 1.44 us
  Pallas kernels: 42.6 us -> 43.9 us
    unnamed x26 -> x20, local copies, waits for them, and re-layouts: 2.99 us -> 0.69 us
    pallas_call x1, Pallas kernels: 4.72 us -> 6.01 us  [psd_call(): pl.pallas_call(psd_kernel, grid_spec=pltpu.PrefetchScalarGridSpec(num_sca...]
  transfers between devices with their start and end apart: 14 -> 14, of which waited for: 5 -> 5; matrix products, arithmetic and copies ran while one was open for 9% -> 9% of each run, Pallas kernels for 28% -> 30%
where the time goes in v6:
time: 86.2 us; the launch traced here: 85.8 us
  Pallas kernels  43.9 us (51%)
  starting transfers between devices  22.6 us (26%)
  waiting for transfers between devices  10.2 us (12%)
  other arithmetic  7.24 us (8%)
  local copies, waits for them, and re-layouts  1.44 us (2%)
    pallas_call x5, Pallas kernels, inv_call(): pl.pallas_call(inv_kernel, grid_spec=pltpu.PrefetchScalarGridSpec(num_sca...  22.5 us
    ppermute x12, starting transfers between devices, sent(): return lax.ppermute(v, 'tmpl', route)  10.8 us
    pallas_call x1, Pallas kernels, out_call(): pl.pallas_call(out_kernel, grid=(16,), in_specs=[pl.BlockSpec((1, 64, 2,...  9.33 us
    all_to_all x1, starting transfers between devices, local(): lax.all_to_all(sent_out, 'tmpl', split_axis=0, concat_axis=0, tiled=True)  7.76 us
    pallas_call x1, Pallas kernels, psd_call(): pl.pallas_call(psd_kernel, grid_spec=pltpu.PrefetchScalarGridSpec(num_sca...  6.01 us
    all_to_all x1, waiting for transfers between devices, local(): lax.all_to_all(sent_out, 'tmpl', split_axis=0, concat_axis=0, tiled=True)  5.31 us
    ppermute x12, waiting for transfers between devices, sent(): return lax.ppermute(v, 'tmpl', route)  4.89 us
    pallas_call x1, Pallas kernels, fwd_call(): pl.pallas_call(fwd_kernel, grid_spec=pltpu.PrefetchScalarGridSpec(num_sca...  4.48 us
  transfers between devices with their start and end apart: 14, of which 5 were waited for; matrix products, arithmetic and copies ran while one was open for 9% of the time, Pallas kernels for 30%

profile of v6, /device:TPU:1, one launch (start us, length us, event | category | flops | bytes accessed | tf_op | source)
XLA Modules:
  0.0 85.8 jit_solution(1697298652305678274)
XLA Ops:
  0.0 4.0 %collective-permute-start = (f32[256,128]{1,0:T(8,128)}, f32[256,128]{1,0:T(8,128)S(1)}, u32[]{:S(2)}, u32[]{:S(2)}) collective-permute-start(f32[256,128]{1,0:T(8,128)} %bitcast.34), channel_id=1, source_target_pairs={{0,16},{16,32},{32,48},{48,64},{64,80},{80,96},{96,112},{1,17},{17... | collective-permute-start | bytes 393224 | tf_op jit(solution)/shard_map/ppermute | solution.py:468
  4.1 6.0 %shard_map.154.extra = f32[16,16,128]{2,1,0:T(8,128)} custom-call(s32[1]{0:T(128)} %bitcast.me, s32[8,4096]{1,0:T(8,128)} %bins_hbm.1, f32[64,128]{1,0:T(8,128)} %bitcast.36), custom_call_target="tpu_custom_call" | custom-call | tf_op jit(solution)/shard_map/pallas_call | solution.py:147
  10.1 0.0 copy-start.8
  10.1 0.0 copy-start.9
  10.1 0.0 copy-start.6
  10.1 0.0 copy-start.7
  10.2 0.0 collective-permute-done.tail
  10.2 0.0 copy-start.5
  10.2 0.6 copy-done.5
  10.8 4.5 %shard_map.155 = f32[16,80,128]{2,1,0:T(8,128)} custom-call(s32[1]{0:T(128)} %bitcast.me, f32[256,128]{1,0:T(8,128)} %copy-done.5, f32[256,128]{1,0:T(8,128)} %bitcast.35, bf16[2,1024,512]{2,1,0:T(8,128)(2,1)} %constant.125.clone.l1, f32[2,512,128]{2,1,0:T(8,128)} %constant.126.clone.tw1, bf16[768,256]{1,0:T(8,128)(2,1)} %constant.127.clone.m2, ...), custom_call_target="tpu_custom_call" | custom-call | tf_op jit(solution)/shard_map/pallas_call | solution.py:192
  15.3 0.0 copy-start.3
  15.3 0.0 copy-start.4
  15.3 7.8 %all-to-all-start = ((f32[16,80,128]{2,1,0:T(8,128)}), f32[16,80,128]{2,1,0:T(8,128)S(1)}, u32[]{:S(2)}, u32[]{:S(2)}) async-start(f32[16,80,128]{2,1,0:T(8,128)} %shard_map.155), calls=%async_computation | async-start | bytes 1310720 | tf_op jit(solution)/shard_map/all_to_all | solution.py:475
  23.1 0.0 copy-done.8
  23.1 0.0 copy-done.9
  23.1 0.7 fusion.15
  23.8 1.2 %compare_select_fusion.3 = s32[128]{0:T(128)S(1)} fusion(s32[]{:T(128)} %bitcast.4, s32[]{:T(128)} %bitcast.3), kind=kLoop, calls=%fused_computation.38 | loop fusion | flops 256 | bytes 520 | tf_op jit(solution)/shard_map/jit(_where)/select_n | solution.py:453
  25.0 1.3 %fusion.9 = s32[128]{0:T(128)S(1)} fusion(s32[]{:T(128)} %bitcast.6, s32[]{:T(128)} %bitcast.5), kind=kLoop, calls=%fused_computation.43 | loop fusion | flops 384 | bytes 520 | tf_op jit(solution)/shard_map/mul | solution.py:457
  26.3 0.1 add_select_fusion.2
  26.4 1.2 %compare_select_fusion.5 = s32[4]{0:T(128)S(1)} fusion(s32[]{:T(128)} %bitcast.4, s32[]{:T(128)} %bitcast.3), kind=kLoop, calls=%fused_computation.40 | loop fusion | flops 8 | bytes 24 | tf_op jit(solution)/shard_map/jit(_where)/select_n | solution.py:446
  27.6 1.3 %compare_select_fusion.4 = s32[4]{0:T(128)S(1)} fusion(s32[]{:T(128)} %bitcast.6, s32[]{:T(128)} %bitcast.5), kind=kLoop, calls=%fused_computation.39 | loop fusion | flops 8 | bytes 24 | tf_op jit(solution)/shard_map/jit(_where)/select_n | solution.py:447
  28.9 0.0 copy-done.6
  28.9 0.0 copy-done.7
  28.9 1.1 %fusion.7.phi = f32[8,8,4,128]{3,2,1,0:T(4,128)S(1)} fusion(s32[4]{0:T(128)S(1)} %fusion.10, s32[8,8,128]{2,1,0:T(8,128)S(1)} %copy-done.6, s32[4]{0:T(128)S(1)} %compare_select_fusion.4, s32[8,8,128]{2,1,0:T(8,128)S(1)} %copy-done.7, s32[4]{0:T(128)S(1)} %compare_select_fusion.5), kind=kLoop, calls=%fused_computation.26 | loop fusion | flops 557056 | bytes 196656 | tf_op jit(solution)/shard_map/cos | solution.py:451
  30.0 0.7 fusion.3.psi
  30.7 5.3 %all-to-all-done = f32[16,80,128]{2,1,0:T(8,128)S(1)} async-done(((f32[16,80,128]{2,1,0:T(8,128)}), f32[16,80,128]{2,1,0:T(8,128)S(1)}, u32[]{:S(2)}, u32[]{:S(2)}) %all-to-all-start) | async-done | bytes 655392 | tf_op jit(solution)/shard_map/all_to_all | solution.py:475
  36.0 1.6 %shard_map.156 = (f32[4,96,128]{2,1,0:T(8,128)S(1)}, f32[8,128]{1,0:T(8,128)S(1)}) custom-call(f32[1280,128]{1,0:T(8,128)S(1)} %bitcast.25), custom_call_target="tpu_custom_call" | custom-call | tf_op jit(solution)/shard_map/pallas_call | solution.py:262
  37.6 1.0 %collective-permute-start.4 = (f32[1,4,96,128]{3,2,1,0:T(8,128)S(1)}, f32[1,4,96,128]{3,2,1,0:T(8,128)S(1)}, u32[]{:S(2)}, u32[]{:S(2)}) collective-permute-start(f32[1,4,96,128]{3,2,1,0:T(8,128)S(1)} %bitcast.26), channel_id=1, source_target_pairs={{0,1},{1,0},{2,3},{3,2},{4,5},{5,4},{6,7},{7,6},{8,9},{9,8},{10,11... | collective-permute-start | bytes 589832 | tf_op jit(solution)/shard_map/ppermute | solution.py:441
  38.6 0.1 collective-permute-start.3
  38.7 1.3 %collective-permute-start.2 = (f32[4,96,128]{2,1,0:T(8,128)S(1)}, f32[4,96,128]{2,1,0:T(8,128)S(1)}, u32[]{:S(2)}, u32[]{:S(2)}) collective-permute-start(f32[4,96,128]{2,1,0:T(8,128)S(1)} %get-tuple-element.27), channel_id=1, source_target_pairs={{0,2},{1,3},{2,4},{3,5},{4,6},{5,7},{6,0},{7,1},{8,10},{9,11},{10,... | collective-permute-start | bytes 589832 | tf_op jit(solution)/shard_map/ppermute | solution.py:441
  40.1 0.3 collective-permute-start.1
  40.4 0.0 collective-permute-done.4
  40.4 0.0 copy-done
  40.4 0.0 copy-done.1
  40.4 0.0 copy-done.2
  40.4 0.0 copy-done.3
  40.4 0.0 copy-done.4
  40.5 2.7 %shard_map.157.rest_0_ = f32[16,64,2,8,256]{4,3,2,1,0:T(8,128)S(1)} custom-call(s32[1]{0:T(128)} %bitcast.me, f32[1,8,96,128]{3,2,1,0:T(8,128)S(1)} %pad_maximum_fusion.3.w, f32[8,8,4,128]{3,2,1,0:T(4,128)S(1)} %fusion.7.phi, f32[8,48,128]{2,1,0:T(8,128)S(1)} %fusion.3.psi, f32[2,128,128]{2,1,0:T(8,128)S(1)} %copy-done.3, f32[64,2,128]{2,1,0:T(2,128)S(1)} %copy-done.4, ...), custom_call_target="tpu_custom_call" | custom-call | flops 1500000000 | bytes 3000000 | tf_op jit(solution)/shard_map/pallas_call | solution.py:335
  43.2 1.9 %collective-permute-done.3 = f32[4,96,128]{2,1,0:T(8,128)S(1)} collective-permute-done((f32[4,96,128]{2,1,0:T(8,128)S(1)}, f32[4,96,128]{2,1,0:T(8,128)S(1)}, u32[]{:S(2)}, u32[]{:S(2)}) %collective-permute-start.3) | collective-permute-done | bytes 196640 | tf_op jit(solution)/shard_map/ppermute | solution.py:441
  45.1 0.6 collective-permute-done.2
  45.7 1.7 %collective-permute-done.1 = f32[4,96,128]{2,1,0:T(8,128)S(1)} collective-permute-done((f32[4,96,128]{2,1,0:T(8,128)S(1)}, f32[4,96,128]{2,1,0:T(8,128)S(1)}, u32[]{:S(2)}, u32[]{:S(2)}) %collective-permute-start.1) | collective-permute-done | bytes 196640 | tf_op jit(solution)/shard_map/ppermute | solution.py:441
  47.5 1.6 %collective-permute-start.7 = (f32[3,4,96,128]{3,2,1,0:T(8,128)S(1)}, f32[3,4,96,128]{3,2,1,0:T(8,128)S(1)}, u32[]{:S(2)}, u32[]{:S(2)}) collective-permute-start(f32[3,4,96,128]{3,2,1,0:T(8,128)S(1)} %pad_maximum_fusion.2), channel_id=1, source_target_pairs={{0,1},{1,0},{2,3},{3,2},{4,5},{5,4},{6,7},{7,6},{8,9},{9,8},{10,11... | collective-permute-start | bytes 1769480 | tf_op jit(solution)/shard_map/ppermute | solution.py:441
  49.1 1.4 %collective-permute-start.6 = (f32[6,96,128]{2,1,0:T(8,128)S(1)}, f32[6,96,128]{2,1,0:T(8,128)S(1)}, u32[]{:S(2)}, u32[]{:S(2)}) collective-permute-start(f32[6,96,128]{2,1,0:T(8,128)S(1)} %get-tuple-element.45), channel_id=1, source_target_pairs={{0,6},{1,7},{2,0},{3,1},{4,2},{5,3},{6,4},{7,5},{8,14},{9,15},{10,... | collective-permute-start | bytes 884744 | tf_op jit(solution)/shard_map/ppermute | solution.py:441
  50.5 0.1 collective-permute-start.5
  50.6 0.0 collective-permute-done.7
  50.7 0.1 pad_maximum_fusion.w
  50.7 8.6 %shard_map.158.rest_0_ = f32[16,64,2,8,256]{4,3,2,1,0:T(8,128)S(1)} custom-call(s32[1]{0:T(128)} %bitcast.me, f32[3,8,96,128]{3,2,1,0:T(8,128)S(1)} %pad_maximum_fusion.w, f32[8,8,4,128]{3,2,1,0:T(4,128)S(1)} %fusion.7.phi, f32[8,48,128]{2,1,0:T(8,128)S(1)} %fusion.3.psi, f32[2,128,128]{2,1,0:T(8,128)S(1)} %copy-done.3, ...), custom_call_target="tpu_custom_call", output_to_operand_aliasing={{}: (9, {})} | custom-call | flops 4499999744 | bytes 9000000 | tf_op jit(solution)/shard_map/pallas_call | solution.py:335
  59.4 0.0 collective-permute-done.6
  59.4 0.6 collective-permute-done.5
  60.1 1.4 %collective-permute-start.10 = (f32[2,4,96,128]{3,2,1,0:T(8,128)S(1)}, f32[2,4,96,128]{3,2,1,0:T(8,128)S(1)}, u32[]{:S(2)}, u32[]{:S(2)}) collective-permute-start(f32[2,4,96,128]{3,2,1,0:T(8,128)S(1)} %pad_maximum_fusion.4), channel_id=1, source_target_pairs={{0,1},{1,0},{2,3},{3,2},{4,5},{5,4},{6,7},{7,6},{8,9},{9,8},{10,11... | collective-permute-start | bytes 1179656 | tf_op jit(solution)/shard_map/ppermute | solution.py:441
  61.5 0.1 collective-permute-start.8
  61.6 2.7 %collective-permute-start.9 = (f32[2,96,128]{2,1,0:T(8,128)S(1)}, f32[2,96,128]{2,1,0:T(8,128)S(1)}, u32[]{:S(2)}, u32[]{:S(2)}) collective-permute-start(f32[2,96,128]{2,1,0:T(8,128)S(1)} %get-tuple-element.44), channel_id=1, source_target_pairs={{0,6},{1,7},{2,0},{3,1},{4,2},{5,3},{6,4},{7,5},{8,14},{9,15},{10,... | collective-permute-start | bytes 294920 | tf_op jit(solution)/shard_map/ppermute | solution.py:441
  64.3 0.7 collective-permute-start.12
  65.0 0.0 collective-permute-done.10
  65.0 0.1 pad_maximum_fusion.1.w
  65.1 5.8 %shard_map.159.rest_0_ = f32[16,64,2,8,256]{4,3,2,1,0:T(8,128)S(1)} custom-call(s32[1]{0:T(128)} %bitcast.me, f32[2,8,96,128]{3,2,1,0:T(8,128)S(1)} %pad_maximum_fusion.1.w, f32[8,8,4,128]{3,2,1,0:T(4,128)S(1)} %fusion.7.phi, f32[8,48,128]{2,1,0:T(8,128)S(1)} %fusion.3.psi, f32[2,128,128]{2,1,0:T(8,128)S(1)} %copy-done.3, ...), custom_call_target="tpu_custom_call", output_to_operand_aliasing={{}: (9, {})} | custom-call | flops 3000000000 | bytes 6000000 | tf_op jit(solution)/shard_map/pallas_call | solution.py:335
  70.8 0.0 collective-permute-done.8
  70.8 0.0 collective-permute-done.9
  70.9 0.1 collective-permute-start.11
  71.0 0.0 collective-permute-done.12
  71.0 2.7 %shard_map.160.rest_0_ = f32[16,64,2,8,256]{4,3,2,1,0:T(8,128)S(1)} custom-call(s32[1]{0:T(128)} %bitcast.me, f32[1,8,96,128]{3,2,1,0:T(8,128)S(1)} %pad_maximum_fusion.6.w, f32[8,8,4,128]{3,2,1,0:T(4,128)S(1)} %fusion.7.phi, f32[8,48,128]{2,1,0:T(8,128)S(1)} %fusion.3.psi, f32[2,128,128]{2,1,0:T(8,128)S(1)} %copy-done.3, ...), custom_call_target="tpu_custom_call", output_to_operand_aliasing={{}: (9, {})} | custom-call | flops 1500000000 | bytes 3000000 | tf_op jit(solution)/shard_map/pallas_call | solution.py:335
  73.7 0.0 collective-permute-done.11
  73.8 2.7 %shard_map.161.h = f32[16,64,2,8,256]{4,3,2,1,0:T(8,128)S(1)} custom-call(s32[1]{0:T(128)} %bitcast.me, f32[1,8,96,128]{3,2,1,0:T(8,128)S(1)} %pad_maximum_fusion.5.w, f32[8,8,4,128]{3,2,1,0:T(4,128)S(1)} %fusion.7.phi, f32[8,48,128]{2,1,0:T(8,128)S(1)} %fusion.3.psi, f32[2,128,128]{2,1,0:T(8,128)S(1)} %copy-done.3, ...), custom_call_target="tpu_custom_call", output_to_operand_aliasing={{}: (9, {})} | custom-call | flops 1500000000 | bytes 3000000 | tf_op jit(solution)/shard_map/pallas_call | solution.py:335
  76.5 9.3 %shard_map.162 = f32[32,256,128]{2,1,0:T(8,128)} custom-call(f32[16,64,2,8,256]{4,3,2,1,0:T(8,128)S(1)} %shard_map.161.h, f32[8,128]{1,0:T(8,128)S(1)} %get-tuple-element.40.sig), custom_call_target="tpu_custom_call" | custom-call | tf_op jit(solution)/shard_map/pallas_call | solution.py:416
  (21 shorter events, 0.3 us)
Async XLA Ops:
  0.0 10.2 %collective-permute-start = (f32[256,128]{1,0:T(8,128)}, f32[256,128]{1,0:T(8,128)S(1)}, u32[]{:S(2)}, u32[]{:S(2)}) collective-permute-start(f32[256,128]{1,0:T(8,128)} %bitcast.34), channel_id=1, source_target_pairs={{0,16},{16,32},{32,48},{48,64},{64,80},{80,96},{96,112},{1,17},{17... | collective-permute-start | bytes 393224 | tf_op jit(solution)/shard_map/ppermute | solution.py:468
  10.1 13.0 %copy-start.8 = (s32[2]{0:T(128)S(1)}, s32[2]{0:T(128)}, u32[]{:S(2)}) copy-start(s32[2]{0:T(128)} %param.19) | copy-start | bytes 28
  10.1 13.0 %copy-start.9 = (s32[2]{0:T(128)S(1)}, s32[2]{0:T(128)}, u32[]{:S(2)}) copy-start(s32[2]{0:T(128)} %param.20) | copy-start | bytes 28
  10.1 18.8 %copy-start.6 = (s32[8,8,128]{2,1,0:T(8,128)S(1)}, s32[8,8,128]{2,1,0:T(8,128)}, u32[]{:S(2)}) copy-start(s32[8,8,128]{2,1,0:T(8,128)} %constant.141) | copy-start | bytes 98308
  10.1 18.8 %copy-start.7 = (s32[8,8,128]{2,1,0:T(8,128)S(1)}, s32[8,8,128]{2,1,0:T(8,128)}, u32[]{:S(2)}) copy-start(s32[8,8,128]{2,1,0:T(8,128)} %constant.140) | copy-start | bytes 98308
  10.2 0.7 copy-start.5
  15.3 25.1 %copy-start = (f32[8,128,128]{2,1,0:T(8,128)S(1)}, f32[8,128,128]{2,1,0:T(8,128)}, u32[]{:S(2)}) copy-start(f32[8,128,128]{2,1,0:T(8,128)} %constant.133.clone.tw3) | copy-start | bytes 1572868
  15.3 25.1 %copy-start.1 = (bf16[256,768]{1,0:T(8,128)(2,1)S(1)}, bf16[256,768]{1,0:T(8,128)(2,1)}, u32[]{:S(2)}) copy-start(bf16[256,768]{1,0:T(8,128)(2,1)} %constant.130.clone.e2) | copy-start | bytes 1179652
  15.3 25.1 %copy-start.2 = (bf16[288,256]{1,0:T(8,128)(2,1)S(1)}, bf16[288,256]{1,0:T(8,128)(2,1)}, u32[]{:S(2)}) copy-start(bf16[288,256]{1,0:T(8,128)(2,1)} %constant.129.clone.e1) | copy-start | bytes 442372
  15.3 25.1 %copy-start.3 = (f32[2,128,128]{2,1,0:T(8,128)S(1)}, f32[2,128,128]{2,1,0:T(8,128)}, u32[]{:S(2)}) copy-start(f32[2,128,128]{2,1,0:T(8,128)} %constant.131.clone.tw) | copy-start | bytes 393220
  15.3 25.1 %copy-start.4 = (f32[64,2,128]{2,1,0:T(2,128)S(1)}, f32[64,2,128]{2,1,0:T(2,128)}, u32[]{:S(2)}) copy-start(f32[64,2,128]{2,1,0:T(2,128)} %constant.132.clone.twb) | copy-start | bytes 196612
  15.3 20.7 %all-to-all-start = ((f32[16,80,128]{2,1,0:T(8,128)}), f32[16,80,128]{2,1,0:T(8,128)S(1)}, u32[]{:S(2)}, u32[]{:S(2)}) async-start(f32[16,80,128]{2,1,0:T(8,128)} %shard_map.155), calls=%async_computation | async-start | bytes 1310720 | tf_op jit(solution)/shard_map/all_to_all | solution.py:475
  37.6 2.8 %collective-permute-start.4 = (f32[1,4,96,128]{3,2,1,0:T(8,128)S(1)}, f32[1,4,96,128]{3,2,1,0:T(8,128)S(1)}, u32[]{:S(2)}, u32[]{:S(2)}) collective-permute-start(f32[1,4,96,128]{3,2,1,0:T(8,128)S(1)} %bitcast.26), channel_id=1, source_target_pairs={{0,1},{1,0},{2,3},{3,2},{4,5},{5,4},{6,7},{7,6},{8,9},{9,8},{10,11... | collective-permute-start | bytes 589832 | tf_op jit(solution)/shard_map/ppermute | solution.py:441
  38.6 6.5 %collective-permute-start.3 = (f32[4,96,128]{2,1,0:T(8,128)S(1)}, f32[4,96,128]{2,1,0:T(8,128)S(1)}, u32[]{:S(2)}, u32[]{:S(2)}) collective-permute-start(f32[4,96,128]{2,1,0:T(8,128)S(1)} %get-tuple-element.27), channel_id=1, source_target_pairs={{0,6},{1,7},{2,0},{3,1},{4,2},{5,3},{6,4},{7,5},{8,14},{9,15},{10,... | collective-permute-start | bytes 589832 | tf_op jit(solution)/shard_map/ppermute | solution.py:441
  38.7 6.9 %collective-permute-start.2 = (f32[4,96,128]{2,1,0:T(8,128)S(1)}, f32[4,96,128]{2,1,0:T(8,128)S(1)}, u32[]{:S(2)}, u32[]{:S(2)}) collective-permute-start(f32[4,96,128]{2,1,0:T(8,128)S(1)} %get-tuple-element.27), channel_id=1, source_target_pairs={{0,2},{1,3},{2,4},{3,5},{4,6},{5,7},{6,0},{7,1},{8,10},{9,11},{10,... | collective-permute-start | bytes 589832 | tf_op jit(solution)/shard_map/ppermute | solution.py:441
  40.1 7.3 %collective-permute-start.1 = (f32[4,96,128]{2,1,0:T(8,128)S(1)}, f32[4,96,128]{2,1,0:T(8,128)S(1)}, u32[]{:S(2)}, u32[]{:S(2)}) collective-permute-start(f32[4,96,128]{2,1,0:T(8,128)S(1)} %get-tuple-element.27), channel_id=1, source_target_pairs={{0,8},{1,9},{2,10},{3,11},{4,12},{5,13},{6,14},{7,15},{8,0},{9,1},... | collective-permute-start | bytes 589832 | tf_op jit(solution)/shard_map/ppermute | solution.py:441
  47.5 3.2 %collective-permute-start.7 = (f32[3,4,96,128]{3,2,1,0:T(8,128)S(1)}, f32[3,4,96,128]{3,2,1,0:T(8,128)S(1)}, u32[]{:S(2)}, u32[]{:S(2)}) collective-permute-start(f32[3,4,96,128]{3,2,1,0:T(8,128)S(1)} %pad_maximum_fusion.2), channel_id=1, source_target_pairs={{0,1},{1,0},{2,3},{3,2},{4,5},{5,4},{6,7},{7,6},{8,9},{9,8},{10,11... | collective-permute-start | bytes 1769480 | tf_op jit(solution)/shard_map/ppermute | solution.py:441
  49.1 10.3 %collective-permute-start.6 = (f32[6,96,128]{2,1,0:T(8,128)S(1)}, f32[6,96,128]{2,1,0:T(8,128)S(1)}, u32[]{:S(2)}, u32[]{:S(2)}) collective-permute-start(f32[6,96,128]{2,1,0:T(8,128)S(1)} %get-tuple-element.45), channel_id=1, source_target_pairs={{0,6},{1,7},{2,0},{3,1},{4,2},{5,3},{6,4},{7,5},{8,14},{9,15},{10,... | collective-permute-start | bytes 884744 | tf_op jit(solution)/shard_map/ppermute | solution.py:441
  50.5 9.5 %collective-permute-start.5 = (f32[6,96,128]{2,1,0:T(8,128)S(1)}, f32[6,96,128]{2,1,0:T(8,128)S(1)}, u32[]{:S(2)}, u32[]{:S(2)}) collective-permute-start(f32[6,96,128]{2,1,0:T(8,128)S(1)} %get-tuple-element.46), channel_id=1, source_target_pairs={{0,2},{1,3},{2,4},{3,5},{4,6},{5,7},{6,0},{7,1},{8,10},{9,11},{10,... | collective-permute-start | bytes 884744 | tf_op jit(solution)/shard_map/ppermute | solution.py:441
  60.1 4.9 %collective-permute-start.10 = (f32[2,4,96,128]{3,2,1,0:T(8,128)S(1)}, f32[2,4,96,128]{3,2,1,0:T(8,128)S(1)}, u32[]{:S(2)}, u32[]{:S(2)}) collective-permute-start(f32[2,4,96,128]{3,2,1,0:T(8,128)S(1)} %pad_maximum_fusion.4), channel_id=1, source_target_pairs={{0,1},{1,0},{2,3},{3,2},{4,5},{5,4},{6,7},{7,6},{8,9},{9,8},{10,11... | collective-permute-start | bytes 1179656 | tf_op jit(solution)/shard_map/ppermute | solution.py:441
  61.5 9.3 %collective-permute-start.8 = (f32[2,96,128]{2,1,0:T(8,128)S(1)}, f32[2,96,128]{2,1,0:T(8,128)S(1)}, u32[]{:S(2)}, u32[]{:S(2)}) collective-permute-start(f32[2,96,128]{2,1,0:T(8,128)S(1)} %get-tuple-element.42), channel_id=1, source_target_pairs={{0,2},{1,3},{2,4},{3,5},{4,6},{5,7},{6,0},{7,1},{8,10},{9,11},{10,... | collective-permute-start | bytes 294920 | tf_op jit(solution)/shard_map/ppermute | solution.py:441
  61.6 9.2 %collective-permute-start.9 = (f32[2,96,128]{2,1,0:T(8,128)S(1)}, f32[2,96,128]{2,1,0:T(8,128)S(1)}, u32[]{:S(2)}, u32[]{:S(2)}) collective-permute-start(f32[2,96,128]{2,1,0:T(8,128)S(1)} %get-tuple-element.44), channel_id=1, source_target_pairs={{0,6},{1,7},{2,0},{3,1},{4,2},{5,3},{6,4},{7,5},{8,14},{9,15},{10,... | collective-permute-start | bytes 294920 | tf_op jit(solution)/shard_map/ppermute | solution.py:441
  64.3 6.6 %collective-permute-start.12 = (f32[1,4,96,128]{3,2,1,0:T(8,128)S(1)}, f32[1,4,96,128]{3,2,1,0:T(8,128)S(1)}, u32[]{:S(2)}, u32[]{:S(2)}) collective-permute-start(f32[1,4,96,128]{3,2,1,0:T(8,128)S(1)} %maximum_bitcast_fusion.1), channel_id=1, source_target_pairs={{0,1},{1,0},{2,3},{3,2},{4,5},{5,4},{6,7},{7,6},{8,9},{9,8},{10,11... | collective-permute-start | bytes 589832 | tf_op jit(solution)/shard_map/ppermute | solution.py:441
  70.9 2.9 %collective-permute-start.11 = (f32[1,4,96,128]{3,2,1,0:T(8,128)S(1)}, f32[1,4,96,128]{3,2,1,0:T(8,128)S(1)}, u32[]{:S(2)}, u32[]{:S(2)}) collective-permute-start(f32[1,4,96,128]{3,2,1,0:T(8,128)S(1)} %maximum_bitcast_fusion), channel_id=1, source_target_pairs={{0,1},{1,0},{2,3},{3,2},{4,5},{5,4},{6,7},{7,6},{8,9},{9,8},{10,11... | collective-permute-start | bytes 589832 | tf_op jit(solution)/shard_map/ppermute | solution.py:441

commit v7 on v6

--- a/solution.py
+++ b/solution.py
@@ -391,10 +391,10 @@
 
 def out_kernel(h, sig, out, mid):
     scale = sig[...]
-    for m in range(2):
+    for tile, m in ((0, 0), (0, 1), (1, 0), (1, 1)):
         at = slice(128 * m, 128 * m + 128)
         for lo in range(8):
-            x = [(h[0, 8 * hi + lo, 0, :, at], h[0, 8 * hi + lo, 1, :, at]) for hi in range(8)]
+            x = [(h[tile, 8 * hi + lo, 0, :, at], h[tile, 8 * hi + lo, 1, :, at]) for hi in range(8)]
             ev, od = fft4(x[0::2]), fft4(x[1::2])
             for f in range(4):
                 o = cmul(od[f], f, 8)
@@ -409,18 +409,18 @@
                 v = sub(ev[f], cmul(od[f], f, 8))
                 power = v[0] * v[0] + v[1] * v[1]
                 mag = power * lax.rsqrt(jnp.maximum(power, 1e-37)) * scale
-                out[f2 + 8 * f, pl.ds(m, 8, stride=2), :] = mag
+                out[f2 + 8 * f, pl.ds(16 * tile + m, 8, stride=2), :] = mag
 
 
 def out_call(h, sig):
     return pl.pallas_call(
         out_kernel,
-        grid=(16,),
+        grid=(8,),
         in_specs=[
-            pl.BlockSpec((1, 64, 2, 8, 256), lambda i: (i, 0, 0, 0, 0)),
+            pl.BlockSpec((2, 64, 2, 8, 256), lambda i: (i, 0, 0, 0, 0)),
             pl.BlockSpec((8, 128), lambda i: (0, 0)),
         ],
-        out_specs=pl.BlockSpec((32, 16, 128), lambda i: (0, i, 0)),
+        out_specs=pl.BlockSpec((32, 32, 128), lambda i: (0, i, 0)),
         out_shape=jax.ShapeDtypeStruct((32, 256, 128), F32),
         scratch_shapes=[pltpu.VMEM((8, 8, 2, 8, 128), F32)],
         compiler_params=pltpu.CompilerParams(vmem_limit_bytes=OUT_VMEM),

time: 86.2 us -> 84.2 us (0.977)
  Pallas kernels: 43.9 us -> 42 us
    pallas_call x1, Pallas kernels: 9.33 us -> 7.38 us  [out_call(): pl.pallas_call(out_kernel, grid=(8,), in_specs=[pl.BlockSpec((2, 64, 2, 8...]
  transfers between devices with their start and end apart: 14 -> 14, of which waited for: 5 -> 5; matrix products, arithmetic and copies ran while one was open for 9% -> 9% of each run, Pallas kernels for 30% -> 31%
where the time goes in v7:
time: 84.2 us; the launch traced here: 83.9 us
  Pallas kernels  42 us (50%)
  starting transfers between devices  22.6 us (27%)
  waiting for transfers between devices  10.2 us (12%)
  other arithmetic  7.24 us (9%)
  local copies, waits for them, and re-layouts  1.44 us (2%)
    pallas_call x5, Pallas kernels, inv_call(): pl.pallas_call(inv_kernel, grid_spec=pltpu.PrefetchScalarGridSpec(num_sca...  22.5 us
    ppermute x12, starting transfers between devices, sent(): return lax.ppermute(v, 'tmpl', route)  10.8 us
    all_to_all x1, starting transfers between devices, local(): lax.all_to_all(sent_out, 'tmpl', split_axis=0, concat_axis=0, tiled=True)  7.76 us
    pallas_call x1, Pallas kernels, out_call(): pl.pallas_call(out_kernel, grid=(8,), in_specs=[pl.BlockSpec((2, 64, 2, 8...  7.38 us
    pallas_call x1, Pallas kernels, psd_call(): pl.pallas_call(psd_kernel, grid_spec=pltpu.PrefetchScalarGridSpec(num_sca...  6.01 us
    all_to_all x1, waiting for transfers between devices, local(): lax.all_to_all(sent_out, 'tmpl', split_axis=0, concat_axis=0, tiled=True)  5.31 us
    ppermute x12, waiting for transfers between devices, sent(): return lax.ppermute(v, 'tmpl', route)  4.89 us
    pallas_call x1, Pallas kernels, fwd_call(): pl.pallas_call(fwd_kernel, grid_spec=pltpu.PrefetchScalarGridSpec(num_sca...  4.48 us
  transfers between devices with their start and end apart: 14, of which 5 were waited for; matrix products, arithmetic and copies ran while one was open for 9% of the time, Pallas kernels for 31%

profile of v7, /device:TPU:1, one launch (start us, length us, event | category | flops | bytes accessed | tf_op | source)
XLA Modules:
  0.0 83.9 jit_solution(742418077603571704)
XLA Ops:
  0.0 4.0 %collective-permute-start = (f32[256,128]{1,0:T(8,128)}, f32[256,128]{1,0:T(8,128)S(1)}, u32[]{:S(2)}, u32[]{:S(2)}) collective-permute-start(f32[256,128]{1,0:T(8,128)} %bitcast.34), channel_id=1, source_target_pairs={{0,16},{16,32},{32,48},{48,64},{64,80},{80,96},{96,112},{1,17},{17... | collective-permute-start | bytes 393224 | tf_op jit(solution)/shard_map/ppermute | solution.py:468
  4.1 6.0 %shard_map.154.extra = f32[16,16,128]{2,1,0:T(8,128)} custom-call(s32[1]{0:T(128)} %bitcast.me, s32[8,4096]{1,0:T(8,128)} %bins_hbm.1, f32[64,128]{1,0:T(8,128)} %bitcast.36), custom_call_target="tpu_custom_call" | custom-call | tf_op jit(solution)/shard_map/pallas_call | solution.py:147
  10.1 0.0 copy-start.8
  10.1 0.0 copy-start.9
  10.1 0.0 copy-start.6
  10.1 0.0 copy-start.7
  10.2 0.0 collective-permute-done.tail
  10.2 0.0 copy-start.5
  10.2 0.6 copy-done.5
  10.8 4.5 %shard_map.155 = f32[16,80,128]{2,1,0:T(8,128)} custom-call(s32[1]{0:T(128)} %bitcast.me, f32[256,128]{1,0:T(8,128)} %copy-done.5, f32[256,128]{1,0:T(8,128)} %bitcast.35, bf16[2,1024,512]{2,1,0:T(8,128)(2,1)} %constant.125.clone.l1, f32[2,512,128]{2,1,0:T(8,128)} %constant.126.clone.tw1, bf16[768,256]{1,0:T(8,128)(2,1)} %constant.127.clone.m2, ...), custom_call_target="tpu_custom_call" | custom-call | tf_op jit(solution)/shard_map/pallas_call | solution.py:192
  15.3 0.0 copy-start.3
  15.3 0.0 copy-start.4
  15.3 7.8 %all-to-all-start = ((f32[16,80,128]{2,1,0:T(8,128)}), f32[16,80,128]{2,1,0:T(8,128)S(1)}, u32[]{:S(2)}, u32[]{:S(2)}) async-start(f32[16,80,128]{2,1,0:T(8,128)} %shard_map.155), calls=%async_computation | async-start | bytes 1310720 | tf_op jit(solution)/shard_map/all_to_all | solution.py:475
  23.1 0.0 copy-done.8
  23.1 0.0 copy-done.9
  23.1 0.7 fusion.15
  23.8 1.2 %compare_select_fusion.3 = s32[128]{0:T(128)S(1)} fusion(s32[]{:T(128)} %bitcast.4, s32[]{:T(128)} %bitcast.3), kind=kLoop, calls=%fused_computation.38 | loop fusion | flops 256 | bytes 520 | tf_op jit(solution)/shard_map/jit(_where)/select_n | solution.py:453
  25.0 1.3 %fusion.9 = s32[128]{0:T(128)S(1)} fusion(s32[]{:T(128)} %bitcast.6, s32[]{:T(128)} %bitcast.5), kind=kLoop, calls=%fused_computation.43 | loop fusion | flops 384 | bytes 520 | tf_op jit(solution)/shard_map/mul | solution.py:457
  26.3 0.1 add_select_fusion.2
  26.4 1.2 %compare_select_fusion.5 = s32[4]{0:T(128)S(1)} fusion(s32[]{:T(128)} %bitcast.4, s32[]{:T(128)} %bitcast.3), kind=kLoop, calls=%fused_computation.40 | loop fusion | flops 8 | bytes 24 | tf_op jit(solution)/shard_map/jit(_where)/select_n | solution.py:446
  27.6 1.3 %compare_select_fusion.4 = s32[4]{0:T(128)S(1)} fusion(s32[]{:T(128)} %bitcast.6, s32[]{:T(128)} %bitcast.5), kind=kLoop, calls=%fused_computation.39 | loop fusion | flops 8 | bytes 24 | tf_op jit(solution)/shard_map/jit(_where)/select_n | solution.py:447
  28.9 0.0 copy-done.6
  28.9 0.0 copy-done.7
  28.9 1.1 %fusion.7.phi = f32[8,8,4,128]{3,2,1,0:T(4,128)S(1)} fusion(s32[4]{0:T(128)S(1)} %fusion.10, s32[8,8,128]{2,1,0:T(8,128)S(1)} %copy-done.6, s32[4]{0:T(128)S(1)} %compare_select_fusion.4, s32[8,8,128]{2,1,0:T(8,128)S(1)} %copy-done.7, s32[4]{0:T(128)S(1)} %compare_select_fusion.5), kind=kLoop, calls=%fused_computation.26 | loop fusion | flops 557056 | bytes 196656 | tf_op jit(solution)/shard_map/cos | solution.py:451
  30.0 0.7 fusion.3.psi
  30.7 5.3 %all-to-all-done = f32[16,80,128]{2,1,0:T(8,128)S(1)} async-done(((f32[16,80,128]{2,1,0:T(8,128)}), f32[16,80,128]{2,1,0:T(8,128)S(1)}, u32[]{:S(2)}, u32[]{:S(2)}) %all-to-all-start) | async-done | bytes 655392 | tf_op jit(solution)/shard_map/all_to_all | solution.py:475
  36.0 1.6 %shard_map.156 = (f32[4,96,128]{2,1,0:T(8,128)S(1)}, f32[8,128]{1,0:T(8,128)S(1)}) custom-call(f32[1280,128]{1,0:T(8,128)S(1)} %bitcast.25), custom_call_target="tpu_custom_call" | custom-call | tf_op jit(solution)/shard_map/pallas_call | solution.py:262
  37.6 1.0 %collective-permute-start.4 = (f32[1,4,96,128]{3,2,1,0:T(8,128)S(1)}, f32[1,4,96,128]{3,2,1,0:T(8,128)S(1)}, u32[]{:S(2)}, u32[]{:S(2)}) collective-permute-start(f32[1,4,96,128]{3,2,1,0:T(8,128)S(1)} %bitcast.26), channel_id=1, source_target_pairs={{0,1},{1,0},{2,3},{3,2},{4,5},{5,4},{6,7},{7,6},{8,9},{9,8},{10,11... | collective-permute-start | bytes 589832 | tf_op jit(solution)/shard_map/ppermute | solution.py:441
  38.6 0.1 collective-permute-start.3
  38.7 1.3 %collective-permute-start.2 = (f32[4,96,128]{2,1,0:T(8,128)S(1)}, f32[4,96,128]{2,1,0:T(8,128)S(1)}, u32[]{:S(2)}, u32[]{:S(2)}) collective-permute-start(f32[4,96,128]{2,1,0:T(8,128)S(1)} %get-tuple-element.27), channel_id=1, source_target_pairs={{0,2},{1,3},{2,4},{3,5},{4,6},{5,7},{6,0},{7,1},{8,10},{9,11},{10,... | collective-permute-start | bytes 589832 | tf_op jit(solution)/shard_map/ppermute | solution.py:441
  40.1 0.3 collective-permute-start.1
  40.4 0.0 collective-permute-done.4
  40.4 0.0 copy-done
  40.4 0.0 copy-done.1
  40.4 0.0 copy-done.2
  40.4 0.0 copy-done.3
  40.4 0.0 copy-done.4
  40.5 2.7 %shard_map.157.rest_0_ = f32[16,64,2,8,256]{4,3,2,1,0:T(8,128)S(1)} custom-call(s32[1]{0:T(128)} %bitcast.me, f32[1,8,96,128]{3,2,1,0:T(8,128)S(1)} %pad_maximum_fusion.3.w, f32[8,8,4,128]{3,2,1,0:T(4,128)S(1)} %fusion.7.phi, f32[8,48,128]{2,1,0:T(8,128)S(1)} %fusion.3.psi, f32[2,128,128]{2,1,0:T(8,128)S(1)} %copy-done.3, f32[64,2,128]{2,1,0:T(2,128)S(1)} %copy-done.4, ...), custom_call_target="tpu_custom_call" | custom-call | flops 1500000000 | bytes 3000000 | tf_op jit(solution)/shard_map/pallas_call | solution.py:335
  43.2 1.9 %collective-permute-done.3 = f32[4,96,128]{2,1,0:T(8,128)S(1)} collective-permute-done((f32[4,96,128]{2,1,0:T(8,128)S(1)}, f32[4,96,128]{2,1,0:T(8,128)S(1)}, u32[]{:S(2)}, u32[]{:S(2)}) %collective-permute-start.3) | collective-permute-done | bytes 196640 | tf_op jit(solution)/shard_map/ppermute | solution.py:441
  45.1 0.6 collective-permute-done.2
  45.7 1.7 %collective-permute-done.1 = f32[4,96,128]{2,1,0:T(8,128)S(1)} collective-permute-done((f32[4,96,128]{2,1,0:T(8,128)S(1)}, f32[4,96,128]{2,1,0:T(8,128)S(1)}, u32[]{:S(2)}, u32[]{:S(2)}) %collective-permute-start.1) | collective-permute-done | bytes 196640 | tf_op jit(solution)/shard_map/ppermute | solution.py:441
  47.5 1.6 %collective-permute-start.7 = (f32[3,4,96,128]{3,2,1,0:T(8,128)S(1)}, f32[3,4,96,128]{3,2,1,0:T(8,128)S(1)}, u32[]{:S(2)}, u32[]{:S(2)}) collective-permute-start(f32[3,4,96,128]{3,2,1,0:T(8,128)S(1)} %pad_maximum_fusion.2), channel_id=1, source_target_pairs={{0,1},{1,0},{2,3},{3,2},{4,5},{5,4},{6,7},{7,6},{8,9},{9,8},{10,11... | collective-permute-start | bytes 1769480 | tf_op jit(solution)/shard_map/ppermute | solution.py:441
  49.1 1.4 %collective-permute-start.6 = (f32[6,96,128]{2,1,0:T(8,128)S(1)}, f32[6,96,128]{2,1,0:T(8,128)S(1)}, u32[]{:S(2)}, u32[]{:S(2)}) collective-permute-start(f32[6,96,128]{2,1,0:T(8,128)S(1)} %get-tuple-element.45), channel_id=1, source_target_pairs={{0,6},{1,7},{2,0},{3,1},{4,2},{5,3},{6,4},{7,5},{8,14},{9,15},{10,... | collective-permute-start | bytes 884744 | tf_op jit(solution)/shard_map/ppermute | solution.py:441
  50.5 0.1 collective-permute-start.5
  50.6 0.0 collective-permute-done.7
  50.7 0.1 pad_maximum_fusion.w
  50.7 8.6 %shard_map.158.rest_0_ = f32[16,64,2,8,256]{4,3,2,1,0:T(8,128)S(1)} custom-call(s32[1]{0:T(128)} %bitcast.me, f32[3,8,96,128]{3,2,1,0:T(8,128)S(1)} %pad_maximum_fusion.w, f32[8,8,4,128]{3,2,1,0:T(4,128)S(1)} %fusion.7.phi, f32[8,48,128]{2,1,0:T(8,128)S(1)} %fusion.3.psi, f32[2,128,128]{2,1,0:T(8,128)S(1)} %copy-done.3, ...), custom_call_target="tpu_custom_call", output_to_operand_aliasing={{}: (9, {})} | custom-call | flops 4499999744 | bytes 9000000 | tf_op jit(solution)/shard_map/pallas_call | solution.py:335
  59.4 0.0 collective-permute-done.6
  59.4 0.6 collective-permute-done.5
  60.1 1.4 %collective-permute-start.10 = (f32[2,4,96,128]{3,2,1,0:T(8,128)S(1)}, f32[2,4,96,128]{3,2,1,0:T(8,128)S(1)}, u32[]{:S(2)}, u32[]{:S(2)}) collective-permute-start(f32[2,4,96,128]{3,2,1,0:T(8,128)S(1)} %pad_maximum_fusion.4), channel_id=1, source_target_pairs={{0,1},{1,0},{2,3},{3,2},{4,5},{5,4},{6,7},{7,6},{8,9},{9,8},{10,11... | collective-permute-start | bytes 1179656 | tf_op jit(solution)/shard_map/ppermute | solution.py:441
  61.5 0.1 collective-permute-start.8
  61.6 2.7 %collective-permute-start.9 = (f32[2,96,128]{2,1,0:T(8,128)S(1)}, f32[2,96,128]{2,1,0:T(8,128)S(1)}, u32[]{:S(2)}, u32[]{:S(2)}) collective-permute-start(f32[2,96,128]{2,1,0:T(8,128)S(1)} %get-tuple-element.44), channel_id=1, source_target_pairs={{0,6},{1,7},{2,0},{3,1},{4,2},{5,3},{6,4},{7,5},{8,14},{9,15},{10,... | collective-permute-start | bytes 294920 | tf_op jit(solution)/shard_map/ppermute | solution.py:441
  64.3 0.7 collective-permute-start.12
  65.0 0.0 collective-permute-done.10
  65.0 0.1 pad_maximum_fusion.1.w
  65.1 5.8 %shard_map.159.rest_0_ = f32[16,64,2,8,256]{4,3,2,1,0:T(8,128)S(1)} custom-call(s32[1]{0:T(128)} %bitcast.me, f32[2,8,96,128]{3,2,1,0:T(8,128)S(1)} %pad_maximum_fusion.1.w, f32[8,8,4,128]{3,2,1,0:T(4,128)S(1)} %fusion.7.phi, f32[8,48,128]{2,1,0:T(8,128)S(1)} %fusion.3.psi, f32[2,128,128]{2,1,0:T(8,128)S(1)} %copy-done.3, ...), custom_call_target="tpu_custom_call", output_to_operand_aliasing={{}: (9, {})} | custom-call | flops 3000000000 | bytes 6000000 | tf_op jit(solution)/shard_map/pallas_call | solution.py:335
  70.8 0.0 collective-permute-done.8
  70.8 0.0 collective-permute-done.9
  70.9 0.1 collective-permute-start.11
  71.0 0.0 collective-permute-done.12
  71.0 2.7 %shard_map.160.rest_0_ = f32[16,64,2,8,256]{4,3,2,1,0:T(8,128)S(1)} custom-call(s32[1]{0:T(128)} %bitcast.me, f32[1,8,96,128]{3,2,1,0:T(8,128)S(1)} %pad_maximum_fusion.6.w, f32[8,8,4,128]{3,2,1,0:T(4,128)S(1)} %fusion.7.phi, f32[8,48,128]{2,1,0:T(8,128)S(1)} %fusion.3.psi, f32[2,128,128]{2,1,0:T(8,128)S(1)} %copy-done.3, ...), custom_call_target="tpu_custom_call", output_to_operand_aliasing={{}: (9, {})} | custom-call | flops 1500000000 | bytes 3000000 | tf_op jit(solution)/shard_map/pallas_call | solution.py:335
  73.7 0.0 collective-permute-done.11
  73.8 2.7 %shard_map.161.h = f32[16,64,2,8,256]{4,3,2,1,0:T(8,128)S(1)} custom-call(s32[1]{0:T(128)} %bitcast.me, f32[1,8,96,128]{3,2,1,0:T(8,128)S(1)} %pad_maximum_fusion.5.w, f32[8,8,4,128]{3,2,1,0:T(4,128)S(1)} %fusion.7.phi, f32[8,48,128]{2,1,0:T(8,128)S(1)} %fusion.3.psi, f32[2,128,128]{2,1,0:T(8,128)S(1)} %copy-done.3, ...), custom_call_target="tpu_custom_call", output_to_operand_aliasing={{}: (9, {})} | custom-call | flops 1500000000 | bytes 3000000 | tf_op jit(solution)/shard_map/pallas_call | solution.py:335
  76.5 7.4 %shard_map.162 = f32[32,256,128]{2,1,0:T(8,128)} custom-call(f32[16,64,2,8,256]{4,3,2,1,0:T(8,128)S(1)} %shard_map.161.h, f32[8,128]{1,0:T(8,128)S(1)} %get-tuple-element.40.sig), custom_call_target="tpu_custom_call" | custom-call | tf_op jit(solution)/shard_map/pallas_call | solution.py:416
  (21 shorter events, 0.3 us)
Async XLA Ops:
  0.0 10.2 %collective-permute-start = (f32[256,128]{1,0:T(8,128)}, f32[256,128]{1,0:T(8,128)S(1)}, u32[]{:S(2)}, u32[]{:S(2)}) collective-permute-start(f32[256,128]{1,0:T(8,128)} %bitcast.34), channel_id=1, source_target_pairs={{0,16},{16,32},{32,48},{48,64},{64,80},{80,96},{96,112},{1,17},{17... | collective-permute-start | bytes 393224 | tf_op jit(solution)/shard_map/ppermute | solution.py:468
  10.1 13.0 %copy-start.8 = (s32[2]{0:T(128)S(1)}, s32[2]{0:T(128)}, u32[]{:S(2)}) copy-start(s32[2]{0:T(128)} %param.19) | copy-start | bytes 28
  10.1 13.0 %copy-start.9 = (s32[2]{0:T(128)S(1)}, s32[2]{0:T(128)}, u32[]{:S(2)}) copy-start(s32[2]{0:T(128)} %param.20) | copy-start | bytes 28
  10.1 18.8 %copy-start.6 = (s32[8,8,128]{2,1,0:T(8,128)S(1)}, s32[8,8,128]{2,1,0:T(8,128)}, u32[]{:S(2)}) copy-start(s32[8,8,128]{2,1,0:T(8,128)} %constant.141) | copy-start | bytes 98308
  10.1 18.8 %copy-start.7 = (s32[8,8,128]{2,1,0:T(8,128)S(1)}, s32[8,8,128]{2,1,0:T(8,128)}, u32[]{:S(2)}) copy-start(s32[8,8,128]{2,1,0:T(8,128)} %constant.140) | copy-start | bytes 98308
  10.2 0.7 copy-start.5
  15.3 25.1 %copy-start = (f32[8,128,128]{2,1,0:T(8,128)S(1)}, f32[8,128,128]{2,1,0:T(8,128)}, u32[]{:S(2)}) copy-start(f32[8,128,128]{2,1,0:T(8,128)} %constant.133.clone.tw3) | copy-start | bytes 1572868
  15.3 25.1 %copy-start.1 = (bf16[256,768]{1,0:T(8,128)(2,1)S(1)}, bf16[256,768]{1,0:T(8,128)(2,1)}, u32[]{:S(2)}) copy-start(bf16[256,768]{1,0:T(8,128)(2,1)} %constant.130.clone.e2) | copy-start | bytes 1179652
  15.3 25.1 %copy-start.2 = (bf16[288,256]{1,0:T(8,128)(2,1)S(1)}, bf16[288,256]{1,0:T(8,128)(2,1)}, u32[]{:S(2)}) copy-start(bf16[288,256]{1,0:T(8,128)(2,1)} %constant.129.clone.e1) | copy-start | bytes 442372
  15.3 25.1 %copy-start.3 = (f32[2,128,128]{2,1,0:T(8,128)S(1)}, f32[2,128,128]{2,1,0:T(8,128)}, u32[]{:S(2)}) copy-start(f32[2,128,128]{2,1,0:T(8,128)} %constant.131.clone.tw) | copy-start | bytes 393220
  15.3 25.1 %copy-start.4 = (f32[64,2,128]{2,1,0:T(2,128)S(1)}, f32[64,2,128]{2,1,0:T(2,128)}, u32[]{:S(2)}) copy-start(f32[64,2,128]{2,1,0:T(2,128)} %constant.132.clone.twb) | copy-start | bytes 196612
  15.3 20.7 %all-to-all-start = ((f32[16,80,128]{2,1,0:T(8,128)}), f32[16,80,128]{2,1,0:T(8,128)S(1)}, u32[]{:S(2)}, u32[]{:S(2)}) async-start(f32[16,80,128]{2,1,0:T(8,128)} %shard_map.155), calls=%async_computation | async-start | bytes 1310720 | tf_op jit(solution)/shard_map/all_to_all | solution.py:475
  37.6 2.8 %collective-permute-start.4 = (f32[1,4,96,128]{3,2,1,0:T(8,128)S(1)}, f32[1,4,96,128]{3,2,1,0:T(8,128)S(1)}, u32[]{:S(2)}, u32[]{:S(2)}) collective-permute-start(f32[1,4,96,128]{3,2,1,0:T(8,128)S(1)} %bitcast.26), channel_id=1, source_target_pairs={{0,1},{1,0},{2,3},{3,2},{4,5},{5,4},{6,7},{7,6},{8,9},{9,8},{10,11... | collective-permute-start | bytes 589832 | tf_op jit(solution)/shard_map/ppermute | solution.py:441
  38.6 6.5 %collective-permute-start.3 = (f32[4,96,128]{2,1,0:T(8,128)S(1)}, f32[4,96,128]{2,1,0:T(8,128)S(1)}, u32[]{:S(2)}, u32[]{:S(2)}) collective-permute-start(f32[4,96,128]{2,1,0:T(8,128)S(1)} %get-tuple-element.27), channel_id=1, source_target_pairs={{0,6},{1,7},{2,0},{3,1},{4,2},{5,3},{6,4},{7,5},{8,14},{9,15},{10,... | collective-permute-start | bytes 589832 | tf_op jit(solution)/shard_map/ppermute | solution.py:441
  38.7 6.9 %collective-permute-start.2 = (f32[4,96,128]{2,1,0:T(8,128)S(1)}, f32[4,96,128]{2,1,0:T(8,128)S(1)}, u32[]{:S(2)}, u32[]{:S(2)}) collective-permute-start(f32[4,96,128]{2,1,0:T(8,128)S(1)} %get-tuple-element.27), channel_id=1, source_target_pairs={{0,2},{1,3},{2,4},{3,5},{4,6},{5,7},{6,0},{7,1},{8,10},{9,11},{10,... | collective-permute-start | bytes 589832 | tf_op jit(solution)/shard_map/ppermute | solution.py:441
  40.1 7.3 %collective-permute-start.1 = (f32[4,96,128]{2,1,0:T(8,128)S(1)}, f32[4,96,128]{2,1,0:T(8,128)S(1)}, u32[]{:S(2)}, u32[]{:S(2)}) collective-permute-start(f32[4,96,128]{2,1,0:T(8,128)S(1)} %get-tuple-element.27), channel_id=1, source_target_pairs={{0,8},{1,9},{2,10},{3,11},{4,12},{5,13},{6,14},{7,15},{8,0},{9,1},... | collective-permute-start | bytes 589832 | tf_op jit(solution)/shard_map/ppermute | solution.py:441
  47.5 3.2 %collective-permute-start.7 = (f32[3,4,96,128]{3,2,1,0:T(8,128)S(1)}, f32[3,4,96,128]{3,2,1,0:T(8,128)S(1)}, u32[]{:S(2)}, u32[]{:S(2)}) collective-permute-start(f32[3,4,96,128]{3,2,1,0:T(8,128)S(1)} %pad_maximum_fusion.2), channel_id=1, source_target_pairs={{0,1},{1,0},{2,3},{3,2},{4,5},{5,4},{6,7},{7,6},{8,9},{9,8},{10,11... | collective-permute-start | bytes 1769480 | tf_op jit(solution)/shard_map/ppermute | solution.py:441
  49.1 10.3 %collective-permute-start.6 = (f32[6,96,128]{2,1,0:T(8,128)S(1)}, f32[6,96,128]{2,1,0:T(8,128)S(1)}, u32[]{:S(2)}, u32[]{:S(2)}) collective-permute-start(f32[6,96,128]{2,1,0:T(8,128)S(1)} %get-tuple-element.45), channel_id=1, source_target_pairs={{0,6},{1,7},{2,0},{3,1},{4,2},{5,3},{6,4},{7,5},{8,14},{9,15},{10,... | collective-permute-start | bytes 884744 | tf_op jit(solution)/shard_map/ppermute | solution.py:441
  50.5 9.5 %collective-permute-start.5 = (f32[6,96,128]{2,1,0:T(8,128)S(1)}, f32[6,96,128]{2,1,0:T(8,128)S(1)}, u32[]{:S(2)}, u32[]{:S(2)}) collective-permute-start(f32[6,96,128]{2,1,0:T(8,128)S(1)} %get-tuple-element.46), channel_id=1, source_target_pairs={{0,2},{1,3},{2,4},{3,5},{4,6},{5,7},{6,0},{7,1},{8,10},{9,11},{10,... | collective-permute-start | bytes 884744 | tf_op jit(solution)/shard_map/ppermute | solution.py:441
  60.1 4.9 %collective-permute-start.10 = (f32[2,4,96,128]{3,2,1,0:T(8,128)S(1)}, f32[2,4,96,128]{3,2,1,0:T(8,128)S(1)}, u32[]{:S(2)}, u32[]{:S(2)}) collective-permute-start(f32[2,4,96,128]{3,2,1,0:T(8,128)S(1)} %pad_maximum_fusion.4), channel_id=1, source_target_pairs={{0,1},{1,0},{2,3},{3,2},{4,5},{5,4},{6,7},{7,6},{8,9},{9,8},{10,11... | collective-permute-start | bytes 1179656 | tf_op jit(solution)/shard_map/ppermute | solution.py:441
  61.5 9.3 %collective-permute-start.8 = (f32[2,96,128]{2,1,0:T(8,128)S(1)}, f32[2,96,128]{2,1,0:T(8,128)S(1)}, u32[]{:S(2)}, u32[]{:S(2)}) collective-permute-start(f32[2,96,128]{2,1,0:T(8,128)S(1)} %get-tuple-element.42), channel_id=1, source_target_pairs={{0,2},{1,3},{2,4},{3,5},{4,6},{5,7},{6,0},{7,1},{8,10},{9,11},{10,... | collective-permute-start | bytes 294920 | tf_op jit(solution)/shard_map/ppermute | solution.py:441
  61.6 9.2 %collective-permute-start.9 = (f32[2,96,128]{2,1,0:T(8,128)S(1)}, f32[2,96,128]{2,1,0:T(8,128)S(1)}, u32[]{:S(2)}, u32[]{:S(2)}) collective-permute-start(f32[2,96,128]{2,1,0:T(8,128)S(1)} %get-tuple-element.44), channel_id=1, source_target_pairs={{0,6},{1,7},{2,0},{3,1},{4,2},{5,3},{6,4},{7,5},{8,14},{9,15},{10,... | collective-permute-start | bytes 294920 | tf_op jit(solution)/shard_map/ppermute | solution.py:441
  64.3 6.6 %collective-permute-start.12 = (f32[1,4,96,128]{3,2,1,0:T(8,128)S(1)}, f32[1,4,96,128]{3,2,1,0:T(8,128)S(1)}, u32[]{:S(2)}, u32[]{:S(2)}) collective-permute-start(f32[1,4,96,128]{3,2,1,0:T(8,128)S(1)} %maximum_bitcast_fusion.1), channel_id=1, source_target_pairs={{0,1},{1,0},{2,3},{3,2},{4,5},{5,4},{6,7},{7,6},{8,9},{9,8},{10,11... | collective-permute-start | bytes 589832 | tf_op jit(solution)/shard_map/ppermute | solution.py:441
  70.9 2.9 %collective-permute-start.11 = (f32[1,4,96,128]{3,2,1,0:T(8,128)S(1)}, f32[1,4,96,128]{3,2,1,0:T(8,128)S(1)}, u32[]{:S(2)}, u32[]{:S(2)}) collective-permute-start(f32[1,4,96,128]{3,2,1,0:T(8,128)S(1)} %maximum_bitcast_fusion), channel_id=1, source_target_pairs={{0,1},{1,0},{2,3},{3,2},{4,5},{5,4},{6,7},{7,6},{8,9},{9,8},{10,11... | collective-permute-start | bytes 589832 | tf_op jit(solution)/shard_map/ppermute | solution.py:441

commit v8 on v7

--- a/solution.py
+++ b/solution.py
@@ -391,7 +391,7 @@
 
 def out_kernel(h, sig, out, mid):
     scale = sig[...]
-    for tile, m in ((0, 0), (0, 1), (1, 0), (1, 1)):
+    for tile, m in [(n // 2, n % 2) for n in range(8)]:
         at = slice(128 * m, 128 * m + 128)
         for lo in range(8):
             x = [(h[tile, 8 * hi + lo, 0, :, at], h[tile, 8 * hi + lo, 1, :, at]) for hi in range(8)]
@@ -415,12 +415,12 @@
 def out_call(h, sig):
     return pl.pallas_call(
         out_kernel,
-        grid=(8,),
+        grid=(4,),
         in_specs=[
-            pl.BlockSpec((2, 64, 2, 8, 256), lambda i: (i, 0, 0, 0, 0)),
+            pl.BlockSpec((4, 64, 2, 8, 256), lambda i: (i, 0, 0, 0, 0)),
             pl.BlockSpec((8, 128), lambda i: (0, 0)),
         ],
-        out_specs=pl.BlockSpec((32, 32, 128), lambda i: (0, i, 0)),
+        out_specs=pl.BlockSpec((32, 64, 128), lambda i: (0, i, 0)),
         out_shape=jax.ShapeDtypeStruct((32, 256, 128), F32),
         scratch_shapes=[pltpu.VMEM((8, 8, 2, 8, 128), F32)],
         compiler_params=pltpu.CompilerParams(vmem_limit_bytes=OUT_VMEM),

time: 84.2 us -> 84.3 us (level)
  no operation moved by 1% of the time
where the time goes in v8:
time: 84.3 us; the launch traced here: 84 us
  Pallas kernels  42 us (50%)
  starting transfers between devices  22.6 us (27%)
  waiting for transfers between devices  10.2 us (12%)
  other arithmetic  7.24 us (9%)
  local copies, waits for them, and re-layouts  1.44 us (2%)
    pallas_call x5, Pallas kernels, inv_call(): pl.pallas_call(inv_kernel, grid_spec=pltpu.PrefetchScalarGridSpec(num_sca...  22.5 us
    ppermute x12, starting transfers between devices, sent(): return lax.ppermute(v, 'tmpl', route)  10.8 us
    all_to_all x1, starting transfers between devices, local(): lax.all_to_all(sent_out, 'tmpl', split_axis=0, concat_axis=0, tiled=True)  7.76 us
    pallas_call x1, Pallas kernels, out_call(): pl.pallas_call(out_kernel, grid=(4,), in_specs=[pl.BlockSpec((4, 64, 2, 8...  7.47 us
    pallas_call x1, Pallas kernels, psd_call(): pl.pallas_call(psd_kernel, grid_spec=pltpu.PrefetchScalarGridSpec(num_sca...  6.01 us
    all_to_all x1, waiting for transfers between devices, local(): lax.all_to_all(sent_out, 'tmpl', split_axis=0, concat_axis=0, tiled=True)  5.31 us
    ppermute x12, waiting for transfers between devices, sent(): return lax.ppermute(v, 'tmpl', route)  4.89 us
    pallas_call x1, Pallas kernels, fwd_call(): pl.pallas_call(fwd_kernel, grid_spec=pltpu.PrefetchScalarGridSpec(num_sca...  4.48 us
  transfers between devices with their start and end apart: 14, of which 5 were waited for; matrix products, arithmetic and copies ran while one was open for 9% of the time, Pallas kernels for 31%

profile of v8, /device:TPU:1, one launch (start us, length us, event | category | flops | bytes accessed | tf_op | source)
XLA Modules:
  0.0 84.0 jit_solution(10021400196888097829)
XLA Ops:
  0.0 4.0 %collective-permute-start = (f32[256,128]{1,0:T(8,128)}, f32[256,128]{1,0:T(8,128)S(1)}, u32[]{:S(2)}, u32[]{:S(2)}) collective-permute-start(f32[256,128]{1,0:T(8,128)} %bitcast.34), channel_id=1, source_target_pairs={{0,16},{16,32},{32,48},{48,64},{64,80},{80,96},{96,112},{1,17},{17... | collective-permute-start | bytes 393224 | tf_op jit(solution)/shard_map/ppermute | solution.py:468
  4.1 6.0 %shard_map.154.extra = f32[16,16,128]{2,1,0:T(8,128)} custom-call(s32[1]{0:T(128)} %bitcast.me, s32[8,4096]{1,0:T(8,128)} %bins_hbm.1, f32[64,128]{1,0:T(8,128)} %bitcast.36), custom_call_target="tpu_custom_call" | custom-call | tf_op jit(solution)/shard_map/pallas_call | solution.py:147
  10.1 0.0 copy-start.8
  10.1 0.0 copy-start.9
  10.1 0.0 copy-start.6
  10.1 0.0 copy-start.7
  10.2 0.0 collective-permute-done.tail
  10.2 0.0 copy-start.5
  10.2 0.6 copy-done.5
  10.8 4.5 %shard_map.155 = f32[16,80,128]{2,1,0:T(8,128)} custom-call(s32[1]{0:T(128)} %bitcast.me, f32[256,128]{1,0:T(8,128)} %copy-done.5, f32[256,128]{1,0:T(8,128)} %bitcast.35, bf16[2,1024,512]{2,1,0:T(8,128)(2,1)} %constant.125.clone.l1, f32[2,512,128]{2,1,0:T(8,128)} %constant.126.clone.tw1, bf16[768,256]{1,0:T(8,128)(2,1)} %constant.127.clone.m2, ...), custom_call_target="tpu_custom_call" | custom-call | tf_op jit(solution)/shard_map/pallas_call | solution.py:192
  15.3 0.0 copy-start.3
  15.3 0.0 copy-start.4
  15.3 7.8 %all-to-all-start = ((f32[16,80,128]{2,1,0:T(8,128)}), f32[16,80,128]{2,1,0:T(8,128)S(1)}, u32[]{:S(2)}, u32[]{:S(2)}) async-start(f32[16,80,128]{2,1,0:T(8,128)} %shard_map.155), calls=%async_computation | async-start | bytes 1310720 | tf_op jit(solution)/shard_map/all_to_all | solution.py:475
  23.1 0.0 copy-done.8
  23.1 0.0 copy-done.9
  23.1 0.7 fusion.15
  23.8 1.2 %compare_select_fusion.3 = s32[128]{0:T(128)S(1)} fusion(s32[]{:T(128)} %bitcast.4, s32[]{:T(128)} %bitcast.3), kind=kLoop, calls=%fused_computation.38 | loop fusion | flops 256 | bytes 520 | tf_op jit(solution)/shard_map/jit(_where)/select_n | solution.py:453
  25.0 1.3 %fusion.9 = s32[128]{0:T(128)S(1)} fusion(s32[]{:T(128)} %bitcast.6, s32[]{:T(128)} %bitcast.5), kind=kLoop, calls=%fused_computation.43 | loop fusion | flops 384 | bytes 520 | tf_op jit(solution)/shard_map/mul | solution.py:457
  26.3 0.1 add_select_fusion.2
  26.4 1.2 %compare_select_fusion.5 = s32[4]{0:T(128)S(1)} fusion(s32[]{:T(128)} %bitcast.4, s32[]{:T(128)} %bitcast.3), kind=kLoop, calls=%fused_computation.40 | loop fusion | flops 8 | bytes 24 | tf_op jit(solution)/shard_map/jit(_where)/select_n | solution.py:446
  27.6 1.3 %compare_select_fusion.4 = s32[4]{0:T(128)S(1)} fusion(s32[]{:T(128)} %bitcast.6, s32[]{:T(128)} %bitcast.5), kind=kLoop, calls=%fused_computation.39 | loop fusion | flops 8 | bytes 24 | tf_op jit(solution)/shard_map/jit(_where)/select_n | solution.py:447
  28.9 0.0 copy-done.6
  28.9 0.0 copy-done.7
  28.9 1.1 %fusion.7.phi = f32[8,8,4,128]{3,2,1,0:T(4,128)S(1)} fusion(s32[4]{0:T(128)S(1)} %fusion.10, s32[8,8,128]{2,1,0:T(8,128)S(1)} %copy-done.6, s32[4]{0:T(128)S(1)} %compare_select_fusion.4, s32[8,8,128]{2,1,0:T(8,128)S(1)} %copy-done.7, s32[4]{0:T(128)S(1)} %compare_select_fusion.5), kind=kLoop, calls=%fused_computation.26 | loop fusion | flops 557056 | bytes 196656 | tf_op jit(solution)/shard_map/cos | solution.py:451
  30.0 0.7 fusion.3.psi
  30.7 5.3 %all-to-all-done = f32[16,80,128]{2,1,0:T(8,128)S(1)} async-done(((f32[16,80,128]{2,1,0:T(8,128)}), f32[16,80,128]{2,1,0:T(8,128)S(1)}, u32[]{:S(2)}, u32[]{:S(2)}) %all-to-all-start) | async-done | bytes 655392 | tf_op jit(solution)/shard_map/all_to_all | solution.py:475
  36.0 1.6 %shard_map.156 = (f32[4,96,128]{2,1,0:T(8,128)S(1)}, f32[8,128]{1,0:T(8,128)S(1)}) custom-call(f32[1280,128]{1,0:T(8,128)S(1)} %bitcast.25), custom_call_target="tpu_custom_call" | custom-call | tf_op jit(solution)/shard_map/pallas_call | solution.py:262
  37.6 1.0 %collective-permute-start.4 = (f32[1,4,96,128]{3,2,1,0:T(8,128)S(1)}, f32[1,4,96,128]{3,2,1,0:T(8,128)S(1)}, u32[]{:S(2)}, u32[]{:S(2)}) collective-permute-start(f32[1,4,96,128]{3,2,1,0:T(8,128)S(1)} %bitcast.26), channel_id=1, source_target_pairs={{0,1},{1,0},{2,3},{3,2},{4,5},{5,4},{6,7},{7,6},{8,9},{9,8},{10,11... | collective-permute-start | bytes 589832 | tf_op jit(solution)/shard_map/ppermute | solution.py:441
  38.6 0.1 collective-permute-start.3
  38.7 1.3 %collective-permute-start.2 = (f32[4,96,128]{2,1,0:T(8,128)S(1)}, f32[4,96,128]{2,1,0:T(8,128)S(1)}, u32[]{:S(2)}, u32[]{:S(2)}) collective-permute-start(f32[4,96,128]{2,1,0:T(8,128)S(1)} %get-tuple-element.27), channel_id=1, source_target_pairs={{0,2},{1,3},{2,4},{3,5},{4,6},{5,7},{6,0},{7,1},{8,10},{9,11},{10,... | collective-permute-start | bytes 589832 | tf_op jit(solution)/shard_map/ppermute | solution.py:441
  40.1 0.3 collective-permute-start.1
  40.4 0.0 collective-permute-done.4
  40.4 0.0 copy-done
  40.4 0.0 copy-done.1
  40.4 0.0 copy-done.2
  40.4 0.0 copy-done.3
  40.4 0.0 copy-done.4
  40.5 2.7 %shard_map.157.rest_0_ = f32[16,64,2,8,256]{4,3,2,1,0:T(8,128)S(1)} custom-call(s32[1]{0:T(128)} %bitcast.me, f32[1,8,96,128]{3,2,1,0:T(8,128)S(1)} %pad_maximum_fusion.3.w, f32[8,8,4,128]{3,2,1,0:T(4,128)S(1)} %fusion.7.phi, f32[8,48,128]{2,1,0:T(8,128)S(1)} %fusion.3.psi, f32[2,128,128]{2,1,0:T(8,128)S(1)} %copy-done.3, f32[64,2,128]{2,1,0:T(2,128)S(1)} %copy-done.4, ...), custom_call_target="tpu_custom_call" | custom-call | flops 1500000000 | bytes 3000000 | tf_op jit(solution)/shard_map/pallas_call | solution.py:335
  43.2 1.9 %collective-permute-done.3 = f32[4,96,128]{2,1,0:T(8,128)S(1)} collective-permute-done((f32[4,96,128]{2,1,0:T(8,128)S(1)}, f32[4,96,128]{2,1,0:T(8,128)S(1)}, u32[]{:S(2)}, u32[]{:S(2)}) %collective-permute-start.3) | collective-permute-done | bytes 196640 | tf_op jit(solution)/shard_map/ppermute | solution.py:441
  45.1 0.6 collective-permute-done.2
  45.7 1.7 %collective-permute-done.1 = f32[4,96,128]{2,1,0:T(8,128)S(1)} collective-permute-done((f32[4,96,128]{2,1,0:T(8,128)S(1)}, f32[4,96,128]{2,1,0:T(8,128)S(1)}, u32[]{:S(2)}, u32[]{:S(2)}) %collective-permute-start.1) | collective-permute-done | bytes 196640 | tf_op jit(solution)/shard_map/ppermute | solution.py:441
  47.5 1.6 %collective-permute-start.7 = (f32[3,4,96,128]{3,2,1,0:T(8,128)S(1)}, f32[3,4,96,128]{3,2,1,0:T(8,128)S(1)}, u32[]{:S(2)}, u32[]{:S(2)}) collective-permute-start(f32[3,4,96,128]{3,2,1,0:T(8,128)S(1)} %pad_maximum_fusion.2), channel_id=1, source_target_pairs={{0,1},{1,0},{2,3},{3,2},{4,5},{5,4},{6,7},{7,6},{8,9},{9,8},{10,11... | collective-permute-start | bytes 1769480 | tf_op jit(solution)/shard_map/ppermute | solution.py:441
  49.1 1.4 %collective-permute-start.6 = (f32[6,96,128]{2,1,0:T(8,128)S(1)}, f32[6,96,128]{2,1,0:T(8,128)S(1)}, u32[]{:S(2)}, u32[]{:S(2)}) collective-permute-start(f32[6,96,128]{2,1,0:T(8,128)S(1)} %get-tuple-element.45), channel_id=1, source_target_pairs={{0,6},{1,7},{2,0},{3,1},{4,2},{5,3},{6,4},{7,5},{8,14},{9,15},{10,... | collective-permute-start | bytes 884744 | tf_op jit(solution)/shard_map/ppermute | solution.py:441
  50.5 0.1 collective-permute-start.5
  50.6 0.0 collective-permute-done.7
  50.7 0.1 pad_maximum_fusion.w
  50.7 8.6 %shard_map.158.rest_0_ = f32[16,64,2,8,256]{4,3,2,1,0:T(8,128)S(1)} custom-call(s32[1]{0:T(128)} %bitcast.me, f32[3,8,96,128]{3,2,1,0:T(8,128)S(1)} %pad_maximum_fusion.w, f32[8,8,4,128]{3,2,1,0:T(4,128)S(1)} %fusion.7.phi, f32[8,48,128]{2,1,0:T(8,128)S(1)} %fusion.3.psi, f32[2,128,128]{2,1,0:T(8,128)S(1)} %copy-done.3, ...), custom_call_target="tpu_custom_call", output_to_operand_aliasing={{}: (9, {})} | custom-call | flops 4499999744 | bytes 9000000 | tf_op jit(solution)/shard_map/pallas_call | solution.py:335
  59.4 0.0 collective-permute-done.6
  59.4 0.6 collective-permute-done.5
  60.1 1.4 %collective-permute-start.10 = (f32[2,4,96,128]{3,2,1,0:T(8,128)S(1)}, f32[2,4,96,128]{3,2,1,0:T(8,128)S(1)}, u32[]{:S(2)}, u32[]{:S(2)}) collective-permute-start(f32[2,4,96,128]{3,2,1,0:T(8,128)S(1)} %pad_maximum_fusion.4), channel_id=1, source_target_pairs={{0,1},{1,0},{2,3},{3,2},{4,5},{5,4},{6,7},{7,6},{8,9},{9,8},{10,11... | collective-permute-start | bytes 1179656 | tf_op jit(solution)/shard_map/ppermute | solution.py:441
  61.5 0.1 collective-permute-start.8
  61.6 2.7 %collective-permute-start.9 = (f32[2,96,128]{2,1,0:T(8,128)S(1)}, f32[2,96,128]{2,1,0:T(8,128)S(1)}, u32[]{:S(2)}, u32[]{:S(2)}) collective-permute-start(f32[2,96,128]{2,1,0:T(8,128)S(1)} %get-tuple-element.44), channel_id=1, source_target_pairs={{0,6},{1,7},{2,0},{3,1},{4,2},{5,3},{6,4},{7,5},{8,14},{9,15},{10,... | collective-permute-start | bytes 294920 | tf_op jit(solution)/shard_map/ppermute | solution.py:441
  64.3 0.7 collective-permute-start.12
  65.0 0.0 collective-permute-done.10
  65.0 0.1 pad_maximum_fusion.1.w
  65.1 5.8 %shard_map.159.rest_0_ = f32[16,64,2,8,256]{4,3,2,1,0:T(8,128)S(1)} custom-call(s32[1]{0:T(128)} %bitcast.me, f32[2,8,96,128]{3,2,1,0:T(8,128)S(1)} %pad_maximum_fusion.1.w, f32[8,8,4,128]{3,2,1,0:T(4,128)S(1)} %fusion.7.phi, f32[8,48,128]{2,1,0:T(8,128)S(1)} %fusion.3.psi, f32[2,128,128]{2,1,0:T(8,128)S(1)} %copy-done.3, ...), custom_call_target="tpu_custom_call", output_to_operand_aliasing={{}: (9, {})} | custom-call | flops 3000000000 | bytes 6000000 | tf_op jit(solution)/shard_map/pallas_call | solution.py:335
  70.8 0.0 collective-permute-done.8
  70.8 0.0 collective-permute-done.9
  70.9 0.1 collective-permute-start.11
  71.0 0.0 collective-permute-done.12
  71.0 2.7 %shard_map.160.rest_0_ = f32[16,64,2,8,256]{4,3,2,1,0:T(8,128)S(1)} custom-call(s32[1]{0:T(128)} %bitcast.me, f32[1,8,96,128]{3,2,1,0:T(8,128)S(1)} %pad_maximum_fusion.6.w, f32[8,8,4,128]{3,2,1,0:T(4,128)S(1)} %fusion.7.phi, f32[8,48,128]{2,1,0:T(8,128)S(1)} %fusion.3.psi, f32[2,128,128]{2,1,0:T(8,128)S(1)} %copy-done.3, ...), custom_call_target="tpu_custom_call", output_to_operand_aliasing={{}: (9, {})} | custom-call | flops 1500000000 | bytes 3000000 | tf_op jit(solution)/shard_map/pallas_call | solution.py:335
  73.7 0.0 collective-permute-done.11
  73.8 2.7 %shard_map.161.h = f32[16,64,2,8,256]{4,3,2,1,0:T(8,128)S(1)} custom-call(s32[1]{0:T(128)} %bitcast.me, f32[1,8,96,128]{3,2,1,0:T(8,128)S(1)} %pad_maximum_fusion.5.w, f32[8,8,4,128]{3,2,1,0:T(4,128)S(1)} %fusion.7.phi, f32[8,48,128]{2,1,0:T(8,128)S(1)} %fusion.3.psi, f32[2,128,128]{2,1,0:T(8,128)S(1)} %copy-done.3, ...), custom_call_target="tpu_custom_call", output_to_operand_aliasing={{}: (9, {})} | custom-call | flops 1500000000 | bytes 3000000 | tf_op jit(solution)/shard_map/pallas_call | solution.py:335
  76.5 7.5 %shard_map.162 = f32[32,256,128]{2,1,0:T(8,128)} custom-call(f32[16,64,2,8,256]{4,3,2,1,0:T(8,128)S(1)} %shard_map.161.h, f32[8,128]{1,0:T(8,128)S(1)} %get-tuple-element.40.sig), custom_call_target="tpu_custom_call" | custom-call | tf_op jit(solution)/shard_map/pallas_call | solution.py:416
  (21 shorter events, 0.3 us)
Async XLA Ops:
  0.0 10.2 %collective-permute-start = (f32[256,128]{1,0:T(8,128)}, f32[256,128]{1,0:T(8,128)S(1)}, u32[]{:S(2)}, u32[]{:S(2)}) collective-permute-start(f32[256,128]{1,0:T(8,128)} %bitcast.34), channel_id=1, source_target_pairs={{0,16},{16,32},{32,48},{48,64},{64,80},{80,96},{96,112},{1,17},{17... | collective-permute-start | bytes 393224 | tf_op jit(solution)/shard_map/ppermute | solution.py:468
  10.1 13.0 %copy-start.8 = (s32[2]{0:T(128)S(1)}, s32[2]{0:T(128)}, u32[]{:S(2)}) copy-start(s32[2]{0:T(128)} %param.19) | copy-start | bytes 28
  10.1 13.0 %copy-start.9 = (s32[2]{0:T(128)S(1)}, s32[2]{0:T(128)}, u32[]{:S(2)}) copy-start(s32[2]{0:T(128)} %param.20) | copy-start | bytes 28
  10.1 18.8 %copy-start.6 = (s32[8,8,128]{2,1,0:T(8,128)S(1)}, s32[8,8,128]{2,1,0:T(8,128)}, u32[]{:S(2)}) copy-start(s32[8,8,128]{2,1,0:T(8,128)} %constant.141) | copy-start | bytes 98308
  10.1 18.8 %copy-start.7 = (s32[8,8,128]{2,1,0:T(8,128)S(1)}, s32[8,8,128]{2,1,0:T(8,128)}, u32[]{:S(2)}) copy-start(s32[8,8,128]{2,1,0:T(8,128)} %constant.140) | copy-start | bytes 98308
  10.2 0.7 copy-start.5
  15.3 25.1 %copy-start = (f32[8,128,128]{2,1,0:T(8,128)S(1)}, f32[8,128,128]{2,1,0:T(8,128)}, u32[]{:S(2)}) copy-start(f32[8,128,128]{2,1,0:T(8,128)} %constant.133.clone.tw3) | copy-start | bytes 1572868
  15.3 25.1 %copy-start.1 = (bf16[256,768]{1,0:T(8,128)(2,1)S(1)}, bf16[256,768]{1,0:T(8,128)(2,1)}, u32[]{:S(2)}) copy-start(bf16[256,768]{1,0:T(8,128)(2,1)} %constant.130.clone.e2) | copy-start | bytes 1179652
  15.3 25.1 %copy-start.2 = (bf16[288,256]{1,0:T(8,128)(2,1)S(1)}, bf16[288,256]{1,0:T(8,128)(2,1)}, u32[]{:S(2)}) copy-start(bf16[288,256]{1,0:T(8,128)(2,1)} %constant.129.clone.e1) | copy-start | bytes 442372
  15.3 25.1 %copy-start.3 = (f32[2,128,128]{2,1,0:T(8,128)S(1)}, f32[2,128,128]{2,1,0:T(8,128)}, u32[]{:S(2)}) copy-start(f32[2,128,128]{2,1,0:T(8,128)} %constant.131.clone.tw) | copy-start | bytes 393220
  15.3 25.1 %copy-start.4 = (f32[64,2,128]{2,1,0:T(2,128)S(1)}, f32[64,2,128]{2,1,0:T(2,128)}, u32[]{:S(2)}) copy-start(f32[64,2,128]{2,1,0:T(2,128)} %constant.132.clone.twb) | copy-start | bytes 196612
  15.3 20.7 %all-to-all-start = ((f32[16,80,128]{2,1,0:T(8,128)}), f32[16,80,128]{2,1,0:T(8,128)S(1)}, u32[]{:S(2)}, u32[]{:S(2)}) async-start(f32[16,80,128]{2,1,0:T(8,128)} %shard_map.155), calls=%async_computation | async-start | bytes 1310720 | tf_op jit(solution)/shard_map/all_to_all | solution.py:475
  37.6 2.8 %collective-permute-start.4 = (f32[1,4,96,128]{3,2,1,0:T(8,128)S(1)}, f32[1,4,96,128]{3,2,1,0:T(8,128)S(1)}, u32[]{:S(2)}, u32[]{:S(2)}) collective-permute-start(f32[1,4,96,128]{3,2,1,0:T(8,128)S(1)} %bitcast.26), channel_id=1, source_target_pairs={{0,1},{1,0},{2,3},{3,2},{4,5},{5,4},{6,7},{7,6},{8,9},{9,8},{10,11... | collective-permute-start | bytes 589832 | tf_op jit(solution)/shard_map/ppermute | solution.py:441
  38.6 6.5 %collective-permute-start.3 = (f32[4,96,128]{2,1,0:T(8,128)S(1)}, f32[4,96,128]{2,1,0:T(8,128)S(1)}, u32[]{:S(2)}, u32[]{:S(2)}) collective-permute-start(f32[4,96,128]{2,1,0:T(8,128)S(1)} %get-tuple-element.27), channel_id=1, source_target_pairs={{0,6},{1,7},{2,0},{3,1},{4,2},{5,3},{6,4},{7,5},{8,14},{9,15},{10,... | collective-permute-start | bytes 589832 | tf_op jit(solution)/shard_map/ppermute | solution.py:441
  38.7 6.9 %collective-permute-start.2 = (f32[4,96,128]{2,1,0:T(8,128)S(1)}, f32[4,96,128]{2,1,0:T(8,128)S(1)}, u32[]{:S(2)}, u32[]{:S(2)}) collective-permute-start(f32[4,96,128]{2,1,0:T(8,128)S(1)} %get-tuple-element.27), channel_id=1, source_target_pairs={{0,2},{1,3},{2,4},{3,5},{4,6},{5,7},{6,0},{7,1},{8,10},{9,11},{10,... | collective-permute-start | bytes 589832 | tf_op jit(solution)/shard_map/ppermute | solution.py:441
  40.1 7.3 %collective-permute-start.1 = (f32[4,96,128]{2,1,0:T(8,128)S(1)}, f32[4,96,128]{2,1,0:T(8,128)S(1)}, u32[]{:S(2)}, u32[]{:S(2)}) collective-permute-start(f32[4,96,128]{2,1,0:T(8,128)S(1)} %get-tuple-element.27), channel_id=1, source_target_pairs={{0,8},{1,9},{2,10},{3,11},{4,12},{5,13},{6,14},{7,15},{8,0},{9,1},... | collective-permute-start | bytes 589832 | tf_op jit(solution)/shard_map/ppermute | solution.py:441
  47.5 3.2 %collective-permute-start.7 = (f32[3,4,96,128]{3,2,1,0:T(8,128)S(1)}, f32[3,4,96,128]{3,2,1,0:T(8,128)S(1)}, u32[]{:S(2)}, u32[]{:S(2)}) collective-permute-start(f32[3,4,96,128]{3,2,1,0:T(8,128)S(1)} %pad_maximum_fusion.2), channel_id=1, source_target_pairs={{0,1},{1,0},{2,3},{3,2},{4,5},{5,4},{6,7},{7,6},{8,9},{9,8},{10,11... | collective-permute-start | bytes 1769480 | tf_op jit(solution)/shard_map/ppermute | solution.py:441
  49.1 10.3 %collective-permute-start.6 = (f32[6,96,128]{2,1,0:T(8,128)S(1)}, f32[6,96,128]{2,1,0:T(8,128)S(1)}, u32[]{:S(2)}, u32[]{:S(2)}) collective-permute-start(f32[6,96,128]{2,1,0:T(8,128)S(1)} %get-tuple-element.45), channel_id=1, source_target_pairs={{0,6},{1,7},{2,0},{3,1},{4,2},{5,3},{6,4},{7,5},{8,14},{9,15},{10,... | collective-permute-start | bytes 884744 | tf_op jit(solution)/shard_map/ppermute | solution.py:441
  50.5 9.5 %collective-permute-start.5 = (f32[6,96,128]{2,1,0:T(8,128)S(1)}, f32[6,96,128]{2,1,0:T(8,128)S(1)}, u32[]{:S(2)}, u32[]{:S(2)}) collective-permute-start(f32[6,96,128]{2,1,0:T(8,128)S(1)} %get-tuple-element.46), channel_id=1, source_target_pairs={{0,2},{1,3},{2,4},{3,5},{4,6},{5,7},{6,0},{7,1},{8,10},{9,11},{10,... | collective-permute-start | bytes 884744 | tf_op jit(solution)/shard_map/ppermute | solution.py:441
  60.1 4.9 %collective-permute-start.10 = (f32[2,4,96,128]{3,2,1,0:T(8,128)S(1)}, f32[2,4,96,128]{3,2,1,0:T(8,128)S(1)}, u32[]{:S(2)}, u32[]{:S(2)}) collective-permute-start(f32[2,4,96,128]{3,2,1,0:T(8,128)S(1)} %pad_maximum_fusion.4), channel_id=1, source_target_pairs={{0,1},{1,0},{2,3},{3,2},{4,5},{5,4},{6,7},{7,6},{8,9},{9,8},{10,11... | collective-permute-start | bytes 1179656 | tf_op jit(solution)/shard_map/ppermute | solution.py:441
  61.5 9.3 %collective-permute-start.8 = (f32[2,96,128]{2,1,0:T(8,128)S(1)}, f32[2,96,128]{2,1,0:T(8,128)S(1)}, u32[]{:S(2)}, u32[]{:S(2)}) collective-permute-start(f32[2,96,128]{2,1,0:T(8,128)S(1)} %get-tuple-element.42), channel_id=1, source_target_pairs={{0,2},{1,3},{2,4},{3,5},{4,6},{5,7},{6,0},{7,1},{8,10},{9,11},{10,... | collective-permute-start | bytes 294920 | tf_op jit(solution)/shard_map/ppermute | solution.py:441
  61.6 9.2 %collective-permute-start.9 = (f32[2,96,128]{2,1,0:T(8,128)S(1)}, f32[2,96,128]{2,1,0:T(8,128)S(1)}, u32[]{:S(2)}, u32[]{:S(2)}) collective-permute-start(f32[2,96,128]{2,1,0:T(8,128)S(1)} %get-tuple-element.44), channel_id=1, source_target_pairs={{0,6},{1,7},{2,0},{3,1},{4,2},{5,3},{6,4},{7,5},{8,14},{9,15},{10,... | collective-permute-start | bytes 294920 | tf_op jit(solution)/shard_map/ppermute | solution.py:441
  64.3 6.6 %collective-permute-start.12 = (f32[1,4,96,128]{3,2,1,0:T(8,128)S(1)}, f32[1,4,96,128]{3,2,1,0:T(8,128)S(1)}, u32[]{:S(2)}, u32[]{:S(2)}) collective-permute-start(f32[1,4,96,128]{3,2,1,0:T(8,128)S(1)} %maximum_bitcast_fusion.1), channel_id=1, source_target_pairs={{0,1},{1,0},{2,3},{3,2},{4,5},{5,4},{6,7},{7,6},{8,9},{9,8},{10,11... | collective-permute-start | bytes 589832 | tf_op jit(solution)/shard_map/ppermute | solution.py:441
  70.9 2.9 %collective-permute-start.11 = (f32[1,4,96,128]{3,2,1,0:T(8,128)S(1)}, f32[1,4,96,128]{3,2,1,0:T(8,128)S(1)}, u32[]{:S(2)}, u32[]{:S(2)}) collective-permute-start(f32[1,4,96,128]{3,2,1,0:T(8,128)S(1)} %maximum_bitcast_fusion), channel_id=1, source_target_pairs={{0,1},{1,0},{2,3},{3,2},{4,5},{5,4},{6,7},{7,6},{8,9},{9,8},{10,11... | collective-permute-start | bytes 589832 | tf_op jit(solution)/shard_map/ppermute | solution.py:441
